TPU v7x, 512 devices: a whole 4x8x8 slice. The times are simulated.
512 devices in a mesh: tm: 16 (over y, core), space: 32 (over x, z).
Axes of the slice: x: 4, y: 8, z: 8, core: 2. Of those that a mesh axis runs over, the one named last changes fastest.
Arguments:
- coupling: bfloat16 [16, 2048, 2048], P('tm', 'space'), may hold values from -0.125 to 0.125
- arrow_link: float32 [16, 2048, 64], P('tm'), may hold values from -0.75 to 0.75
- local_cov: float32 [16, 2048, 2048], P('tm', 'space'), as said below
- boundary_cov: float32 [16, 2048, 2048], P('tm', 'space'), as said below
- boundary_arrow: float32 [16, 2048, 64], P('tm', 'space'), may hold values from -6 to 6
- fixed_cov: float32 [64, 64], replicated, as said below
Outputs:
- diag_blocks: float32 [16, 2048, 2048], P('tm', 'space')
- cross_blocks: float32 [16, 2048, 2048], P('tm', 'space')
- arrow_covs: float32 [16, 2048, 64], P('tm', 'space')
Inputs may be any that keep to these rules, and one draw needn't show every extreme that they name: `local_cov`: each block is symmetric. `boundary_cov`: each block is symmetric. `fixed_cov`: symmetric.
All inputs are finite; a program needn't handle non-finite values.
Results may differ from a plain program's by a relative error of at most 0.0003.
Values may be sent and summed in bfloat16 or wider, within the bound.
No kernel may reach another device: no remote copies, remote signals or barrier semaphores. Data moves between devices by JAX's collectives and lax.ppermute only.
A program may use at most 64 MiB of HBM per device.

v0:
```python
import jax
import jax.numpy as jnp
from jax import lax
from jax.sharding import PartitionSpec as P


def passed_along(block, axis, distance):
    devices = range(lax.axis_size(axis))
    route = [(i - distance, i) for i in devices if i - distance in devices]
    return lax.ppermute(block, axis, route)


def shards(coupling, arrow_link, local_cov, boundary_cov, boundary_arrow, fixed_cov):
    highest = lax.Precision.HIGHEST
    next_block, next_arrow = passed_along((boundary_cov, boundary_arrow), "tm", -1)
    panels = lax.all_gather(coupling, "space", axis=1, tiled=True)[0]
    groups = lax.axis_size("space")
    rows_here = coupling.shape[1]
    offset = lax.axis_index("space") * rows_here
    link_block = arrow_link[0]
    link_rows = lax.dynamic_slice_in_dim(link_block, offset, rows_here, 0)
    succ_rows = next_block[0]
    succ_arrow = next_arrow[0]
    gathered = lax.all_gather(succ_arrow, "space", axis=0, tiled=True)
    carried = jnp.dot(coupling[0], gathered, precision=highest, preferred_element_type=jnp.float32)
    arrow_rows = carried + jnp.dot(
        link_rows, fixed_cov, precision=highest, preferred_element_type=jnp.float32
    )
    cross_turned = jnp.dot(
        succ_rows, panels.T, precision=highest, preferred_element_type=jnp.float32
    )
    cross_turned = cross_turned + jnp.dot(
        succ_arrow, link_block.T, precision=highest, preferred_element_type=jnp.float32
    )
    pieces = (
        cross_turned.reshape(rows_here, groups, rows_here)
        .transpose(2, 1, 0)
        .reshape(rows_here, groups * rows_here)
    )
    cross_rows = lax.all_to_all(pieces, "space", split_axis=1, concat_axis=1, tiled=True)
    diag_rows = local_cov[0] + jnp.dot(
        cross_rows, panels.T, precision=highest, preferred_element_type=jnp.float32
    )
    diag_rows = diag_rows + jnp.dot(
        arrow_rows, link_block.T, precision=highest, preferred_element_type=jnp.float32
    )
    return (diag_rows[None], cross_rows[None], arrow_rows[None])


def solution(mesh):
    return jax.shard_map(
        shards,
        mesh=mesh,
        in_specs=(
            P("tm", "space", None),
            P("tm", None, None),
            P("tm", "space", None),
            P("tm", "space", None),
            P("tm", "space", None),
            P(),
        ),
        out_specs=(P("tm", "space", None), P("tm", "space", None), P("tm", "space", None)),
        check_vma=False,
    )
```

profile of v0, /device:TPU:56, one launch (start us, length us, event | category | flops | bytes accessed | tf_op | source)
XLA Modules:
  0.0 217.5 jit_solution(1109246769169374447)
XLA Ops:
  7.2 0.0 copy-start
  7.2 0.0 all-gather.3.cloned.1.call-start
  7.2 0.7 all-gather.3.cloned.1.call-update
  7.9 2.7 %collective-permute-start = (f32[1,64,2048]{2,1,0:T(8,128)}, f32[1,64,2048]{2,1,0:T(8,128)S(1)}, u32[]{:S(2)}, u32[]{:S(2)}) collective-permute-start(f32[1,64,2048]{2,1,0:T(8,128)} %param.9), channel_id=1, source_target_pairs={{32,0},{64,32},{96,64},{128,96},{160,128},{192,160},{224,192},{256... | collective-permute-start | bytes 1572872 | tf_op jit(solution)/shard_map/ppermute | solution.py:10
  10.6 2.6 %collective-permute-start.1 = (f32[1,64,64]{2,1,0:T(8,128)}, f32[1,64,64]{2,1,0:T(8,128)S(1)}, u32[]{:S(2)}, u32[]{:S(2)}) collective-permute-start(f32[1,64,64]{2,1,0:T(8,128)} %param.10), channel_id=1, source_target_pairs={{32,0},{64,32},{96,64},{128,96},{160,128},{192,160},{224,192},{256... | collective-permute-start | bytes 49160 | tf_op jit(solution)/shard_map/ppermute | solution.py:10
  13.2 4.8 %collective-permute-done.1 = f32[1,64,64]{2,1,0:T(8,128)S(1)} collective-permute-done((f32[1,64,64]{2,1,0:T(8,128)}, f32[1,64,64]{2,1,0:T(8,128)S(1)}, u32[]{:S(2)}, u32[]{:S(2)}) %collective-permute-start.1) | collective-permute-done | bytes 16416 | tf_op jit(solution)/shard_map/ppermute | solution.py:10
  18.0 0.6 fusion.13
  18.6 101.2 %all-gather.3.cloned.1.call-done = bf16[1,2048,2048]{2,1,0:T(8,128)(2,1)} async-done(((bf16[1,64,2048]{2,1,0:T(8,128)(2,1)}), bf16[1,2048,2048]{2,1,0:T(8,128)(2,1)}) %all-gather.3.cloned.1.call-update) | async-done | bytes 8388624 | tf_op jit(solution)/shard_map/all_gather | solution.py:16
  119.8 10.0 %fusion.5 = f32[64,2048]{1,0:T(8,128)S(1)} fusion(f32[64,2048]{1,0:T(8,128)S(1)} %fusion.13, bf16[1,2048,2048]{2,1,0:T(8,128)(2,1)} %all-gather.3.cloned.1.call-done, f32[1,64,2048]{2,1,0:T(8,128)S(1)} %collective-permute-done), kind=kOutput, calls=%fused_computation.6 | convolution fusion | flops 3221356544 | bytes 9961472 | tf_op jit(solution)/shard_map/dot_general | solution.py:29
  129.8 0.3 copy.16
  130.2 1.5 reshape.17
  131.6 5.4 %all-to-all-start = ((f32[32,1,4096]{2,1,0:T(1,128)}), f32[32,1,4096]{2,1,0:T(1,128)S(1)}, u32[]{:S(2)}, u32[]{:S(2)}) async-start(f32[32,1,4096]{2,1,0:T(1,128)} %reshape.17), calls=%async_computation | async-start | bytes 1048576 | tf_op jit(solution)/shard_map/all_to_all | solution.py:40
  137.1 0.3 fusion.17
  137.4 56.4 %all-gather = f32[1,2048,64]{2,1,0:T(8,128)S(1)} all-gather(f32[1,64,64]{2,1,0:T(8,128)S(1)} %collective-permute-done.1), channel_id=2, replica_groups=mesh['tm'=16,'space'=32] {'space'}, dimensions={1}, use_global_device_ids=true | all-gather | bytes 540672 | tf_op jit(solution)/shard_map/all_gather | solution.py:24
  193.8 0.5 convolution_add_fusion.1
  194.3 0.0 copy-start.3
  194.3 0.5 broadcast
  194.8 1.9 reduce
  196.7 0.4 reshape.18
  197.1 0.6 copy.14
  197.7 0.4 all_to_all.7
  198.1 1.2 broadcast_in_dim.10
  199.3 10.0 %fusion.8 = f32[64,2048]{1,0:T(8,128)S(1)} fusion(f32[64,2048]{1,0:T(8,128)S(1)} %all_to_all.7, bf16[1,2048,2048]{2,1,0:T(8,128)(2,1)} %all-gather.3.cloned.1.call-done, f32[1,64,2048]{2,1,0:T(8,128)S(1)} %copy-done.2), kind=kOutput, calls=%fused_computation.7 | convolution fusion | flops 3221356544 | bytes 9961472 | tf_op jit(solution)/shard_map/dot_general | solution.py:41
  209.3 1.4 fusion.4
  (10 shorter events, 0.0 us)
Async XLA Ops:
  7.2 10.8 %copy-start = (f32[1,2048,64]{1,2,0:T(8,128)S(1)}, f32[1,2048,64]{1,2,0:T(8,128)}, u32[]{:S(2)}) copy-start(f32[1,2048,64]{1,2,0:T(8,128)} %param.7) | copy-start | bytes 1572868
  7.2 186.6 %copy-start.1 = (bf16[1,64,2048]{2,1,0:T(8,128)(2,1)S(1)}, bf16[1,64,2048]{2,1,0:T(8,128)(2,1)}, u32[]{:S(2)}) copy-start(bf16[1,64,2048]{2,1,0:T(8,128)(2,1)} %param.6) | copy-start | bytes 786436
  7.2 129.9 %copy-start.4 = (f32[64,64]{1,0:T(8,128)S(1)}, f32[64,64]{1,0:T(8,128)}, u32[]{:S(2)}) copy-start(f32[64,64]{1,0:T(8,128)} %param.11) | copy-start | bytes 49156
  7.2 112.6 %all-gather.3.cloned.1.call-start = ((), (), s32[]{:S(2)}) async-start(), calls=%async_computation.1 | async-start | bytes 8650752 | tf_op jit(solution)/shard_map/all_gather | solution.py:16
  7.9 10.6 %collective-permute-start = (f32[1,64,2048]{2,1,0:T(8,128)}, f32[1,64,2048]{2,1,0:T(8,128)S(1)}, u32[]{:S(2)}, u32[]{:S(2)}) collective-permute-start(f32[1,64,2048]{2,1,0:T(8,128)} %param.9), channel_id=1, source_target_pairs={{32,0},{64,32},{96,64},{128,96},{160,128},{192,160},{224,192},{256... | collective-permute-start | bytes 1572872 | tf_op jit(solution)/shard_map/ppermute | solution.py:10
  10.6 7.3 %collective-permute-start.1 = (f32[1,64,64]{2,1,0:T(8,128)}, f32[1,64,64]{2,1,0:T(8,128)S(1)}, u32[]{:S(2)}, u32[]{:S(2)}) collective-permute-start(f32[1,64,64]{2,1,0:T(8,128)} %param.10), channel_id=1, source_target_pairs={{32,0},{64,32},{96,64},{128,96},{160,128},{192,160},{224,192},{256... | collective-permute-start | bytes 49160 | tf_op jit(solution)/shard_map/ppermute | solution.py:10
  129.8 69.4 %copy-start.2 = (f32[1,64,2048]{2,1,0:T(8,128)S(1)}, f32[1,64,2048]{2,1,0:T(8,128)}, u32[]{:S(2)}) copy-start(f32[1,64,2048]{2,1,0:T(8,128)} %param.8) | copy-start | bytes 1572868
  131.6 62.7 %all-to-all-start = ((f32[32,1,4096]{2,1,0:T(1,128)}), f32[32,1,4096]{2,1,0:T(1,128)S(1)}, u32[]{:S(2)}, u32[]{:S(2)}) async-start(f32[32,1,4096]{2,1,0:T(1,128)} %reshape.17), calls=%async_computation | async-start | bytes 1048576 | tf_op jit(solution)/shard_map/all_to_all | solution.py:40
  194.3 15.0 %copy-start.3 = (f32[64,64]{1,0:T(8,128)}, f32[64,64]{1,0:T(8,128)S(1)}, u32[]{:S(2)}) copy-start(f32[64,64]{1,0:T(8,128)S(1)} %convolution_add_fusion.1) | copy-start | bytes 49156
Sparse Core Ops, SparseCore 0:
  11.2 108.5 all-gather.2
where the time goes:
time: 218 us
  waiting for transfers between devices  107 us (49%)
  blocking collectives  56.4 us (26%)
  matrix products  22.8 us (10%)
  between operations  14.2 us (7%)
  starting transfers between devices  10.8 us (5%)
  local copies, waits for them, and re-layouts  4.86 us (2%)
    all_gather x1, waiting for transfers between devices, shards(): panels = lax.all_gather(coupling, 'space', axis=1, tiled=True)[0]  101 us
    all_gather x1, blocking collectives, shards(): gathered = lax.all_gather(succ_arrow, 'space', axis=0, tiled=True)  56.4 us
    dot_general x1, matrix products, shards(): jnp.dot(cross_rows, panels.T, precision=highest, preferred_element_type=j...  10 us
    dot_general x1, matrix products, shards(): jnp.dot(succ_rows, panels.T, precision=highest, preferred_element_type=jn...  10 us
    all_to_all x1, starting transfers between devices, shards(): lax.all_to_all(pieces, 'space', split_axis=1, concat_axis=1, tiled=True)  5.45 us
    ppermute x2, starting transfers between devices, passed_along(): return lax.ppermute(block, axis, route)  5.28 us
    ppermute x2, waiting for transfers between devices, passed_along(): return lax.ppermute(block, axis, route)  4.76 us
  transfers between devices with their start and end apart: 4, of which 2 were waited for; matrix products, arithmetic and copies ran while one was open for 1% of the time, Pallas kernels for 0%

commit v1 on v0

v1 whole, which is shorter than its diff:
```python
import jax
import jax.numpy as jnp
from jax import lax
from jax.sharding import Mesh, PartitionSpec as P

F32, F16, BF16 = jnp.float32, jnp.float16, jnp.bfloat16
HIGH = lax.Precision.HIGH


def exponent(largest):
    return jnp.floor(jnp.log2(jnp.clip(largest, 1e-30, 1e38)))


def dot_t(a, b, **kw):
    return lax.dot_general(a, b, (((1,), (1,)), ((), ())), preferred_element_type=F32, **kw)


def two_parts(v, axis):
    top = lax.reduce_precision(v, 8, 7)
    return jnp.concatenate([top.astype(BF16), (v - top).astype(BF16)], axis=axis)


def spread(v, axis):
    n = lax.axis_size(axis)
    return lax.all_to_all(jnp.broadcast_to(v[None], (n,) + v.shape), axis, 0, 0, tiled=True)


def shards(coupling, arrow_link, local_cov, boundary_cov, boundary_arrow, fixed_cov):
    c_own, link, local = coupling[0], arrow_link[0], local_cov[0]
    s_own, a_own = boundary_cov[0], boundary_arrow[0]
    nx, nz = lax.axis_size("x"), lax.axis_size("z")
    steps = lax.axis_size("y") * lax.axis_size("c")
    rows, ns = c_own.shape
    nf = a_own.shape[1]
    ix, iz = lax.axis_index("x"), lax.axis_index("z")

    exp_s = exponent(jnp.max(jnp.abs(s_own), axis=1, keepdims=True))
    exp_a = exponent(jnp.max(jnp.abs(a_own), axis=1, keepdims=True))
    bound = 0.125 * jnp.sum(jnp.abs(s_own), axis=1, keepdims=True)
    bound = bound + 0.75 * jnp.sum(jnp.abs(a_own), axis=1, keepdims=True)
    exp_b = exponent(bound) + 2
    lane = lax.broadcasted_iota(jnp.int32, (rows, nf), 1)
    exps = jnp.where(lane == 0, exp_s, jnp.where(lane == 1, exp_a, exp_b))
    packed = jnp.concatenate(
        [
            (s_own * jnp.exp2(13 - exp_s)).astype(F16),
            (a_own * jnp.exp2(13 - exp_a)).astype(F16),
            exps.astype(F16),
        ],
        axis=1,
    )
    group = nx * nz
    route = [
        (t * group + b, (t - 1) * group + (b % nx) * nz + b // nx)
        for t in range(1, steps)
        for b in range(group)
    ]
    packed = lax.ppermute(packed, ("y", "c", "x", "z"), route)

    c_rows = lax.all_gather(c_own, "z", axis=0, tiled=True)
    link_rows = lax.dynamic_slice_in_dim(link, ix * nz * rows, nz * rows, 0)

    tails = spread(spread(packed[:, ns:], "z"), "x").astype(F32)
    tails = tails.transpose(1, 0, 2, 3).reshape(ns, 2 * nf)
    exp_z = jnp.max(tails[:, nf + 2].reshape(nz, -1), axis=1)
    a_all = tails[:, :nf] * jnp.exp2(tails[:, nf + 1 : nf + 2] - 13)
    arrow2 = jnp.dot(c_own, two_parts(a_all, 1), preferred_element_type=F32)
    link_own = lax.dynamic_slice_in_dim(link, (ix * nz + iz) * rows, rows, 0)
    arrow = arrow2[:, :nf] + arrow2[:, nf:]
    arrow = arrow + jnp.dot(link_own, fixed_cov, precision=lax.Precision.HIGHEST)
    arrows = spread(arrow, "x").reshape(nx * rows, nf)

    succ = spread(packed, "x").reshape(nx * rows, -1).astype(F32)
    s_cols = succ[:, :ns] * jnp.exp2(succ[:, ns + nf : ns + nf + 1] - 13)
    a_cols = succ[:, ns : ns + nf] * jnp.exp2(succ[:, ns + nf + 1 : ns + nf + 2] - 13)
    exp_own = jnp.max(succ[:, ns + nf + 2])
    cross2 = dot_t(c_rows, two_parts(s_cols, 0))
    cross = cross2[:, : nx * rows] + cross2[:, nx * rows :]
    cross = cross + dot_t(link_rows, a_cols, precision=HIGH)
    cross = (cross * jnp.exp2(14 - exp_own)).astype(F16)
    cross = cross.reshape(nz, rows, nx * rows)
    cross = lax.all_to_all(cross, "z", 0, 0, tiled=True)
    scale = jnp.exp2(exp_z - 14)[:, None, None]
    cross_rows = (cross.astype(F32) * scale).transpose(1, 0, 2).reshape(rows, ns)

    cross_all = spread(cross, "x").astype(F32) * scale[None]
    cross_all = cross_all.transpose(0, 2, 1, 3).reshape(nx * rows, ns)
    diag2 = dot_t(two_parts(cross_all, 0), c_rows)
    diag = diag2[: nx * rows] + diag2[nx * rows :]
    diag = diag + dot_t(arrows, link_rows, precision=HIGH)
    diag = lax.all_to_all(diag.reshape(nx, rows, nz * rows), "x", 0, 0, tiled=True)
    diag_rows = local + diag.transpose(1, 0, 2).reshape(rows, ns)
    return (diag_rows[None], cross_rows[None], arrow[None])


def solution(mesh):
    mesh = Mesh(mesh.devices.reshape(8, 2, 4, 8), ("y", "c", "x", "z"))
    step, space = ("y", "c"), ("x", "z")
    row_split = P(step, space, None)
    return jax.shard_map(
        shards,
        mesh=mesh,
        in_specs=(row_split, P(step, None, None), row_split, row_split, row_split, P()),
        out_specs=(row_split, row_split, row_split),
        check_vma=False,
    )
```

time: 218 us -> 176 us (0.81)
  the two profiles are of different devices: /device:TPU:56 before, /device:TPU:8 now
where the time goes in v1:
time: 176 us; the launch traced here: 175 us
  blocking collectives  63.3 us (36%)
  waiting for transfers between devices  47.3 us (27%)
  starting transfers between devices  19.3 us (11%)
  between operations  15 us (9%)
  other arithmetic  12.3 us (7%)
  local copies, waits for them, and re-layouts  9.37 us (5%)
  matrix products  8.53 us (5%)
    all_to_all x2, blocking collectives, spread(): lax.all_to_all(jnp.broadcast_to(v[None], (n,) + v.shape), axis, 0, 0, til...  63.3 us
    all_to_all x3, waiting for transfers between devices, spread(): lax.all_to_all(jnp.broadcast_to(v[None], (n,) + v.shape), axis, 0, 0, til...  27.4 us
    all_to_all x3, starting transfers between devices, spread(): lax.all_to_all(jnp.broadcast_to(v[None], (n,) + v.shape), axis, 0, 0, til...  10.3 us
    all_to_all x1, waiting for transfers between devices, shards(): cross = lax.all_to_all(cross, 'z', 0, 0, tiled=True)  8.49 us
    dot_general x4, matrix products, dot_t(): lax.dot_general(a, b, (((1,), (1,)), ((), ())), preferred_element_type=F3...  7.81 us
    all_to_all x1, waiting for transfers between devices, shards(): lax.all_to_all(diag.reshape(nx, rows, nz * rows), 'x', 0, 0, tiled=True)  6.73 us
    unnamed x17, local copies, waits for them, and re-layouts  4.36 us
    ppermute x1, waiting for transfers between devices, shards(): packed = lax.ppermute(packed, ('y', 'c', 'x', 'z'), route)  4.04 us
  transfers between devices with their start and end apart: 7, of which 6 were waited for; matrix products, arithmetic and copies ran while one was open for 9% of the time, Pallas kernels for 0%

profile of v1, /device:TPU:8, one launch (start us, length us, event | category | flops | bytes accessed | tf_op | source)
XLA Modules:
  0.0 175.2 jit_solution(5549230704443145912)
XLA Ops:
  7.9 1.2 fusion.27
  11.0 1.2 fusion.26
  12.3 1.9 %collective-permute-start = (f16[64,2176]{1,0:T(8,128)(2,1)S(1)}, f16[64,2176]{1,0:T(8,128)(2,1)S(1)}, u32[]{:S(2)}, u32[]{:S(2)}) collective-permute-start(f16[64,2176]{1,0:T(8,128)(2,1)S(1)} %concatenate.12), channel_id=1, source_target_pairs={{32,0},{33,8},{34,16},{35,24},{36,1},{37,9},{38,17},{39,25},{40,2}... | collective-permute-start | bytes 835592 | tf_op jit(solution)/shard_map/ppermute | solution.py:58
  14.2 4.0 %collective-permute-done = f16[64,2176]{1,0:T(8,128)(2,1)S(1)} collective-permute-done((f16[64,2176]{1,0:T(8,128)(2,1)S(1)}, f16[64,2176]{1,0:T(8,128)(2,1)S(1)}, u32[]{:S(2)}, u32[]{:S(2)}) %collective-permute-start) | collective-permute-done | bytes 278560 | tf_op jit(solution)/shard_map/ppermute | solution.py:58
  18.3 45.7 %all_to_all.35 = f16[8,64,128]{2,1,0:T(8,128)(2,1)S(1)} all-to-all(f16[8,64,128]{2,1,0:T(8,128)(2,1)S(1)} %broadcast_in_dim.41), channel_id=1, replica_groups=mesh['y'=8,'c'=2,'x'=4,'z'=8] {'z'}, dimensions={0} | all-to-all | bytes 262144 | tf_op jit(solution)/shard_map/all_to_all | solution.py:25
  64.2 17.6 %all_to_all.36 = f16[4,8,64,128]{3,2,1,0:T(8,128)(2,1)S(1)} all-to-all(f16[4,8,64,128]{3,2,1,0:T(8,128)(2,1)S(1)} %broadcast_in_dim.42), channel_id=1, replica_groups=mesh['y'=8,'c'=2,'x'=4,'z'=8] {'x'}, dimensions={0} | all-to-all | bytes 1048576 | tf_op jit(solution)/shard_map/all_to_all | solution.py:25
  82.8 3.5 %all-to-all-start = ((f16[4,64,2176]{2,1,0:T(8,128)(2,1)}), f16[4,64,2176]{2,1,0:T(8,128)(2,1)S(1)}, u32[]{:S(2)}, u32[]{:S(2)}) async-start(f16[4,64,2176]{2,1,0:T(8,128)(2,1)} %broadcast_in_dim.39), calls=%async_computation | async-start | bytes 2228224 | tf_op jit(solution)/shard_map/all_to_all | solution.py:25
  86.4 1.2 slice_reduce_fusion
  87.6 12.7 %all-to-all-done = f16[4,64,2176]{2,1,0:T(8,128)(2,1)S(1)} async-done(((f16[4,64,2176]{2,1,0:T(8,128)(2,1)}), f16[4,64,2176]{2,1,0:T(8,128)(2,1)S(1)}, u32[]{:S(2)}, u32[]{:S(2)}) %all-to-all-start) | async-done | bytes 1114144 | tf_op jit(solution)/shard_map/all_to_all | solution.py:25
  100.6 1.4 copy-done.1
  103.4 2.9 %reduce-precision_convert_fusion.1 = (bf16[256,2048]{1,0:T(8,128)(2,1)S(1)}, bf16[256,2048]{1,0:T(8,128)(2,1)}) fusion(f32[256,2176]{1,0:T(8,128)} %copy-done.1, f32[256]{0:T(256)S(1)} %get-tuple-element.5), kind=kLoop, calls=%fused_computation.3 | loop fusion | flops 2621440 | bytes 4195328 | tf_op jit(solution)/shard_map/convert_element_type | solution.py:20
  106.3 3.2 %fusion.12 = f32[512,512]{1,0:T(8,128)S(1)} fusion(bf16[1,512,2048]{2,1,0:T(8,128)(2,1)} %all-gather.3.cloned.1.call-done, bf16[256,2048]{1,0:T(8,128)(2,1)} %get-tuple-element.17, bf16[256,2048]{1,0:T(8,128)(2,1)S(1)} %get-tuple-element.16), kind=kOutput, calls=%fused_computation.20 | convolution fusion | flops 1077936128 | bytes 5242880 | tf_op jit(solution)/shard_map/dot_general | solution.py:15
  109.6 2.1 %fusion.18 = f16[512,256]{1,0:T(8,128)(2,1)} fusion(f32[512,512]{1,0:T(8,128)S(1)} %fusion.12, f32[]{:T(128)S(6)} %exp2.90, f32[256,2176]{1,0:T(8,128)} %copy-done.1, f32[1,2048,64]{1,2,0:T(8,128)S(1)} %copy-done, s32[]{:T(128)S(6)} %select_n.16, f32[256]{0:T(256)S(1)} %get-tuple-element.3), kind=kOutput, calls=%fused_computation.24 | convolution fusion | flops 50872320 | bytes 1573896 | tf_op jit(solution)/shard_map/dot_general | solution.py:15
  111.7 3.5 %all-to-all-start.1 = ((f16[8,64,256]{2,1,0:T(8,128)(2,1)}), f16[8,64,256]{2,1,0:T(8,128)(2,1)S(1)}, u32[]{:S(2)}, u32[]{:S(2)}) async-start(f16[8,64,256]{2,1,0:T(8,128)(2,1)} %bitcast.7), calls=%async_computation.1 | async-start | bytes 524288 | tf_op jit(solution)/shard_map/all_to_all | solution.py:82
  117.2 8.5 %all-to-all-done.1 = f16[8,64,256]{2,1,0:T(8,128)(2,1)S(1)} async-done(((f16[8,64,256]{2,1,0:T(8,128)(2,1)}), f16[8,64,256]{2,1,0:T(8,128)(2,1)S(1)}, u32[]{:S(2)}, u32[]{:S(2)}) %all-to-all-start.1) | async-done | bytes 262176 | tf_op jit(solution)/shard_map/all_to_all | solution.py:82
  125.6 3.3 %all-to-all-start.5 = ((f32[4,1,4096]{2,1,0:T(1,128)}), f32[4,1,4096]{2,1,0:T(1,128)S(1)}, u32[]{:S(2)}, u32[]{:S(2)}) async-start(f32[4,1,4096]{2,1,0:T(1,128)} %reshape.121), calls=%async_computation.5 | async-start | bytes 131072 | tf_op jit(solution)/shard_map/all_to_all | solution.py:25
  129.1 5.4 %all-to-all-done.5 = f32[4,1,4096]{2,1,0:T(1,128)S(1)} async-done(((f32[4,1,4096]{2,1,0:T(1,128)}), f32[4,1,4096]{2,1,0:T(1,128)S(1)}, u32[]{:S(2)}, u32[]{:S(2)}) %all-to-all-start.5) | async-done | bytes 65568 | tf_op jit(solution)/shard_map/all_to_all | solution.py:25
  135.6 3.5 %all-to-all-start.2 = ((f16[4,8,64,256]{3,1,2,0:T(8,128)(2,1)}), f16[4,8,64,256]{3,1,2,0:T(8,128)(2,1)S(1)}, u32[]{:S(2)}, u32[]{:S(2)}) async-start(f16[4,8,64,256]{3,1,2,0:T(8,128)(2,1)} %broadcast_in_dim.40), calls=%async_computation.2 | async-start | bytes 2097152 | tf_op jit(solution)/shard_map/all_to_all | solution.py:25
  140.7 9.3 %all-to-all-done.2 = f16[4,8,64,256]{3,1,2,0:T(8,128)(2,1)S(1)} async-done(((f16[4,8,64,256]{3,1,2,0:T(8,128)(2,1)}), f16[4,8,64,256]{3,1,2,0:T(8,128)(2,1)S(1)}, u32[]{:S(2)}, u32[]{:S(2)}) %all-to-all-start.2) | async-done | bytes 1048608 | tf_op jit(solution)/shard_map/all_to_all | solution.py:25
  151.5 1.2 copy-done.6
  152.7 1.3 fusion.6
  154.0 1.2 convolution_add_fusion
  155.2 3.5 %all-to-all-start.6 = ((f32[4,64,512]{2,1,0:T(8,128)}), f32[4,64,512]{2,1,0:T(8,128)S(1)}, u32[]{:S(2)}, u32[]{:S(2)}) async-start(f32[4,64,512]{2,1,0:T(8,128)} %bitcast.16), calls=%async_computation.6 | async-start | bytes 1048576 | tf_op jit(solution)/shard_map/all_to_all | solution.py:91
  160.0 6.7 %all-to-all-done.6 = f32[4,64,512]{2,1,0:T(8,128)S(1)} async-done(((f32[4,64,512]{2,1,0:T(8,128)}), f32[4,64,512]{2,1,0:T(8,128)S(1)}, u32[]{:S(2)}, u32[]{:S(2)}) %all-to-all-start.6) | async-done | bytes 524320 | tf_op jit(solution)/shard_map/all_to_all | solution.py:91
  (51 shorter events, 14.1 us)
Async XLA Ops:
  7.2 102.4 %copy-start = (f32[1,2048,64]{1,2,0:T(8,128)S(1)}, f32[1,2048,64]{1,2,0:T(8,128)}, u32[]{:S(2)}) copy-start(f32[1,2048,64]{1,2,0:T(8,128)} %param.7) | copy-start | bytes 1572868
  7.2 99.2 %all-gather.3.cloned.1.call-start = ((), (), s32[]{:S(2)}) async-start(), calls=%async_computation.7 | async-start | bytes 2359296 | tf_op jit(solution)/shard_map/all_gather | solution.py:60
  12.3 6.0 %collective-permute-start = (f16[64,2176]{1,0:T(8,128)(2,1)S(1)}, f16[64,2176]{1,0:T(8,128)(2,1)S(1)}, u32[]{:S(2)}, u32[]{:S(2)}) collective-permute-start(f16[64,2176]{1,0:T(8,128)(2,1)S(1)} %concatenate.12), channel_id=1, source_target_pairs={{32,0},{33,8},{34,16},{35,24},{36,1},{37,9},{38,17},{39,25},{40,2}... | collective-permute-start | bytes 835592 | tf_op jit(solution)/shard_map/ppermute | solution.py:58
  82.8 17.5 %all-to-all-start = ((f16[4,64,2176]{2,1,0:T(8,128)(2,1)}), f16[4,64,2176]{2,1,0:T(8,128)(2,1)S(1)}, u32[]{:S(2)}, u32[]{:S(2)}) async-start(f16[4,64,2176]{2,1,0:T(8,128)(2,1)} %broadcast_in_dim.39), calls=%async_computation | async-start | bytes 2228224 | tf_op jit(solution)/shard_map/all_to_all | solution.py:25
  100.5 1.4 copy-start.1
  109.6 6.1 %copy-start.2 = (bf16[1,64,2048]{2,1,0:T(8,128)(2,1)S(1)}, bf16[1,64,2048]{2,1,0:T(8,128)(2,1)}, u32[]{:S(2)}) copy-start(bf16[1,64,2048]{2,1,0:T(8,128)(2,1)} %param.6) | copy-start | bytes 786436
  111.7 4.3 %copy-start.5 = (f32[64,64]{1,0:T(8,128)S(1)}, f32[64,64]{1,0:T(8,128)}, u32[]{:S(2)}) copy-start(f32[64,64]{1,0:T(8,128)} %param.11) | copy-start | bytes 49156
  111.7 13.9 %all-to-all-start.1 = ((f16[8,64,256]{2,1,0:T(8,128)(2,1)}), f16[8,64,256]{2,1,0:T(8,128)(2,1)S(1)}, u32[]{:S(2)}, u32[]{:S(2)}) async-start(f16[8,64,256]{2,1,0:T(8,128)(2,1)} %bitcast.7), calls=%async_computation.1 | async-start | bytes 524288 | tf_op jit(solution)/shard_map/all_to_all | solution.py:82
  116.4 19.2 %copy-start.4 = (f32[64,64]{1,0:T(8,128)}, f32[64,64]{1,0:T(8,128)S(1)}, u32[]{:S(2)}) copy-start(f32[64,64]{1,0:T(8,128)S(1)} %convolution_add_fusion.2) | copy-start | bytes 49156
  125.6 8.9 %all-to-all-start.5 = ((f32[4,1,4096]{2,1,0:T(1,128)}), f32[4,1,4096]{2,1,0:T(1,128)S(1)}, u32[]{:S(2)}, u32[]{:S(2)}) async-start(f32[4,1,4096]{2,1,0:T(1,128)} %reshape.121), calls=%async_computation.5 | async-start | bytes 131072 | tf_op jit(solution)/shard_map/all_to_all | solution.py:25
  135.6 14.4 %all-to-all-start.2 = ((f16[4,8,64,256]{3,1,2,0:T(8,128)(2,1)}), f16[4,8,64,256]{3,1,2,0:T(8,128)(2,1)S(1)}, u32[]{:S(2)}, u32[]{:S(2)}) async-start(f16[4,8,64,256]{3,1,2,0:T(8,128)(2,1)} %broadcast_in_dim.40), calls=%async_computation.2 | async-start | bytes 2097152 | tf_op jit(solution)/shard_map/all_to_all | solution.py:25
  151.1 1.6 copy-start.6
  155.2 11.5 %all-to-all-start.6 = ((f32[4,64,512]{2,1,0:T(8,128)}), f32[4,64,512]{2,1,0:T(8,128)S(1)}, u32[]{:S(2)}, u32[]{:S(2)}) async-start(f32[4,64,512]{2,1,0:T(8,128)} %bitcast.16), calls=%async_computation.6 | async-start | bytes 1048576 | tf_op jit(solution)/shard_map/all_to_all | solution.py:91
  158.8 8.7 %copy-start.3 = (f32[1,64,2048]{2,1,0:T(8,128)S(1)}, f32[1,64,2048]{2,1,0:T(8,128)}, u32[]{:S(2)}) copy-start(f32[1,64,2048]{2,1,0:T(8,128)} %param.8) | copy-start | bytes 1572868
Sparse Core Ops, SparseCore 0:
  10.1 60.9 all-gather.2

commit v2 on v1

v2 whole, which is shorter than its diff:
```python
import jax
import jax.numpy as jnp
from jax import lax
from jax.sharding import Mesh, PartitionSpec as P

F32, F16, BF16 = jnp.float32, jnp.float16, jnp.bfloat16
HIGH = lax.Precision.HIGH


def exponent(largest):
    return jnp.floor(jnp.log2(jnp.clip(largest, 1e-30, 1e38)))


def dot_t(a, b, **kw):
    return lax.dot_general(a, b, (((1,), (1,)), ((), ())), preferred_element_type=F32, **kw)


def two_parts(v):
    top = lax.reduce_precision(v, 8, 7)
    return top.astype(BF16), (v - top).astype(BF16)


def spread(v, axis):
    n = lax.axis_size(axis)
    return lax.all_to_all(jnp.broadcast_to(v[None], (n,) + v.shape), axis, 0, 0, tiled=True)


def passed(v, axis, by):
    n = lax.axis_size(axis)
    return lax.ppermute(v, axis, [(i, (i + by) % n) for i in range(n)])


def shards(coupling, arrow_link, local_cov, boundary_cov, boundary_arrow, fixed_cov):
    c_own, link, local = coupling[0], arrow_link[0], local_cov[0]
    s_own, a_own = boundary_cov[0], boundary_arrow[0]
    nx, nz = lax.axis_size("x"), lax.axis_size("z")
    steps = lax.axis_size("y") * lax.axis_size("c")
    group = nx * nz
    rows, ns = c_own.shape
    nf = a_own.shape[1]
    cols = nx * rows
    ix, iz = lax.axis_index("x"), lax.axis_index("z")

    route = []
    for t in range(1, steps):
        for x in range(nx):
            for z in range(nz):
                target = (x - x % 2 + z % 2) * nz + z - z % 2 + x % 2
                route.append((t * group + x * nz + z, (t - 1) * group + target))
    bound_a = jnp.max(jnp.abs(a_own), axis=1, keepdims=True)
    bound = 0.125 * jnp.sum(jnp.abs(s_own), axis=1, keepdims=True) + 0.75 * nf * bound_a
    lane = lax.broadcasted_iota(jnp.int32, (rows, nf), 1)
    exps = jnp.where(lane == 0, exponent(bound) + 2, exponent(0.125 * cols * bound_a) + 2)
    exps = exps.astype(BF16)
    s_top, s_low = two_parts(s_own)
    a_top, a_low = two_parts(a_own)
    packed = jnp.stack(
        [
            jnp.concatenate([s_top, a_top, exps], axis=1),
            jnp.concatenate([s_low, a_low, exps], axis=1),
        ]
    )
    packed = lax.ppermute(packed, ("y", "c", "x", "z"), route)
    before, after = passed(packed, "x", 1), passed(packed, "x", -1)
    far_top, far_low = passed(packed[0], "x", 2), passed(packed[1], "x", -2)
    succ = jnp.zeros((nx,) + packed.shape, BF16)
    for by, block in ((0, packed), (nx - 1, before), (1, after)):
        succ = lax.dynamic_update_index_in_dim(succ, block, (ix + by) % nx, 0)
    far = jnp.stack([far_top, far_low])
    succ = lax.dynamic_update_index_in_dim(succ, far, (ix + 2) % nx, 0)
    succ = succ.transpose(1, 0, 2, 3)
    s_cols = succ[..., :ns].reshape(2 * cols, ns)
    a_two = succ[..., ns : ns + nf].reshape(2, cols, nf)
    exps = jnp.max(succ[0, :, :, ns + nf : ns + nf + 2].astype(F32), axis=(0, 1))

    link_rows = lax.dynamic_slice_in_dim(link, ix * nz * rows, nz * rows, 0)
    arrow_term = dot_t(link_rows, a_two[0].astype(F32) + a_two[1].astype(F32), precision=HIGH)
    place = a_two.reshape(2, nx // 2, 1, 1, 2, rows, nf)
    here = lax.broadcasted_iota(jnp.int32, (2, nz // 2), 0) == iz % 2
    here &= lax.broadcasted_iota(jnp.int32, (2, nz // 2), 1) == iz // 2
    place = jnp.where(here[None, None, :, :, None, None, None], place, jnp.zeros((), BF16))
    place = place.reshape(2, ns, nf)
    place = jnp.concatenate([place[0], place[1]], axis=1)
    s_cols, arrow_term, place = lax.optimization_barrier((s_cols, arrow_term, place))

    c_rows = spread(c_own, "z").reshape(nz * rows, ns)

    cross2 = dot_t(c_rows, s_cols)
    cross = (cross2[:, :cols] + cross2[:, cols:] + arrow_term) * jnp.exp2(14 - exps[0])
    share2 = jnp.dot(c_rows, place, preferred_element_type=F32)
    share = (share2[:, :nf] + share2[:, nf:]) * jnp.exp2(14 - exps[1])
    lane = lax.broadcasted_iota(jnp.int32, (nz * rows, nf), 1)
    marks = jnp.where(lane == 0, exps[0], exps[1])
    sent = jnp.concatenate([cross.astype(F16), share.astype(F16), marks.astype(F16)], axis=1)
    sent = lax.all_to_all(sent.reshape(nz, rows, -1), "z", 0, 0, tiled=True)
    cross = sent[..., :cols]
    marks = sent[:, :1, cols + nf : cols + nf + 2].astype(F32)
    scale = jnp.exp2(marks[..., :1] - 14)

    every = spread(cross, "x").astype(F32) * scale[None]
    every = every.transpose(0, 2, 1, 3).reshape(cols, ns)
    runs = []
    for z in range(nz):
        for q in range(nx // 2):
            first = (2 * q + z % 2) * nz * rows + z // 2 * 2 * rows
            runs.append(c_rows[:, first : first + 2 * rows])
    c_turned = lax.optimization_barrier(jnp.concatenate(runs, axis=1))
    diag2 = dot_t(jnp.concatenate(two_parts(every), axis=0), c_turned)
    diag = (diag2[:cols] + diag2[cols:]).reshape(nx, rows, nz * rows)
    diag = lax.all_to_all(diag, "x", 0, 0, tiled=True)

    own = cross.astype(F32) * scale
    pieces = []
    for x in range(nx):
        for k in range(nz // 2):
            half = slice(x // 2 * 2 * rows, (x // 2 + 1) * 2 * rows)
            pieces.append(own[2 * k + x % 2, :, half])
    cross_rows = jnp.concatenate(pieces, axis=1)
    share = sent[..., cols : cols + nf].astype(F32) * jnp.exp2(marks[..., 1:] - 14)
    link_own = lax.dynamic_slice_in_dim(link, (ix * nz + iz) * rows, rows, 0)
    arrow = jnp.dot(link_own, fixed_cov, precision=lax.Precision.HIGHEST)
    arrow = jnp.sum(share, axis=0) + arrow
    local = lax.optimization_barrier(local + dot_t(arrow, link, precision=HIGH))
    diag_rows = local + diag.transpose(1, 0, 2).reshape(rows, ns)
    return (diag_rows[None], cross_rows[None], arrow[None])


def solution(mesh):
    mesh = Mesh(mesh.devices.reshape(8, 2, 4, 8), ("y", "c", "x", "z"))
    step, space = ("y", "c"), ("x", "z")
    row_split = P(step, space, None)
    return jax.shard_map(
        shards,
        mesh=mesh,
        in_specs=(row_split, P(step, None, None), row_split, row_split, row_split, P()),
        out_specs=(row_split, row_split, row_split),
        check_vma=False,
    )
```

time: 176 us -> 151 us (0.86)
  the two profiles are of different devices: /device:TPU:8 before, /device:TPU:2 now
where the time goes in v2:
time: 151 us; the launch traced here: 150 us
  starting transfers between devices  53.4 us (35%)
  waiting for transfers between devices  47.1 us (31%)
  local copies, waits for them, and re-layouts  31.1 us (21%)
  other arithmetic  9.08 us (6%)
  matrix products  6.76 us (4%)
  between operations  2.42 us (2%)
    unnamed x47, local copies, waits for them, and re-layouts  23 us
    all_to_all x1, starting transfers between devices, shards(): sent = lax.all_to_all(sent.reshape(nz, rows, -1), 'z', 0, 0, tiled=True)  19.5 us
    all_to_all x2, waiting for transfers between devices, spread(): lax.all_to_all(jnp.broadcast_to(v[None], (n,) + v.shape), axis, 0, 0, til...  16.5 us
    ppermute x4, waiting for transfers between devices, passed(): return lax.ppermute(v, axis, [(i, (i + by) % n) for i in range(n)])  16.1 us
    all_to_all x2, starting transfers between devices, spread(): lax.all_to_all(jnp.broadcast_to(v[None], (n,) + v.shape), axis, 0, 0, til...  14.6 us
    ppermute x4, starting transfers between devices, passed(): return lax.ppermute(v, axis, [(i, (i + by) % n) for i in range(n)])  13.2 us
    dot_general x4, matrix products, dot_t(): lax.dot_general(a, b, (((1,), (1,)), ((), ())), preferred_element_type=F3...  5.74 us
    ppermute x1, waiting for transfers between devices, shards(): packed = lax.ppermute(packed, ('y', 'c', 'x', 'z'), route)  5.53 us
  transfers between devices with their start and end apart: 9, of which 7 were waited for; matrix products, arithmetic and copies ran while one was open for 16% of the time, Pallas kernels for 0%

profile of v2, /device:TPU:2, one launch (start us, length us, event | category | flops | bytes accessed | tf_op | source)
XLA Modules:
  0.0 149.9 jit_solution(8059863252698370364)
XLA Ops:
  0.7 1.3 reduce-precision_convert_fusion.1
  4.1 1.3 collective-permute-start
  5.4 1.6 %broadcast_in_dim.100 = bf16[8,64,2048]{2,1,0:T(8,128)(2,1)} broadcast(bf16[64,2048]{1,0:T(8,128)(2,1)S(1)} %bitcast.181), dimensions={1,2} | broadcast | bytes 2359296 | tf_op jit(solution)/shard_map/broadcast_in_dim | solution.py:25
  6.9 10.3 %all-to-all-start = ((bf16[8,64,2048]{2,1,0:T(8,128)(2,1)}), bf16[8,64,2048]{2,1,0:T(8,128)(2,1)S(1)}, u32[]{:S(2)}, u32[]{:S(2)}) async-start(bf16[8,64,2048]{2,1,0:T(8,128)(2,1)} %broadcast_in_dim.100), calls=%async_computation | async-start | bytes 4194304 | tf_op jit(solution)/shard_map/all_to_all | solution.py:25
  17.4 5.5 %collective-permute-done = bf16[2,64,2176]{2,1,0:T(8,128)(2,1)S(1)} collective-permute-done((bf16[2,64,2176]{2,1,0:T(8,128)(2,1)}, bf16[2,64,2176]{2,1,0:T(8,128)(2,1)S(1)}, u32[]{:S(2)}, u32[]{:S(2)}) %collective-permute-start) | collective-permute-done | bytes 557088 | tf_op jit(solution)/shard_map/ppermute | solution.py:63
  22.9 3.7 %collective-permute-start.3 = (bf16[64,2176]{1,0:T(8,128)(2,1)S(1)}, bf16[64,2176]{1,0:T(8,128)(2,1)S(1)}, u32[]{:S(2)}, u32[]{:S(2)}) collective-permute-start(bf16[64,2176]{1,0:T(8,128)(2,1)S(1)} %get-tuple-element.15), channel_id=1, source_target_pairs={{0,16},{8,24},{16,0},{24,8},{1,17},{9,25},{17,1},{25,9},{2,18},{10... | collective-permute-start | bytes 835592 | tf_op jit(solution)/shard_map/ppermute | solution.py:30
  26.7 3.6 %collective-permute-start.4 = (bf16[64,2176]{1,0:T(8,128)(2,1)S(1)}, bf16[64,2176]{1,0:T(8,128)(2,1)S(1)}, u32[]{:S(2)}, u32[]{:S(2)}) collective-permute-start(bf16[64,2176]{1,0:T(8,128)(2,1)S(1)} %get-tuple-element.16), channel_id=1, source_target_pairs={{0,16},{8,24},{16,0},{24,8},{1,17},{9,25},{17,1},{25,9},{2,18},{10... | collective-permute-start | bytes 835592 | tf_op jit(solution)/shard_map/ppermute | solution.py:30
  30.3 1.9 %collective-permute-start.1 = (bf16[2,64,2176]{2,1,0:T(8,128)(2,1)S(1)}, bf16[2,64,2176]{2,1,0:T(8,128)(2,1)S(1)}, u32[]{:S(2)}, u32[]{:S(2)}) collective-permute-start(bf16[2,64,2176]{2,1,0:T(8,128)(2,1)S(1)} %collective-permute-done), channel_id=1, source_target_pairs={{0,8},{8,16},{16,24},{24,0},{1,9},{9,17},{17,25},{25,1},{2,10},{10... | collective-permute-start | bytes 1671176 | tf_op jit(solution)/shard_map/ppermute | solution.py:30
  32.2 3.9 %collective-permute-start.2 = (bf16[2,64,2176]{2,1,0:T(8,128)(2,1)S(1)}, bf16[2,64,2176]{2,1,0:T(8,128)(2,1)S(1)}, u32[]{:S(2)}, u32[]{:S(2)}) collective-permute-start(bf16[2,64,2176]{2,1,0:T(8,128)(2,1)S(1)} %collective-permute-done), channel_id=1, source_target_pairs={{0,24},{8,0},{16,8},{24,16},{1,25},{9,1},{17,9},{25,17},{2,26},{10... | collective-permute-start | bytes 1671176 | tf_op jit(solution)/shard_map/ppermute | solution.py:30
  36.5 9.8 %collective-permute-done.1 = bf16[2,64,2176]{2,1,0:T(8,128)(2,1)S(1)} collective-permute-done((bf16[2,64,2176]{2,1,0:T(8,128)(2,1)S(1)}, bf16[2,64,2176]{2,1,0:T(8,128)(2,1)S(1)}, u32[]{:S(2)}, u32[]{:S(2)}) %collective-permute-start.1) | collective-permute-done | bytes 557088 | tf_op jit(solution)/shard_map/ppermute | solution.py:30
  46.3 6.3 %collective-permute-done.2 = bf16[2,64,2176]{2,1,0:T(8,128)(2,1)S(1)} collective-permute-done((bf16[2,64,2176]{2,1,0:T(8,128)(2,1)S(1)}, bf16[2,64,2176]{2,1,0:T(8,128)(2,1)S(1)}, u32[]{:S(2)}, u32[]{:S(2)}) %collective-permute-start.2) | collective-permute-done | bytes 557088 | tf_op jit(solution)/shard_map/ppermute | solution.py:30
  52.8 1.6 %slice.226 = bf16[2,4,64,2048]{3,2,1,0:T(8,128)(2,1)} slice(bf16[2,4,64,2176]{3,2,1,0:T(8,128)(2,1)S(1)} %bitcast.165), slice={[0:2], [0:4], [0:64], [0:2048]} | slice | bytes 4194304 | tf_op jit(solution)/shard_map/slice | solution.py:72
  58.3 1.3 select_convert_fusion.1
  59.7 6.0 %all-to-all-done = bf16[8,64,2048]{2,1,0:T(8,128)(2,1)S(1)} async-done(((bf16[8,64,2048]{2,1,0:T(8,128)(2,1)}), bf16[8,64,2048]{2,1,0:T(8,128)(2,1)S(1)}, u32[]{:S(2)}, u32[]{:S(2)}) %all-to-all-start) | async-done | bytes 2097184 | tf_op jit(solution)/shard_map/all_to_all | solution.py:25
  66.4 2.9 %convolution_bitcast_fusion = f32[512,512]{1,0:T(8,128)S(1)} fusion(bf16[512,2048]{1,0:T(8,128)(2,1)} %bitcast.171, bf16[512,2048]{1,0:T(8,128)(2,1)S(1)} %bitcast.147), kind=kOutput, calls=%fused_computation.9 | convolution fusion | flops 1073741824 | bytes 5242880 | tf_op jit(solution)/shard_map/dot_general | solution.py:15
  71.4 19.5 %all-to-all-start.1 = ((f16[8,64,384]{2,1,0:T(8,128)(2,1)}), f16[8,64,384]{2,1,0:T(8,128)(2,1)S(1)}, u32[]{:S(2)}, u32[]{:S(2)}) async-start(f16[8,64,384]{2,1,0:T(8,128)(2,1)} %bitcast.29), calls=%async_computation.1 | async-start | bytes 786432 | tf_op jit(solution)/shard_map/all_to_all | solution.py:95
  101.5 4.3 %all-to-all-done.1 = f16[8,64,384]{2,1,0:T(8,128)(2,1)S(1)} async-done(((f16[8,64,384]{2,1,0:T(8,128)(2,1)}), f16[8,64,384]{2,1,0:T(8,128)(2,1)S(1)}, u32[]{:S(2)}, u32[]{:S(2)}) %all-to-all-start.1) | async-done | bytes 393248 | tf_op jit(solution)/shard_map/all_to_all | solution.py:95
  113.8 4.3 %all-to-all-start.2 = ((f16[4,8,64,256]{3,1,2,0:T(8,128)(2,1)}), f16[4,8,64,256]{3,1,2,0:T(8,128)(2,1)S(1)}, u32[]{:S(2)}, u32[]{:S(2)}) async-start(f16[4,8,64,256]{3,1,2,0:T(8,128)(2,1)} %broadcast_in_dim.103), calls=%async_computation.2 | async-start | bytes 2097152 | tf_op jit(solution)/shard_map/all_to_all | solution.py:25
  121.3 10.5 %all-to-all-done.2 = f16[4,8,64,256]{3,1,2,0:T(8,128)(2,1)S(1)} async-done(((f16[4,8,64,256]{3,1,2,0:T(8,128)(2,1)}), f16[4,8,64,256]{3,1,2,0:T(8,128)(2,1)S(1)}, u32[]{:S(2)}, u32[]{:S(2)}) %all-to-all-start.2) | async-done | bytes 1048608 | tf_op jit(solution)/shard_map/all_to_all | solution.py:25
  134.6 1.3 fusion.1
  136.8 4.9 %all-to-all-start.3 = ((f32[4,64,512]{2,1,0:T(8,128)}), f32[4,64,512]{2,1,0:T(8,128)S(1)}, u32[]{:S(2)}, u32[]{:S(2)}) async-start(f32[4,64,512]{2,1,0:T(8,128)} %bitcast.33), calls=%async_computation.3 | async-start | bytes 1048576 | tf_op jit(solution)/shard_map/all_to_all | solution.py:110
  141.7 1.4 constant_dynamic-update-slice_fusion.1
  143.0 1.4 constant_dynamic-update-slice_fusion
  144.4 4.6 %all-to-all-done.3 = f32[4,64,512]{2,1,0:T(8,128)S(1)} async-done(((f32[4,64,512]{2,1,0:T(8,128)}), f32[4,64,512]{2,1,0:T(8,128)S(1)}, u32[]{:S(2)}, u32[]{:S(2)}) %all-to-all-start.3) | async-done | bytes 524320 | tf_op jit(solution)/shard_map/all_to_all | solution.py:110
  (92 shorter events, 34.3 us)
Async XLA Ops:
  0.6 54.4 %copy-start = (f32[1,2048,64]{1,2,0:T(8,128)S(1)}, f32[1,2048,64]{1,2,0:T(8,128)}, u32[]{:S(2)}) copy-start(f32[1,2048,64]{1,2,0:T(8,128)} %param.7) | copy-start | bytes 1572868
  0.6 4.7 %copy-start.4 = (bf16[1,64,2048]{2,1,0:T(8,128)(2,1)S(1)}, bf16[1,64,2048]{2,1,0:T(8,128)(2,1)}, u32[]{:S(2)}) copy-start(bf16[1,64,2048]{2,1,0:T(8,128)(2,1)} %param.6) | copy-start | bytes 786436
  4.1 18.8 %collective-permute-start = (bf16[2,64,2176]{2,1,0:T(8,128)(2,1)}, bf16[2,64,2176]{2,1,0:T(8,128)(2,1)S(1)}, u32[]{:S(2)}, u32[]{:S(2)}) collective-permute-start(bf16[2,64,2176]{2,1,0:T(8,128)(2,1)} %pad_maximum_fusion), channel_id=1, source_target_pairs={{32,0},{33,8},{34,2},{35,10},{36,4},{37,12},{38,6},{39,14},{40,1},... | collective-permute-start | bytes 1671176 | tf_op jit(solution)/shard_map/ppermute | solution.py:63
  6.9 58.8 %all-to-all-start = ((bf16[8,64,2048]{2,1,0:T(8,128)(2,1)}), bf16[8,64,2048]{2,1,0:T(8,128)(2,1)S(1)}, u32[]{:S(2)}, u32[]{:S(2)}) async-start(bf16[8,64,2048]{2,1,0:T(8,128)(2,1)} %broadcast_in_dim.100), calls=%async_computation | async-start | bytes 4194304 | tf_op jit(solution)/shard_map/all_to_all | solution.py:25
  22.9 29.8 %collective-permute-start.3 = (bf16[64,2176]{1,0:T(8,128)(2,1)S(1)}, bf16[64,2176]{1,0:T(8,128)(2,1)S(1)}, u32[]{:S(2)}, u32[]{:S(2)}) collective-permute-start(bf16[64,2176]{1,0:T(8,128)(2,1)S(1)} %get-tuple-element.15), channel_id=1, source_target_pairs={{0,16},{8,24},{16,0},{24,8},{1,17},{9,25},{17,1},{25,9},{2,18},{10... | collective-permute-start | bytes 835592 | tf_op jit(solution)/shard_map/ppermute | solution.py:30
  26.7 26.0 %collective-permute-start.4 = (bf16[64,2176]{1,0:T(8,128)(2,1)S(1)}, bf16[64,2176]{1,0:T(8,128)(2,1)S(1)}, u32[]{:S(2)}, u32[]{:S(2)}) collective-permute-start(bf16[64,2176]{1,0:T(8,128)(2,1)S(1)} %get-tuple-element.16), channel_id=1, source_target_pairs={{0,16},{8,24},{16,0},{24,8},{1,17},{9,25},{17,1},{25,9},{2,18},{10... | collective-permute-start | bytes 835592 | tf_op jit(solution)/shard_map/ppermute | solution.py:30
  30.3 16.0 %collective-permute-start.1 = (bf16[2,64,2176]{2,1,0:T(8,128)(2,1)S(1)}, bf16[2,64,2176]{2,1,0:T(8,128)(2,1)S(1)}, u32[]{:S(2)}, u32[]{:S(2)}) collective-permute-start(bf16[2,64,2176]{2,1,0:T(8,128)(2,1)S(1)} %collective-permute-done), channel_id=1, source_target_pairs={{0,8},{8,16},{16,24},{24,0},{1,9},{9,17},{17,25},{25,1},{2,10},{10... | collective-permute-start | bytes 1671176 | tf_op jit(solution)/shard_map/ppermute | solution.py:30
  32.2 20.4 %collective-permute-start.2 = (bf16[2,64,2176]{2,1,0:T(8,128)(2,1)S(1)}, bf16[2,64,2176]{2,1,0:T(8,128)(2,1)S(1)}, u32[]{:S(2)}, u32[]{:S(2)}) collective-permute-start(bf16[2,64,2176]{2,1,0:T(8,128)(2,1)S(1)} %collective-permute-done), channel_id=1, source_target_pairs={{0,24},{8,0},{16,8},{24,16},{1,25},{9,1},{17,9},{25,17},{2,26},{10... | collective-permute-start | bytes 1671176 | tf_op jit(solution)/shard_map/ppermute | solution.py:30
  69.3 1.0 copy-start.2
  71.4 34.4 %all-to-all-start.1 = ((f16[8,64,384]{2,1,0:T(8,128)(2,1)}), f16[8,64,384]{2,1,0:T(8,128)(2,1)S(1)}, u32[]{:S(2)}, u32[]{:S(2)}) async-start(f16[8,64,384]{2,1,0:T(8,128)(2,1)} %bitcast.29), calls=%async_computation.1 | async-start | bytes 786432 | tf_op jit(solution)/shard_map/all_to_all | solution.py:95
  106.2 14.5 %copy-start.1 = (f32[8,64,256]{2,1,0:T(8,128)}, f32[8,64,256]{2,1,0:T(8,128)S(1)}, u32[]{:S(2)}) copy-start(f32[8,64,256]{2,1,0:T(8,128)S(1)} %convert_multiply_fusion.1) | copy-start | bytes 1572868
  112.5 6.0 %copy-start.3 = (f32[1,64,2048]{2,1,0:T(8,128)S(1)}, f32[1,64,2048]{2,1,0:T(8,128)}, u32[]{:S(2)}) copy-start(f32[1,64,2048]{2,1,0:T(8,128)} %param.8) | copy-start | bytes 1572868
  112.7 5.5 %copy-start.6 = (f32[64,64]{1,0:T(8,128)S(1)}, f32[64,64]{1,0:T(8,128)}, u32[]{:S(2)}) copy-start(f32[64,64]{1,0:T(8,128)} %param.11) | copy-start | bytes 49156
  113.8 18.1 %all-to-all-start.2 = ((f16[4,8,64,256]{3,1,2,0:T(8,128)(2,1)}), f16[4,8,64,256]{3,1,2,0:T(8,128)(2,1)S(1)}, u32[]{:S(2)}, u32[]{:S(2)}) async-start(f16[4,8,64,256]{3,1,2,0:T(8,128)(2,1)} %broadcast_in_dim.103), calls=%async_computation.2 | async-start | bytes 2097152 | tf_op jit(solution)/shard_map/all_to_all | solution.py:25
  118.5 13.7 %copy-start.5 = (f32[64,64]{1,0:T(8,128)}, f32[64,64]{1,0:T(8,128)S(1)}, u32[]{:S(2)}) copy-start(f32[64,64]{1,0:T(8,128)S(1)} %convolution_add_fusion.1) | copy-start | bytes 49156
  133.0 1.6 %copy-start.7 = (bf16[512,2048]{1,0:T(8,128)(2,1)S(1)}, bf16[512,2048]{1,0:T(8,128)(2,1)}, u32[]{:S(2)}) copy-start(bf16[512,2048]{1,0:T(8,128)(2,1)} %slice_dynamic-update-slice_fusion) | copy-start | bytes 6291460
  136.8 12.2 %all-to-all-start.3 = ((f32[4,64,512]{2,1,0:T(8,128)}), f32[4,64,512]{2,1,0:T(8,128)S(1)}, u32[]{:S(2)}, u32[]{:S(2)}) async-start(f32[4,64,512]{2,1,0:T(8,128)} %bitcast.33), calls=%async_computation.3 | async-start | bytes 1048576 | tf_op jit(solution)/shard_map/all_to_all | solution.py:110

commit v3 on v2

v3 whole, which is shorter than its diff:
```python
import functools

import jax
import jax.numpy as jnp
from jax import lax
from jax.experimental import pallas as pl
from jax.experimental.pallas import tpu as pltpu
from jax.sharding import Mesh, PartitionSpec as P

F32, F16, BF16 = jnp.float32, jnp.float16, jnp.bfloat16
HIGH = lax.Precision.HIGH


def exponent(largest):
    return jnp.floor(jnp.log(jnp.clip(largest, 1e-30, 1e38)) * 1.4426950408889634)


def dot_t(a, b, **kw):
    return lax.dot_general(a, b, (((1,), (1,)), ((), ())), preferred_element_type=F32, **kw)


def two_parts(v):
    top = lax.reduce_precision(v, 8, 7)
    return top.astype(BF16), (v - top).astype(BF16)


def spread(v, axis):
    n = lax.axis_size(axis)
    return lax.all_to_all(jnp.broadcast_to(v[None], (n,) + v.shape), axis, 0, 0, tiled=True)


def passed(v, axis, by):
    n = lax.axis_size(axis)
    return lax.ppermute(v, axis, [(i, (i + by) % n) for i in range(n)])


def halves(first, second):
    lane = lax.broadcasted_iota(jnp.int32, first.shape, 1)
    low = jnp.where(lane < 64, first, pltpu.roll(second, 64, 1))
    high = jnp.where(lane < 64, pltpu.roll(first, 64, 1), second)
    return low, high


def pack_kernel(nx, nz, c_ref, s_ref, a_ref, copies_ref, packed_ref):
    rows, ns = s_ref.shape
    nf = a_ref.shape[1]
    run = 2 * rows

    def put(at, value):
        top = value.astype(BF16)
        packed_ref[0, :, at : at + value.shape[1]] = top
        low = (value - top.astype(F32)).astype(BF16)
        packed_ref[1, :, at : at + value.shape[1]] = low

    total = jnp.zeros((rows, run), F32)
    for q in range(nx // 2):
        for k in range(nz // 2):
            first = slice((2 * q * nz // 2 + k) * run, (2 * q * nz // 2 + k + 1) * run)
            second = slice(first.start + nz // 2 * run, first.stop + nz // 2 * run)
            pair = s_ref[:, first], s_ref[:, second]
            total = total + jnp.abs(pair[0]) + jnp.abs(pair[1])
            for h, value in enumerate(halves(*pair)):
                put(((2 * k + h) * nx // 2 + q) * run, value)
            pair = c_ref[:, first].astype(F32), c_ref[:, second].astype(F32)
            for h, value in enumerate(halves(*pair)):
                at = ((2 * k + h) * nx // 2 + q) * run
                value = value.astype(BF16)
                for z in range(nz):
                    copies_ref[z, :, at : at + run] = value
    a_own = a_ref[...]
    bound_a = jnp.max(jnp.abs(a_own), axis=1, keepdims=True)
    bound = 0.125 * jnp.sum(total, axis=1, keepdims=True) + 0.75 * nf * bound_a
    lane = lax.broadcasted_iota(jnp.int32, (rows, nf), 1)
    exps = jnp.where(lane == 0, exponent(bound), exponent(0.125 * nx * rows * bound_a)) + 2
    put(ns, jnp.concatenate([a_own, exps], axis=1))


def natural_kernel(nx, nz, in_ref, out_ref):
    rows = out_ref.shape[0]
    run = 2 * rows
    for q in range(nx // 2):
        for k in range(nz // 2):
            cut = slice(q * run, (q + 1) * run)
            pair = halves(in_ref[2 * k, :, cut], in_ref[2 * k + 1, :, cut])
            for h, value in enumerate(pair):
                at = ((2 * q + h) * nz // 2 + k) * run
                out_ref[:, at : at + run] = value


def shards(coupling, arrow_link, local_cov, boundary_cov, boundary_arrow, fixed_cov):
    c_own, link, local = coupling[0], arrow_link[0], local_cov[0]
    s_own, a_own = boundary_cov[0], boundary_arrow[0]
    nx, nz = lax.axis_size("x"), lax.axis_size("z")
    steps = lax.axis_size("y") * lax.axis_size("c")
    group = nx * nz
    rows, ns = c_own.shape
    nf = a_own.shape[1]
    cols = nx * rows
    ix, iz = lax.axis_index("x"), lax.axis_index("z")

    copies, packed = pl.pallas_call(
        functools.partial(pack_kernel, nx, nz),
        out_shape=(
            jax.ShapeDtypeStruct((nz, rows, ns), BF16),
            jax.ShapeDtypeStruct((2, rows, ns + 2 * nf), BF16),
        ),
        compiler_params=pltpu.CompilerParams(vmem_limit_bytes=32 << 20),
    )(c_own, s_own, a_own)
    route = [(t * group + b, (t - 1) * group + b) for t in range(1, steps) for b in range(group)]
    packed = lax.ppermute(packed, ("y", "c", "x", "z"), route)
    before, after = passed(packed, "x", 1), passed(packed, "x", -1)
    far_top, far_low = passed(packed[0], "x", 2), passed(packed[1], "x", -2)
    succ = jnp.zeros((nx,) + packed.shape, BF16)
    for by, block in ((0, packed), (nx - 1, before), (1, after)):
        succ = lax.dynamic_update_index_in_dim(succ, block, (ix + by) % nx, 0)
    far = jnp.stack([far_top, far_low])
    succ = lax.dynamic_update_index_in_dim(succ, far, (ix + 2) % nx, 0)
    succ = succ.transpose(1, 0, 2, 3)
    s_cols = succ[..., :ns].reshape(2 * cols, ns)
    a_two = succ[..., ns : ns + nf].reshape(2, cols, nf)
    exps = jnp.max(succ[0, :, :, ns + nf : ns + nf + 2].astype(F32), axis=(0, 1))

    link_rows = lax.dynamic_slice_in_dim(link, ix * nz * rows, nz * rows, 0)
    arrow_term = dot_t(link_rows, a_two[0].astype(F32) + a_two[1].astype(F32), precision=HIGH)
    place = jnp.concatenate([a_two[0], a_two[1]], axis=1)
    s_cols, arrow_term, place = lax.optimization_barrier((s_cols, arrow_term, place))

    c_rows = lax.all_to_all(copies, "z", 0, 0, tiled=True).reshape(nz * rows, ns)

    cross2 = dot_t(c_rows, s_cols)
    cross = (cross2[:, :cols] + cross2[:, cols:] + arrow_term) * jnp.exp2(14 - exps[0])
    c_here = lax.dynamic_slice_in_dim(c_rows, iz * cols, cols, 1)
    share2 = jnp.dot(c_here, place, preferred_element_type=F32)
    share = (share2[:, :nf] + share2[:, nf:]) * jnp.exp2(14 - exps[1])
    lane = lax.broadcasted_iota(jnp.int32, (nz * rows, nf), 1)
    marks = jnp.where(lane == 0, exps[0], exps[1])
    sent = jnp.concatenate([cross.astype(F16), share.astype(F16), marks.astype(F16)], axis=1)
    sent = lax.all_to_all(sent.reshape(nz, rows, -1), "z", 0, 0, tiled=True)
    cross = sent[..., :cols]
    marks = sent[:, :1, cols + nf : cols + nf + 2].astype(F32)
    scale = jnp.exp2(marks[..., :1] - 14)

    every = spread(cross, "x").astype(F32) * scale[None]
    every = every.transpose(0, 2, 1, 3).reshape(cols, ns)
    diag2 = dot_t(jnp.concatenate(two_parts(every), axis=0), c_rows)
    diag = (diag2[:cols] + diag2[cols:]).reshape(nx, rows, nz * rows)
    diag = lax.all_to_all(diag, "x", 0, 0, tiled=True)

    cross_rows = pl.pallas_call(
        functools.partial(natural_kernel, nx, nz),
        out_shape=jax.ShapeDtypeStruct((rows, ns), F32),
    )(cross.astype(F32) * scale)
    share = sent[..., cols : cols + nf].astype(F32) * jnp.exp2(marks[..., 1:] - 14)
    link_own = lax.dynamic_slice_in_dim(link, (ix * nz + iz) * rows, rows, 0)
    arrow = jnp.dot(link_own, fixed_cov, precision=lax.Precision.HIGHEST)
    arrow = jnp.sum(share, axis=0) + arrow
    local = lax.optimization_barrier(local + dot_t(arrow, link, precision=HIGH))
    diag_rows = local + diag.transpose(1, 0, 2).reshape(rows, ns)
    return (diag_rows[None], cross_rows[None], arrow[None])


def solution(mesh):
    mesh = Mesh(mesh.devices.reshape(8, 2, 4, 8), ("y", "c", "x", "z"))
    step, space = ("y", "c"), ("x", "z")
    row_split = P(step, space, None)
    return jax.shard_map(
        shards,
        mesh=mesh,
        in_specs=(row_split, P(step, None, None), row_split, row_split, row_split, P()),
        out_specs=(row_split, row_split, row_split),
        check_vma=False,
    )
```

time: 151 us -> 131 us (0.87)
  the two profiles are of different devices: /device:TPU:2 before, /device:TPU:56 now
where the time goes in v3:
time: 131 us
  waiting for transfers between devices  48.4 us (37%)
  starting transfers between devices  35.2 us (27%)
  blocking collectives  17.6 us (13%)
  local copies, waits for them, and re-layouts  11.1 us (8%)
  matrix products  6.26 us (5%)
  other arithmetic  5.7 us (4%)
  Pallas kernels  4.12 us (3%)
  between operations  2.33 us (2%)
    all_to_all x1, blocking collectives, shards(): sent = lax.all_to_all(sent.reshape(nz, rows, -1), 'z', 0, 0, tiled=True)  17.6 us
    all_to_all x1, waiting for transfers between devices, shards(): lax.all_to_all(copies, 'z', 0, 0, tiled=True).reshape(nz * rows, ns)  14.7 us
    ppermute x4, starting transfers between devices, passed(): return lax.ppermute(v, axis, [(i, (i + by) % n) for i in range(n)])  14.4 us
    ppermute x4, waiting for transfers between devices, passed(): return lax.ppermute(v, axis, [(i, (i + by) % n) for i in range(n)])  14.4 us
    all_to_all x1, waiting for transfers between devices, spread(): lax.all_to_all(jnp.broadcast_to(v[None], (n,) + v.shape), axis, 0, 0, til...  11.6 us
    all_to_all x1, starting transfers between devices, shards(): lax.all_to_all(copies, 'z', 0, 0, tiled=True).reshape(nz * rows, ns)  10.3 us
    all_to_all x1, waiting for transfers between devices, shards(): diag = lax.all_to_all(diag, 'x', 0, 0, tiled=True)  7.64 us
    dot_general x4, matrix products, dot_t(): lax.dot_general(a, b, (((1,), (1,)), ((), ())), preferred_element_type=F3...  5.72 us
  transfers between devices with their start and end apart: 8, of which 5 were waited for; matrix products, arithmetic and copies ran while one was open for 7% of the time, Pallas kernels for 2%

profile of v3, /device:TPU:56, one launch (start us, length us, event | category | flops | bytes accessed | tf_op | source)
XLA Modules:
  0.0 130.6 jit_solution(6327242265340341924)
XLA Ops:
  0.7 1.1 copy-done.1
  3.5 2.1 %shard_map.85 = (bf16[8,64,2048]{2,1,0:T(8,128)(2,1)}, bf16[2,64,2176]{2,1,0:T(8,128)(2,1)S(1)}) custom-call(bf16[64,2048]{1,0:T(8,128)(2,1)S(1)} %bitcast.67, f32[64,2048]{1,0:T(8,128)S(1)} %bitcast.66, f32[64,64]{1,0:T(8,128)S(1)} %bitcast.68), custom_call_target="tpu_custom_call" | custom-call | tf_op jit(solution)/shard_map/pallas_call | solution.py:101
  5.5 2.7 %collective-permute-start = (bf16[2,64,2176]{2,1,0:T(8,128)(2,1)S(1)}, bf16[2,64,2176]{2,1,0:T(8,128)(2,1)}, u32[]{:S(2)}, u32[]{:S(2)}) collective-permute-start(bf16[2,64,2176]{2,1,0:T(8,128)(2,1)S(1)} %get-tuple-element.9), channel_id=1, source_target_pairs={{32,0},{33,1},{34,2},{35,3},{36,4},{37,5},{38,6},{39,7},{40,8},{41... | collective-permute-start | bytes 1671176 | tf_op jit(solution)/shard_map/ppermute | solution.py:110
  8.2 10.3 %all-to-all-start = ((bf16[8,64,2048]{2,1,0:T(8,128)(2,1)}), bf16[8,64,2048]{2,1,0:T(8,128)(2,1)S(1)}, u32[]{:S(2)}, u32[]{:S(2)}) async-start(bf16[8,64,2048]{2,1,0:T(8,128)(2,1)} %get-tuple-element.8), calls=%async_computation | async-start | bytes 4194304 | tf_op jit(solution)/shard_map/all_to_all | solution.py:128
  18.6 1.1 slice_bitcast_fusion.1
  19.7 4.9 %collective-permute-start.3 = (bf16[64,2176]{1,0:T(8,128)(2,1)S(1)}, bf16[64,2176]{1,0:T(8,128)(2,1)S(1)}, u32[]{:S(2)}, u32[]{:S(2)}) collective-permute-start(bf16[64,2176]{1,0:T(8,128)(2,1)S(1)} %get-tuple-element.19), channel_id=1, source_target_pairs={{0,16},{8,24},{16,0},{24,8},{1,17},{9,25},{17,1},{25,9},{2,18},{10... | collective-permute-start | bytes 835592 | tf_op jit(solution)/shard_map/ppermute | solution.py:34
  24.6 2.4 %collective-permute-start.4 = (bf16[64,2176]{1,0:T(8,128)(2,1)S(1)}, bf16[64,2176]{1,0:T(8,128)(2,1)S(1)}, u32[]{:S(2)}, u32[]{:S(2)}) collective-permute-start(bf16[64,2176]{1,0:T(8,128)(2,1)S(1)} %get-tuple-element.20), channel_id=1, source_target_pairs={{0,16},{8,24},{16,0},{24,8},{1,17},{9,25},{17,1},{25,9},{2,18},{10... | collective-permute-start | bytes 835592 | tf_op jit(solution)/shard_map/ppermute | solution.py:34
  27.0 3.4 %collective-permute-start.1 = (bf16[2,64,2176]{2,1,0:T(8,128)(2,1)}, bf16[2,64,2176]{2,1,0:T(8,128)(2,1)S(1)}, u32[]{:S(2)}, u32[]{:S(2)}) collective-permute-start(bf16[2,64,2176]{2,1,0:T(8,128)(2,1)} %collective-permute-done), channel_id=1, source_target_pairs={{0,8},{8,16},{16,24},{24,0},{1,9},{9,17},{17,25},{25,1},{2,10},{10... | collective-permute-start | bytes 1671176 | tf_op jit(solution)/shard_map/ppermute | solution.py:34
  30.4 3.7 %collective-permute-start.2 = (bf16[2,64,2176]{2,1,0:T(8,128)(2,1)}, bf16[2,64,2176]{2,1,0:T(8,128)(2,1)S(1)}, u32[]{:S(2)}, u32[]{:S(2)}) collective-permute-start(bf16[2,64,2176]{2,1,0:T(8,128)(2,1)} %collective-permute-done), channel_id=1, source_target_pairs={{0,24},{8,0},{16,8},{24,16},{1,25},{9,1},{17,9},{25,17},{2,26},{10... | collective-permute-start | bytes 1671176 | tf_op jit(solution)/shard_map/ppermute | solution.py:34
  34.4 1.1 bitcast_dynamic-update-slice_fusion.2
  35.5 14.3 %collective-permute-done.1 = bf16[2,64,2176]{2,1,0:T(8,128)(2,1)S(1)} collective-permute-done((bf16[2,64,2176]{2,1,0:T(8,128)(2,1)}, bf16[2,64,2176]{2,1,0:T(8,128)(2,1)S(1)}, u32[]{:S(2)}, u32[]{:S(2)}) %collective-permute-start.1) | collective-permute-done | bytes 557088 | tf_op jit(solution)/shard_map/ppermute | solution.py:34
  50.1 1.6 %slice.87 = bf16[2,4,64,2048]{3,2,1,0:T(8,128)(2,1)} slice(bf16[2,4,64,2176]{3,2,1,0:T(8,128)(2,1)S(1)} %bitcast.69), slice={[0:2], [0:4], [0:64], [0:2048]} | slice | bytes 4194304 | tf_op jit(solution)/shard_map/slice | solution.py:119
  54.4 1.3 fusion.28
  55.7 14.7 %all-to-all-done = bf16[8,64,2048]{2,1,0:T(8,128)(2,1)S(1)} async-done(((bf16[8,64,2048]{2,1,0:T(8,128)(2,1)}), bf16[8,64,2048]{2,1,0:T(8,128)(2,1)S(1)}, u32[]{:S(2)}, u32[]{:S(2)}) %all-to-all-start) | async-done | bytes 2097184 | tf_op jit(solution)/shard_map/all_to_all | solution.py:128
  70.5 3.6 %fusion.32 = f32[512,512]{1,0:T(8,128)S(1)} fusion(bf16[512,2048]{1,0:T(8,128)(2,1)S(1)} %bitcast.75, bf16[512,2048]{1,0:T(8,128)(2,1)} %bitcast.79), kind=kOutput, calls=%fused_computation.57 | convolution fusion | flops 1073741824 | bytes 5242880 | tf_op jit(solution)/shard_map/dot_general | solution.py:19
  74.8 17.6 %all_to_all.20 = f16[8,64,384]{2,1,0:T(8,128)(2,1)S(1)} all-to-all(f16[8,64,384]{2,1,0:T(8,128)(2,1)S(1)} %bitcast.81), channel_id=1, replica_groups=mesh['y'=8,'c'=2,'x'=4,'z'=8] {'z'}, dimensions={0} | all-to-all | bytes 786432 | tf_op jit(solution)/shard_map/all_to_all | solution.py:138
  92.6 1.1 broadcast_in_dim.47
  93.6 4.3 %all-to-all-start.2 = ((f16[4,8,64,256]{3,1,2,0:T(8,128)(2,1)}), f16[4,8,64,256]{3,1,2,0:T(8,128)(2,1)S(1)}, u32[]{:S(2)}, u32[]{:S(2)}) async-start(f16[4,8,64,256]{3,1,2,0:T(8,128)(2,1)} %broadcast_in_dim.47), calls=%async_computation.2 | async-start | bytes 2097152 | tf_op jit(solution)/shard_map/all_to_all | solution.py:29
  99.1 2.0 %shard_map.86 = f32[64,2048]{1,0:T(8,128)} custom-call(f32[8,64,256]{2,1,0:T(8,128)} %convert_multiply_fusion.1.in_ref), custom_call_target="tpu_custom_call" | custom-call | tf_op jit(solution)/shard_map/pallas_call | solution.py:149
  101.3 11.6 %all-to-all-done.2 = f16[4,8,64,256]{3,1,2,0:T(8,128)(2,1)S(1)} async-done(((f16[4,8,64,256]{3,1,2,0:T(8,128)(2,1)}), f16[4,8,64,256]{3,1,2,0:T(8,128)(2,1)S(1)}, u32[]{:S(2)}, u32[]{:S(2)}) %all-to-all-start.2) | async-done | bytes 1048608 | tf_op jit(solution)/shard_map/all_to_all | solution.py:29
  114.4 1.2 copy-done.5
  115.6 1.3 fusion.1
  117.8 3.5 %all-to-all-start.3 = ((f32[4,64,512]{2,1,0:T(8,128)}), f32[4,64,512]{2,1,0:T(8,128)S(1)}, u32[]{:S(2)}, u32[]{:S(2)}) async-start(f32[4,64,512]{2,1,0:T(8,128)} %bitcast.29), calls=%async_computation.3 | async-start | bytes 1048576 | tf_op jit(solution)/shard_map/all_to_all | solution.py:147
  122.0 7.6 %all-to-all-done.3 = f32[4,64,512]{2,1,0:T(8,128)S(1)} async-done(((f32[4,64,512]{2,1,0:T(8,128)}), f32[4,64,512]{2,1,0:T(8,128)S(1)}, u32[]{:S(2)}, u32[]{:S(2)}) %all-to-all-start.3) | async-done | bytes 524320 | tf_op jit(solution)/shard_map/all_to_all | solution.py:147
  (49 shorter events, 9.7 us)
Async XLA Ops:
  0.6 51.2 %copy-start = (f32[1,2048,64]{1,2,0:T(8,128)S(1)}, f32[1,2048,64]{1,2,0:T(8,128)}, u32[]{:S(2)}) copy-start(f32[1,2048,64]{1,2,0:T(8,128)} %param.7) | copy-start | bytes 1572868
  0.6 1.1 copy-start.1
  1.7 0.9 copy-start.2
  2.7 0.8 copy-start.3
  5.5 13.0 %collective-permute-start = (bf16[2,64,2176]{2,1,0:T(8,128)(2,1)S(1)}, bf16[2,64,2176]{2,1,0:T(8,128)(2,1)}, u32[]{:S(2)}, u32[]{:S(2)}) collective-permute-start(bf16[2,64,2176]{2,1,0:T(8,128)(2,1)S(1)} %get-tuple-element.9), channel_id=1, source_target_pairs={{32,0},{33,1},{34,2},{35,3},{36,4},{37,5},{38,6},{39,7},{40,8},{41... | collective-permute-start | bytes 1671176 | tf_op jit(solution)/shard_map/ppermute | solution.py:110
  8.2 62.2 %all-to-all-start = ((bf16[8,64,2048]{2,1,0:T(8,128)(2,1)}), bf16[8,64,2048]{2,1,0:T(8,128)(2,1)S(1)}, u32[]{:S(2)}, u32[]{:S(2)}) async-start(bf16[8,64,2048]{2,1,0:T(8,128)(2,1)} %get-tuple-element.8), calls=%async_computation | async-start | bytes 4194304 | tf_op jit(solution)/shard_map/all_to_all | solution.py:128
  19.7 30.3 %collective-permute-start.3 = (bf16[64,2176]{1,0:T(8,128)(2,1)S(1)}, bf16[64,2176]{1,0:T(8,128)(2,1)S(1)}, u32[]{:S(2)}, u32[]{:S(2)}) collective-permute-start(bf16[64,2176]{1,0:T(8,128)(2,1)S(1)} %get-tuple-element.19), channel_id=1, source_target_pairs={{0,16},{8,24},{16,0},{24,8},{1,17},{9,25},{17,1},{25,9},{2,18},{10... | collective-permute-start | bytes 835592 | tf_op jit(solution)/shard_map/ppermute | solution.py:34
  24.6 25.4 %collective-permute-start.4 = (bf16[64,2176]{1,0:T(8,128)(2,1)S(1)}, bf16[64,2176]{1,0:T(8,128)(2,1)S(1)}, u32[]{:S(2)}, u32[]{:S(2)}) collective-permute-start(bf16[64,2176]{1,0:T(8,128)(2,1)S(1)} %get-tuple-element.20), channel_id=1, source_target_pairs={{0,16},{8,24},{16,0},{24,8},{1,17},{9,25},{17,1},{25,9},{2,18},{10... | collective-permute-start | bytes 835592 | tf_op jit(solution)/shard_map/ppermute | solution.py:34
  27.0 22.8 %collective-permute-start.1 = (bf16[2,64,2176]{2,1,0:T(8,128)(2,1)}, bf16[2,64,2176]{2,1,0:T(8,128)(2,1)S(1)}, u32[]{:S(2)}, u32[]{:S(2)}) collective-permute-start(bf16[2,64,2176]{2,1,0:T(8,128)(2,1)} %collective-permute-done), channel_id=1, source_target_pairs={{0,8},{8,16},{16,24},{24,0},{1,9},{9,17},{17,25},{25,1},{2,10},{10... | collective-permute-start | bytes 1671176 | tf_op jit(solution)/shard_map/ppermute | solution.py:34
  30.4 19.5 %collective-permute-start.2 = (bf16[2,64,2176]{2,1,0:T(8,128)(2,1)}, bf16[2,64,2176]{2,1,0:T(8,128)(2,1)S(1)}, u32[]{:S(2)}, u32[]{:S(2)}) collective-permute-start(bf16[2,64,2176]{2,1,0:T(8,128)(2,1)} %collective-permute-done), channel_id=1, source_target_pairs={{0,24},{8,0},{16,8},{24,16},{1,25},{9,1},{17,9},{25,17},{2,26},{10... | collective-permute-start | bytes 1671176 | tf_op jit(solution)/shard_map/ppermute | solution.py:34
  70.5 3.6 %copy-start.4 = (bf16[8,64,2048]{2,1,0:T(8,128)(2,1)}, bf16[8,64,2048]{2,1,0:T(8,128)(2,1)S(1)}, u32[]{:S(2)}) copy-start(bf16[8,64,2048]{2,1,0:T(8,128)(2,1)S(1)} %all-to-all-done) | copy-start | bytes 6291460
  93.6 19.2 %all-to-all-start.2 = ((f16[4,8,64,256]{3,1,2,0:T(8,128)(2,1)}), f16[4,8,64,256]{3,1,2,0:T(8,128)(2,1)S(1)}, u32[]{:S(2)}, u32[]{:S(2)}) async-start(f16[4,8,64,256]{3,1,2,0:T(8,128)(2,1)} %broadcast_in_dim.47), calls=%async_computation.2 | async-start | bytes 2097152 | tf_op jit(solution)/shard_map/all_to_all | solution.py:29
  114.0 1.6 %copy-start.5 = (bf16[8,64,2048]{2,1,0:T(8,128)(2,1)S(1)}, bf16[8,64,2048]{2,1,0:T(8,128)(2,1)}, u32[]{:S(2)}) copy-start(bf16[8,64,2048]{2,1,0:T(8,128)(2,1)} %copy-done.4) | copy-start | bytes 6291460
  116.9 4.4 %copy-start.8 = (f32[64,64]{1,0:T(8,128)S(1)}, f32[64,64]{1,0:T(8,128)}, u32[]{:S(2)}) copy-start(f32[64,64]{1,0:T(8,128)} %param.11) | copy-start | bytes 49156
  116.9 4.7 %copy-start.6 = (f32[1,64,2048]{2,1,0:T(8,128)S(1)}, f32[1,64,2048]{2,1,0:T(8,128)}, u32[]{:S(2)}) copy-start(f32[1,64,2048]{2,1,0:T(8,128)} %param.8) | copy-start | bytes 1572868
  117.8 11.9 %all-to-all-start.3 = ((f32[4,64,512]{2,1,0:T(8,128)}), f32[4,64,512]{2,1,0:T(8,128)S(1)}, u32[]{:S(2)}, u32[]{:S(2)}) async-start(f32[4,64,512]{2,1,0:T(8,128)} %bitcast.29), calls=%async_computation.3 | async-start | bytes 1048576 | tf_op jit(solution)/shard_map/all_to_all | solution.py:147
  121.7 8.9 %copy-start.7 = (f32[64,64]{1,0:T(8,128)}, f32[64,64]{1,0:T(8,128)S(1)}, u32[]{:S(2)}) copy-start(f32[64,64]{1,0:T(8,128)S(1)} %convolution_add_fusion.1) | copy-start | bytes 49156

commit v4 on v3

--- a/solution.py
+++ b/solution.py
@@ -41,7 +41,7 @@
     return low, high
 
 
-def pack_kernel(nx, nz, c_ref, s_ref, a_ref, copies_ref, packed_ref):
+def pack_kernel(nx, nz, c_ref, s_ref, a_ref, turned_ref, packed_ref):
     rows, ns = s_ref.shape
     nf = a_ref.shape[1]
     run = 2 * rows
@@ -64,9 +64,7 @@
             pair = c_ref[:, first].astype(F32), c_ref[:, second].astype(F32)
             for h, value in enumerate(halves(*pair)):
                 at = ((2 * k + h) * nx // 2 + q) * run
-                value = value.astype(BF16)
-                for z in range(nz):
-                    copies_ref[z, :, at : at + run] = value
+                turned_ref[:, at : at + run] = value.astype(BF16)
     a_own = a_ref[...]
     bound_a = jnp.max(jnp.abs(a_own), axis=1, keepdims=True)
     bound = 0.125 * jnp.sum(total, axis=1, keepdims=True) + 0.75 * nf * bound_a
@@ -98,23 +96,17 @@
     cols = nx * rows
     ix, iz = lax.axis_index("x"), lax.axis_index("z")
 
-    copies, packed = pl.pallas_call(
+    turned, packed = pl.pallas_call(
         functools.partial(pack_kernel, nx, nz),
         out_shape=(
-            jax.ShapeDtypeStruct((nz, rows, ns), BF16),
+            jax.ShapeDtypeStruct((rows, ns), BF16),
             jax.ShapeDtypeStruct((2, rows, ns + 2 * nf), BF16),
         ),
         compiler_params=pltpu.CompilerParams(vmem_limit_bytes=32 << 20),
     )(c_own, s_own, a_own)
     route = [(t * group + b, (t - 1) * group + b) for t in range(1, steps) for b in range(group)]
     packed = lax.ppermute(packed, ("y", "c", "x", "z"), route)
-    before, after = passed(packed, "x", 1), passed(packed, "x", -1)
-    far_top, far_low = passed(packed[0], "x", 2), passed(packed[1], "x", -2)
-    succ = jnp.zeros((nx,) + packed.shape, BF16)
-    for by, block in ((0, packed), (nx - 1, before), (1, after)):
-        succ = lax.dynamic_update_index_in_dim(succ, block, (ix + by) % nx, 0)
-    far = jnp.stack([far_top, far_low])
-    succ = lax.dynamic_update_index_in_dim(succ, far, (ix + 2) % nx, 0)
+    succ = spread(packed, "x")
     succ = succ.transpose(1, 0, 2, 3)
     s_cols = succ[..., :ns].reshape(2 * cols, ns)
     a_two = succ[..., ns : ns + nf].reshape(2, cols, nf)
@@ -125,7 +117,18 @@
     place = jnp.concatenate([a_two[0], a_two[1]], axis=1)
     s_cols, arrow_term, place = lax.optimization_barrier((s_cols, arrow_term, place))
 
-    c_rows = lax.all_to_all(copies, "z", 0, 0, tiled=True).reshape(nz * rows, ns)
+    up1, down1 = passed(turned, "z", -1), passed(turned, "z", 1)
+    up2, down2 = passed(turned, "z", -2), passed(turned, "z", 2)
+    up3, down3 = passed(up2, "z", -1), passed(down2, "z", 1)
+    far_up = passed(up2[: rows // 2], "z", -2)
+    far_down = passed(down2[rows // 2 :], "z", 2)
+    c_rows = jnp.zeros((nz, rows, ns), BF16)
+    blocks = ((0, turned), (1, up1), (-1, down1), (2, up2), (-2, down2), (3, up3), (-3, down3))
+    for by, block in blocks:
+        c_rows = lax.dynamic_update_index_in_dim(c_rows, block, (iz + by) % nz, 0)
+    far = jnp.concatenate([far_up, far_down], axis=0)
+    c_rows = lax.dynamic_update_index_in_dim(c_rows, far, (iz + nz // 2) % nz, 0)
+    c_rows = c_rows.reshape(nz * rows, ns)
 
     cross2 = dot_t(c_rows, s_cols)
     cross = (cross2[:, :cols] + cross2[:, cols:] + arrow_term) * jnp.exp2(14 - exps[0])

time: 131 us -> 143 us (1.092)
  starting transfers between devices: 35.2 us -> 48.4 us
  waiting for transfers between devices: 48.4 us -> 40.8 us
  local copies, waits for them, and re-layouts: 11.1 us -> 16.7 us
  matrix products: 6.26 us -> 8.04 us
  Pallas kernels: 4.12 us -> 2.42 us
  other arithmetic: 5.7 us -> 7.34 us
    ppermute x4 -> x8, starting transfers between devices: 14.4 us -> 35.2 us  [passed(): return lax.ppermute(v, axis, [(i, (i + by) % n) for i in range(n)])]
    all_to_all x1 -> x2, waiting for transfers between devices: 11.6 us -> 29.5 us  [spread(): lax.all_to_all(jnp.broadcast_to(v[None], (n,) + v.shape), axis, 0, 0, til...]
    all_to_all x1 -> x0, waiting for transfers between devices: 14.7 us -> none  [shards(): lax.all_to_all(copies, 'z', 0, 0, tiled=True).reshape(nz * rows, ns)]
    ppermute x4 -> x8, waiting for transfers between devices: 14.4 us -> 3.92 us  [passed(): return lax.ppermute(v, axis, [(i, (i + by) % n) for i in range(n)])]
    all_to_all x1 -> x0, starting transfers between devices: 10.3 us -> none  [shards(): lax.all_to_all(copies, 'z', 0, 0, tiled=True).reshape(nz * rows, ns)]
    dynamic_update_slice x3 -> x7, local copies, waits for them, and re-layouts: 1.23 us -> 5.98 us  [shards(): c_rows = lax.dynamic_update_index_in_dim(c_rows, block, (iz + by) % nz, 0)]
    all_to_all x1 -> x2, starting transfers between devices: 4.29 us -> 7.81 us  [spread(): lax.all_to_all(jnp.broadcast_to(v[None], (n,) + v.shape), axis, 0, 0, til...]
    pallas_call x1, Pallas kernels: 2.09 us -> 0.38 us  [shards(): pl.pallas_call(functools.partial(pack_kernel, nx, nz), out_shape=(jax.Sha...]
  transfers between devices with their start and end apart: 8 -> 12, of which waited for: 5 -> 5; matrix products, arithmetic and copies ran while one was open for 7% -> 10% of each run, Pallas kernels for 2% -> 1%
where the time goes in v4:
time: 143 us
  starting transfers between devices  48.4 us (34%)
  waiting for transfers between devices  40.8 us (29%)
  local copies, waits for them, and re-layouts  16.7 us (12%)
  blocking collectives  16.4 us (11%)
  matrix products  8.04 us (6%)
  other arithmetic  7.34 us (5%)
  between operations  2.49 us (2%)
  Pallas kernels  2.42 us (2%)
    ppermute x8, starting transfers between devices, passed(): return lax.ppermute(v, axis, [(i, (i + by) % n) for i in range(n)])  35.2 us
    all_to_all x2, waiting for transfers between devices, spread(): lax.all_to_all(jnp.broadcast_to(v[None], (n,) + v.shape), axis, 0, 0, til...  29.5 us
    all_to_all x1, blocking collectives, shards(): sent = lax.all_to_all(sent.reshape(nz, rows, -1), 'z', 0, 0, tiled=True)  16.4 us
    all_to_all x2, starting transfers between devices, spread(): lax.all_to_all(jnp.broadcast_to(v[None], (n,) + v.shape), axis, 0, 0, til...  7.81 us
    all_to_all x1, waiting for transfers between devices, shards(): diag = lax.all_to_all(diag, 'x', 0, 0, tiled=True)  7.31 us
    dot_general x4, matrix products, dot_t(): lax.dot_general(a, b, (((1,), (1,)), ((), ())), preferred_element_type=F3...  6.55 us
    dynamic_update_slice x7, local copies, waits for them, and re-layouts, shards(): c_rows = lax.dynamic_update_index_in_dim(c_rows, block, (iz + by) % nz, 0)  5.98 us
    ppermute x8, waiting for transfers between devices, passed(): return lax.ppermute(v, axis, [(i, (i + by) % n) for i in range(n)])  3.92 us
  transfers between devices with their start and end apart: 12, of which 5 were waited for; matrix products, arithmetic and copies ran while one was open for 10% of the time, Pallas kernels for 1%

profile of v4, /device:TPU:56, one launch (start us, length us, event | category | flops | bytes accessed | tf_op | source)
XLA Modules:
  0.0 142.5 jit_solution(5337997280140677679)
XLA Ops:
  3.8 10.9 %collective-permute-start = (bf16[64,2048]{1,0:T(8,128)(2,1)S(1)}, bf16[64,2048]{1,0:T(8,128)(2,1)S(1)}, u32[]{:S(2)}, u32[]{:S(2)}) collective-permute-start(bf16[64,2048]{1,0:T(8,128)(2,1)S(1)} %get-tuple-element.8), channel_id=1, source_target_pairs={{0,7},{1,0},{2,1},{3,2},{4,3},{5,4},{6,5},{7,6},{8,15},{9,8},{10,9... | collective-permute-start | bytes 786440 | tf_op jit(solution)/shard_map/ppermute | solution.py:34
  14.8 1.9 %collective-permute-start.1 = (bf16[64,2048]{1,0:T(8,128)(2,1)S(1)}, bf16[64,2048]{1,0:T(8,128)(2,1)S(1)}, u32[]{:S(2)}, u32[]{:S(2)}) collective-permute-start(bf16[64,2048]{1,0:T(8,128)(2,1)S(1)} %get-tuple-element.8), channel_id=1, source_target_pairs={{0,1},{1,2},{2,3},{3,4},{4,5},{5,6},{6,7},{7,0},{8,9},{9,10},{10,1... | collective-permute-start | bytes 786440 | tf_op jit(solution)/shard_map/ppermute | solution.py:34
  16.7 3.9 %collective-permute-start.2 = (bf16[64,2048]{1,0:T(8,128)(2,1)S(1)}, bf16[64,2048]{1,0:T(8,128)(2,1)S(1)}, u32[]{:S(2)}, u32[]{:S(2)}) collective-permute-start(bf16[64,2048]{1,0:T(8,128)(2,1)S(1)} %get-tuple-element.8), channel_id=1, source_target_pairs={{0,6},{1,7},{2,0},{3,1},{4,2},{5,3},{6,4},{7,5},{8,14},{9,15},{10,... | collective-permute-start | bytes 786440 | tf_op jit(solution)/shard_map/ppermute | solution.py:34
  20.6 2.8 %collective-permute-start.3 = (bf16[64,2048]{1,0:T(8,128)(2,1)S(1)}, bf16[64,2048]{1,0:T(8,128)(2,1)S(1)}, u32[]{:S(2)}, u32[]{:S(2)}) collective-permute-start(bf16[64,2048]{1,0:T(8,128)(2,1)S(1)} %get-tuple-element.8), channel_id=1, source_target_pairs={{0,2},{1,3},{2,4},{3,5},{4,6},{5,7},{6,0},{7,1},{8,10},{9,11},{10,... | collective-permute-start | bytes 786440 | tf_op jit(solution)/shard_map/ppermute | solution.py:34
  23.5 1.9 %collective-permute-start.8 = (bf16[2,64,2176]{2,1,0:T(8,128)(2,1)S(1)}, bf16[2,64,2176]{2,1,0:T(8,128)(2,1)S(1)}, u32[]{:S(2)}, u32[]{:S(2)}) collective-permute-start(bf16[2,64,2176]{2,1,0:T(8,128)(2,1)S(1)} %get-tuple-element.9), channel_id=1, source_target_pairs={{32,0},{33,1},{34,2},{35,3},{36,4},{37,5},{38,6},{39,7},{40,8},{41... | collective-permute-start | bytes 1671176 | tf_op jit(solution)/shard_map/ppermute | solution.py:108
  25.5 1.6 %broadcast_in_dim.58 = bf16[8,64,2048]{2,1,0:T(8,128)(2,1)} broadcast(bf16[]{:T(256)} %constant.87.clone.1), dimensions={} | broadcast | bytes 2097154 | tf_op jit(solution)/shard_map/broadcast_in_dim | solution.py:125
  27.8 3.6 %collective-permute-done.2 = bf16[64,2048]{1,0:T(8,128)(2,1)S(1)} collective-permute-done((bf16[64,2048]{1,0:T(8,128)(2,1)S(1)}, bf16[64,2048]{1,0:T(8,128)(2,1)S(1)}, u32[]{:S(2)}, u32[]{:S(2)}) %collective-permute-start.2) | collective-permute-done | bytes 262176 | tf_op jit(solution)/shard_map/ppermute | solution.py:34
  32.1 5.2 %collective-permute-start.6 = (bf16[32,2048]{1,0:T(8,128)(2,1)}, bf16[32,2048]{1,0:T(8,128)(2,1)}, u32[]{:S(2)}, u32[]{:S(2)}) collective-permute-start(bf16[32,2048]{1,0:T(8,128)(2,1)} %slice.85), channel_id=1, source_target_pairs={{0,6},{1,7},{2,0},{3,1},{4,2},{5,3},{6,4},{7,5},{8,14},{9,15},{10,... | collective-permute-start | bytes 393224 | tf_op jit(solution)/shard_map/ppermute | solution.py:34
  38.2 1.9 %collective-permute-start.7 = (bf16[32,2048]{1,0:T(8,128)(2,1)}, bf16[32,2048]{1,0:T(8,128)(2,1)}, u32[]{:S(2)}, u32[]{:S(2)}) collective-permute-start(bf16[32,2048]{1,0:T(8,128)(2,1)} %slice.86), channel_id=1, source_target_pairs={{0,2},{1,3},{2,4},{3,5},{4,6},{5,7},{6,0},{7,1},{8,10},{9,11},{10,... | collective-permute-start | bytes 393224 | tf_op jit(solution)/shard_map/ppermute | solution.py:34
  40.1 6.7 %collective-permute-start.4 = (bf16[64,2048]{1,0:T(8,128)(2,1)S(1)}, bf16[64,2048]{1,0:T(8,128)(2,1)S(1)}, u32[]{:S(2)}, u32[]{:S(2)}) collective-permute-start(bf16[64,2048]{1,0:T(8,128)(2,1)S(1)} %collective-permute-done.2), channel_id=1, source_target_pairs={{0,7},{1,0},{2,1},{3,2},{4,3},{5,4},{6,5},{7,6},{8,15},{9,8},{10,9... | collective-permute-start | bytes 786440 | tf_op jit(solution)/shard_map/ppermute | solution.py:34
  47.5 1.9 %collective-permute-start.5 = (bf16[64,2048]{1,0:T(8,128)(2,1)S(1)}, bf16[64,2048]{1,0:T(8,128)(2,1)}, u32[]{:S(2)}, u32[]{:S(2)}) collective-permute-start(bf16[64,2048]{1,0:T(8,128)(2,1)S(1)} %collective-permute-done.3), channel_id=1, source_target_pairs={{0,1},{1,2},{2,3},{3,4},{4,5},{5,6},{6,7},{7,0},{8,9},{9,10},{10,1... | collective-permute-start | bytes 786440 | tf_op jit(solution)/shard_map/ppermute | solution.py:34
  50.2 1.6 %broadcast_in_dim.67 = bf16[4,2,64,2176]{3,2,1,0:T(8,128)(2,1)} broadcast(bf16[2,64,2176]{2,1,0:T(8,128)(2,1)S(1)} %collective-permute-done.8), dimensions={1,2,3} | broadcast | bytes 2785280 | tf_op jit(solution)/shard_map/broadcast_in_dim | solution.py:29
  51.8 4.3 %all-to-all-start = ((bf16[4,2,64,2176]{3,2,1,0:T(8,128)(2,1)}), bf16[4,2,64,2176]{3,2,1,0:T(8,128)(2,1)S(1)}, u32[]{:S(2)}, u32[]{:S(2)}) async-start(bf16[4,2,64,2176]{3,2,1,0:T(8,128)(2,1)} %broadcast_in_dim.67), calls=%async_computation | async-start | bytes 4456448 | tf_op jit(solution)/shard_map/all_to_all | solution.py:29
  58.3 1.7 %bitcast_dynamic-update-slice_fusion = bf16[8,64,2048]{2,1,0:T(8,128)(2,1)} fusion(bf16[8,64,2048]{2,1,0:T(8,128)(2,1)} %bitcast_dynamic-update-slice_fusion.1, s32[]{:T(128)S(6)} %select_n.87, bf16[64,2048]{1,0:T(8,128)(2,1)} %collective-permute-done.5), kind=kLoop, calls=%fused_computation.25 | loop fusion | bytes 524292 | tf_op jit(solution)/shard_map/jit(dynamic_update_index_in_dim)/dynamic_update_slice | solution.py:128
  59.9 1.7 %fusion.11 = bf16[8,64,2048]{2,1,0:T(8,128)(2,1)} fusion(bf16[8,64,2048]{2,1,0:T(8,128)(2,1)} %bitcast_dynamic-update-slice_fusion, s32[]{:T(128)S(6)} %select_n.89, bf16[32,2048]{1,0:T(8,128)(2,1)} %collective-permute-done.7, bf16[32,2048]{1,0:T(8,128)(2,1)} %collective-permute-done.6), kind=kLoop, calls=%fused_computation.24 | loop fusion | flops 524288 | bytes 524292 | tf_op jit(solution)/shard_map/jit(dynamic_update_index_in_dim)/dynamic_update_slice | solution.py:130
  61.6 21.4 %all-to-all-done = bf16[4,2,64,2176]{3,2,1,0:T(8,128)(2,1)S(1)} async-done(((bf16[4,2,64,2176]{3,2,1,0:T(8,128)(2,1)}), bf16[4,2,64,2176]{3,2,1,0:T(8,128)(2,1)S(1)}, u32[]{:S(2)}, u32[]{:S(2)}) %all-to-all-start) | async-done | bytes 2228256 | tf_op jit(solution)/shard_map/all_to_all | solution.py:29
  87.5 2.9 %fusion.32 = f32[512,512]{1,0:T(8,128)S(1)} fusion(bf16[512,2048]{1,0:T(8,128)(2,1)} %bitcast.12, bf16[512,2048]{1,0:T(8,128)(2,1)S(1)} %bitcast.72), kind=kOutput, calls=%fused_computation.60 | convolution fusion | flops 1073741824 | bytes 5242880 | tf_op jit(solution)/shard_map/dot_general | solution.py:19
  92.1 16.4 %all_to_all.20 = f16[8,64,384]{2,1,0:T(8,128)(2,1)S(1)} all-to-all(f16[8,64,384]{2,1,0:T(8,128)(2,1)S(1)} %bitcast.74), channel_id=1, replica_groups=mesh['y'=8,'c'=2,'x'=4,'z'=8] {'z'}, dimensions={0} | all-to-all | bytes 786432 | tf_op jit(solution)/shard_map/all_to_all | solution.py:141
  109.7 3.5 %all-to-all-start.2 = ((f16[4,8,64,256]{3,1,2,0:T(8,128)(2,1)}), f16[4,8,64,256]{3,1,2,0:T(8,128)(2,1)S(1)}, u32[]{:S(2)}, u32[]{:S(2)}) async-start(f16[4,8,64,256]{3,1,2,0:T(8,128)(2,1)} %broadcast_in_dim.70), calls=%async_computation.2 | async-start | bytes 2097152 | tf_op jit(solution)/shard_map/all_to_all | solution.py:29
  114.4 2.0 %shard_map.86 = f32[64,2048]{1,0:T(8,128)} custom-call(f32[8,64,256]{2,1,0:T(8,128)} %convert_multiply_fusion.1.in_ref), custom_call_target="tpu_custom_call" | custom-call | tf_op jit(solution)/shard_map/pallas_call | solution.py:152
  116.6 8.1 %all-to-all-done.2 = f16[4,8,64,256]{3,1,2,0:T(8,128)(2,1)S(1)} async-done(((f16[4,8,64,256]{3,1,2,0:T(8,128)(2,1)}), f16[4,8,64,256]{3,1,2,0:T(8,128)(2,1)S(1)}, u32[]{:S(2)}, u32[]{:S(2)}) %all-to-all-start.2) | async-done | bytes 1048608 | tf_op jit(solution)/shard_map/all_to_all | solution.py:29
  126.3 2.9 %fusion.1 = f32[512,512]{1,0:T(8,128)S(1)} fusion(bf16[512,2048]{1,0:T(8,128)(2,1)} %bitcast.12, bf16[256,2048]{1,0:T(8,128)(2,1)S(1)} %get-tuple-element.18, bf16[256,2048]{1,0:T(8,128)(2,1)S(1)} %get-tuple-element.17), kind=kOutput, calls=%fused_computation.5 | convolution fusion | flops 1077936128 | bytes 5242880 | tf_op jit(solution)/shard_map/dot_general | solution.py:19
  130.1 3.5 %all-to-all-start.3 = ((f32[4,64,512]{2,1,0:T(8,128)}), f32[4,64,512]{2,1,0:T(8,128)S(1)}, u32[]{:S(2)}, u32[]{:S(2)}) async-start(f32[4,64,512]{2,1,0:T(8,128)} %bitcast.25), calls=%async_computation.3 | async-start | bytes 1048576 | tf_op jit(solution)/shard_map/all_to_all | solution.py:150
  134.3 7.3 %all-to-all-done.3 = f32[4,64,512]{2,1,0:T(8,128)S(1)} async-done(((f32[4,64,512]{2,1,0:T(8,128)}), f32[4,64,512]{2,1,0:T(8,128)S(1)}, u32[]{:S(2)}, u32[]{:S(2)}) %all-to-all-start.3) | async-done | bytes 524320 | tf_op jit(solution)/shard_map/all_to_all | solution.py:150
  (60 shorter events, 20.5 us)
Async XLA Ops:
  0.6 86.3 %copy-start = (f32[1,2048,64]{1,2,0:T(8,128)S(1)}, f32[1,2048,64]{1,2,0:T(8,128)}, u32[]{:S(2)}) copy-start(f32[1,2048,64]{1,2,0:T(8,128)} %param.7) | copy-start | bytes 1572868
  0.6 1.1 copy-start.1
  1.7 0.9 copy-start.2
  2.7 0.8 copy-start.3
  3.8 36.3 %collective-permute-start = (bf16[64,2048]{1,0:T(8,128)(2,1)S(1)}, bf16[64,2048]{1,0:T(8,128)(2,1)S(1)}, u32[]{:S(2)}, u32[]{:S(2)}) collective-permute-start(bf16[64,2048]{1,0:T(8,128)(2,1)S(1)} %get-tuple-element.8), channel_id=1, source_target_pairs={{0,7},{1,0},{2,1},{3,2},{4,3},{5,4},{6,5},{7,6},{8,15},{9,8},{10,9... | collective-permute-start | bytes 786440 | tf_op jit(solution)/shard_map/ppermute | solution.py:34
  14.8 32.7 %collective-permute-start.1 = (bf16[64,2048]{1,0:T(8,128)(2,1)S(1)}, bf16[64,2048]{1,0:T(8,128)(2,1)S(1)}, u32[]{:S(2)}, u32[]{:S(2)}) collective-permute-start(bf16[64,2048]{1,0:T(8,128)(2,1)S(1)} %get-tuple-element.8), channel_id=1, source_target_pairs={{0,1},{1,2},{2,3},{3,4},{4,5},{5,6},{6,7},{7,0},{8,9},{9,10},{10,1... | collective-permute-start | bytes 786440 | tf_op jit(solution)/shard_map/ppermute | solution.py:34
  16.7 14.7 %collective-permute-start.2 = (bf16[64,2048]{1,0:T(8,128)(2,1)S(1)}, bf16[64,2048]{1,0:T(8,128)(2,1)S(1)}, u32[]{:S(2)}, u32[]{:S(2)}) collective-permute-start(bf16[64,2048]{1,0:T(8,128)(2,1)S(1)} %get-tuple-element.8), channel_id=1, source_target_pairs={{0,6},{1,7},{2,0},{3,1},{4,2},{5,3},{6,4},{7,5},{8,14},{9,15},{10,... | collective-permute-start | bytes 786440 | tf_op jit(solution)/shard_map/ppermute | solution.py:34
  20.6 16.9 %collective-permute-start.3 = (bf16[64,2048]{1,0:T(8,128)(2,1)S(1)}, bf16[64,2048]{1,0:T(8,128)(2,1)S(1)}, u32[]{:S(2)}, u32[]{:S(2)}) collective-permute-start(bf16[64,2048]{1,0:T(8,128)(2,1)S(1)} %get-tuple-element.8), channel_id=1, source_target_pairs={{0,2},{1,3},{2,4},{3,5},{4,6},{5,7},{6,0},{7,1},{8,10},{9,11},{10,... | collective-permute-start | bytes 786440 | tf_op jit(solution)/shard_map/ppermute | solution.py:34
  23.5 26.7 %collective-permute-start.8 = (bf16[2,64,2176]{2,1,0:T(8,128)(2,1)S(1)}, bf16[2,64,2176]{2,1,0:T(8,128)(2,1)S(1)}, u32[]{:S(2)}, u32[]{:S(2)}) collective-permute-start(bf16[2,64,2176]{2,1,0:T(8,128)(2,1)S(1)} %get-tuple-element.9), channel_id=1, source_target_pairs={{32,0},{33,1},{34,2},{35,3},{36,4},{37,5},{38,6},{39,7},{40,8},{41... | collective-permute-start | bytes 1671176 | tf_op jit(solution)/shard_map/ppermute | solution.py:108
  32.1 27.9 %collective-permute-start.6 = (bf16[32,2048]{1,0:T(8,128)(2,1)}, bf16[32,2048]{1,0:T(8,128)(2,1)}, u32[]{:S(2)}, u32[]{:S(2)}) collective-permute-start(bf16[32,2048]{1,0:T(8,128)(2,1)} %slice.85), channel_id=1, source_target_pairs={{0,6},{1,7},{2,0},{3,1},{4,2},{5,3},{6,4},{7,5},{8,14},{9,15},{10,... | collective-permute-start | bytes 393224 | tf_op jit(solution)/shard_map/ppermute | solution.py:34
  38.2 21.7 %collective-permute-start.7 = (bf16[32,2048]{1,0:T(8,128)(2,1)}, bf16[32,2048]{1,0:T(8,128)(2,1)}, u32[]{:S(2)}, u32[]{:S(2)}) collective-permute-start(bf16[32,2048]{1,0:T(8,128)(2,1)} %slice.86), channel_id=1, source_target_pairs={{0,2},{1,3},{2,4},{3,5},{4,6},{5,7},{6,0},{7,1},{8,10},{9,11},{10,... | collective-permute-start | bytes 393224 | tf_op jit(solution)/shard_map/ppermute | solution.py:34
  40.1 17.4 %collective-permute-start.4 = (bf16[64,2048]{1,0:T(8,128)(2,1)S(1)}, bf16[64,2048]{1,0:T(8,128)(2,1)S(1)}, u32[]{:S(2)}, u32[]{:S(2)}) collective-permute-start(bf16[64,2048]{1,0:T(8,128)(2,1)S(1)} %collective-permute-done.2), channel_id=1, source_target_pairs={{0,7},{1,0},{2,1},{3,2},{4,3},{5,4},{6,5},{7,6},{8,15},{9,8},{10,9... | collective-permute-start | bytes 786440 | tf_op jit(solution)/shard_map/ppermute | solution.py:34
  47.5 10.7 %collective-permute-start.5 = (bf16[64,2048]{1,0:T(8,128)(2,1)S(1)}, bf16[64,2048]{1,0:T(8,128)(2,1)}, u32[]{:S(2)}, u32[]{:S(2)}) collective-permute-start(bf16[64,2048]{1,0:T(8,128)(2,1)S(1)} %collective-permute-done.3), channel_id=1, source_target_pairs={{0,1},{1,2},{2,3},{3,4},{4,5},{5,6},{6,7},{7,0},{8,9},{9,10},{10,1... | collective-permute-start | bytes 786440 | tf_op jit(solution)/shard_map/ppermute | solution.py:34
  51.8 31.2 %all-to-all-start = ((bf16[4,2,64,2176]{3,2,1,0:T(8,128)(2,1)}), bf16[4,2,64,2176]{3,2,1,0:T(8,128)(2,1)S(1)}, u32[]{:S(2)}, u32[]{:S(2)}) async-start(bf16[4,2,64,2176]{3,2,1,0:T(8,128)(2,1)} %broadcast_in_dim.67), calls=%async_computation | async-start | bytes 4456448 | tf_op jit(solution)/shard_map/all_to_all | solution.py:29
  109.7 15.0 %all-to-all-start.2 = ((f16[4,8,64,256]{3,1,2,0:T(8,128)(2,1)}), f16[4,8,64,256]{3,1,2,0:T(8,128)(2,1)S(1)}, u32[]{:S(2)}, u32[]{:S(2)}) async-start(f16[4,8,64,256]{3,1,2,0:T(8,128)(2,1)} %broadcast_in_dim.70), calls=%async_computation.2 | async-start | bytes 2097152 | tf_op jit(solution)/shard_map/all_to_all | solution.py:29
  129.2 4.4 %copy-start.6 = (f32[64,64]{1,0:T(8,128)S(1)}, f32[64,64]{1,0:T(8,128)}, u32[]{:S(2)}) copy-start(f32[64,64]{1,0:T(8,128)} %param.11) | copy-start | bytes 49156
  129.2 4.7 %copy-start.4 = (f32[1,64,2048]{2,1,0:T(8,128)S(1)}, f32[1,64,2048]{2,1,0:T(8,128)}, u32[]{:S(2)}) copy-start(f32[1,64,2048]{2,1,0:T(8,128)} %param.8) | copy-start | bytes 1572868
  130.1 11.5 %all-to-all-start.3 = ((f32[4,64,512]{2,1,0:T(8,128)}), f32[4,64,512]{2,1,0:T(8,128)S(1)}, u32[]{:S(2)}, u32[]{:S(2)}) async-start(f32[4,64,512]{2,1,0:T(8,128)} %bitcast.25), calls=%async_computation.3 | async-start | bytes 1048576 | tf_op jit(solution)/shard_map/all_to_all | solution.py:150
  133.9 8.6 %copy-start.5 = (f32[64,64]{1,0:T(8,128)}, f32[64,64]{1,0:T(8,128)S(1)}, u32[]{:S(2)}) copy-start(f32[64,64]{1,0:T(8,128)S(1)} %convolution_add_fusion.1) | copy-start | bytes 49156

commit v5 on v3

--- a/solution.py
+++ b/solution.py
@@ -29,11 +29,6 @@
     return lax.all_to_all(jnp.broadcast_to(v[None], (n,) + v.shape), axis, 0, 0, tiled=True)
 
 
-def passed(v, axis, by):
-    n = lax.axis_size(axis)
-    return lax.ppermute(v, axis, [(i, (i + by) % n) for i in range(n)])
-
-
 def halves(first, second):
     lane = lax.broadcasted_iota(jnp.int32, first.shape, 1)
     low = jnp.where(lane < 64, first, pltpu.roll(second, 64, 1))
@@ -41,10 +36,9 @@
     return low, high
 
 
-def pack_kernel(nx, nz, c_ref, s_ref, a_ref, copies_ref, packed_ref):
+def pack_kernel(cols, s_ref, a_ref, packed_ref):
     rows, ns = s_ref.shape
     nf = a_ref.shape[1]
-    run = 2 * rows
 
     def put(at, value):
         top = value.astype(BF16)
@@ -52,27 +46,36 @@
         low = (value - top.astype(F32)).astype(BF16)
         packed_ref[1, :, at : at + value.shape[1]] = low
 
-    total = jnp.zeros((rows, run), F32)
-    for q in range(nx // 2):
-        for k in range(nz // 2):
-            first = slice((2 * q * nz // 2 + k) * run, (2 * q * nz // 2 + k + 1) * run)
-            second = slice(first.start + nz // 2 * run, first.stop + nz // 2 * run)
-            pair = s_ref[:, first], s_ref[:, second]
-            total = total + jnp.abs(pair[0]) + jnp.abs(pair[1])
-            for h, value in enumerate(halves(*pair)):
-                put(((2 * k + h) * nx // 2 + q) * run, value)
-            pair = c_ref[:, first].astype(F32), c_ref[:, second].astype(F32)
-            for h, value in enumerate(halves(*pair)):
-                at = ((2 * k + h) * nx // 2 + q) * run
-                value = value.astype(BF16)
-                for z in range(nz):
-                    copies_ref[z, :, at : at + run] = value
+    total = jnp.zeros((rows, 128), F32)
+    for at in range(0, ns, 128):
+        value = s_ref[:, at : at + 128]
+        total = total + jnp.abs(value)
+        put(at, value)
     a_own = a_ref[...]
     bound_a = jnp.max(jnp.abs(a_own), axis=1, keepdims=True)
     bound = 0.125 * jnp.sum(total, axis=1, keepdims=True) + 0.75 * nf * bound_a
     lane = lax.broadcasted_iota(jnp.int32, (rows, nf), 1)
-    exps = jnp.where(lane == 0, exponent(bound), exponent(0.125 * nx * rows * bound_a)) + 2
+    exps = jnp.where(lane == 0, exponent(bound), exponent(0.125 * cols * bound_a)) + 2
     put(ns, jnp.concatenate([a_own, exps], axis=1))
+
+
+def turn_kernel(nx, nz, in_ref, out_ref):
+    run = 128
+
+    @pl.loop(0, in_ref.shape[0] // 64)
+    def _(step):
+        at_rows = pl.ds(pl.multiple_of(step * 64, 64), 64)
+        for q in range(nx // 2):
+            for k in range(nz // 2):
+                first = (q * nz + k) * run
+                second = first + nz // 2 * run
+                pair = halves(
+                    in_ref[at_rows, first : first + run].astype(F32),
+                    in_ref[at_rows, second : second + run].astype(F32),
+                )
+                for h, value in enumerate(pair):
+                    at = ((2 * k + h) * nx // 2 + q) * run
+                    out_ref[at_rows, at : at + run] = value.astype(BF16)
 
 
 def natural_kernel(nx, nz, in_ref, out_ref):
@@ -98,23 +101,13 @@
     cols = nx * rows
     ix, iz = lax.axis_index("x"), lax.axis_index("z")
 
-    copies, packed = pl.pallas_call(
-        functools.partial(pack_kernel, nx, nz),
-        out_shape=(
-            jax.ShapeDtypeStruct((nz, rows, ns), BF16),
-            jax.ShapeDtypeStruct((2, rows, ns + 2 * nf), BF16),
-        ),
-        compiler_params=pltpu.CompilerParams(vmem_limit_bytes=32 << 20),
-    )(c_own, s_own, a_own)
+    packed = pl.pallas_call(
+        functools.partial(pack_kernel, cols),
+        out_shape=jax.ShapeDtypeStruct((2, rows, ns + 2 * nf), BF16),
+    )(s_own, a_own)
     route = [(t * group + b, (t - 1) * group + b) for t in range(1, steps) for b in range(group)]
     packed = lax.ppermute(packed, ("y", "c", "x", "z"), route)
-    before, after = passed(packed, "x", 1), passed(packed, "x", -1)
-    far_top, far_low = passed(packed[0], "x", 2), passed(packed[1], "x", -2)
-    succ = jnp.zeros((nx,) + packed.shape, BF16)
-    for by, block in ((0, packed), (nx - 1, before), (1, after)):
-        succ = lax.dynamic_update_index_in_dim(succ, block, (ix + by) % nx, 0)
-    far = jnp.stack([far_top, far_low])
-    succ = lax.dynamic_update_index_in_dim(succ, far, (ix + 2) % nx, 0)
+    succ = spread(packed, "x")
     succ = succ.transpose(1, 0, 2, 3)
     s_cols = succ[..., :ns].reshape(2 * cols, ns)
     a_two = succ[..., ns : ns + nf].reshape(2, cols, nf)
@@ -122,15 +115,22 @@
 
     link_rows = lax.dynamic_slice_in_dim(link, ix * nz * rows, nz * rows, 0)
     arrow_term = dot_t(link_rows, a_two[0].astype(F32) + a_two[1].astype(F32), precision=HIGH)
-    place = jnp.concatenate([a_two[0], a_two[1]], axis=1)
+    place = jnp.concatenate([a_two[0], a_two[1]], axis=1).reshape(nx, 1, rows, 2 * nf)
+    here = lax.broadcasted_iota(jnp.int32, (1, nz, 1, 1), 1) == iz
+    place = jnp.where(here, place, jnp.zeros((), BF16)).reshape(ns, 2 * nf)
     s_cols, arrow_term, place = lax.optimization_barrier((s_cols, arrow_term, place))
 
-    c_rows = lax.all_to_all(copies, "z", 0, 0, tiled=True).reshape(nz * rows, ns)
+    c_rows = lax.all_gather(c_own, "z", axis=0, tiled=True)
+    c_turned = pl.pallas_call(
+        functools.partial(turn_kernel, nx, nz),
+        out_shape=jax.ShapeDtypeStruct(c_rows.shape, BF16),
+        cost_estimate=pl.CostEstimate(flops=0, bytes_accessed=20 << 20, transcendentals=0),
+        compiler_params=pltpu.CompilerParams(vmem_limit_bytes=16 << 20),
+    )(c_rows)
 
     cross2 = dot_t(c_rows, s_cols)
     cross = (cross2[:, :cols] + cross2[:, cols:] + arrow_term) * jnp.exp2(14 - exps[0])
-    c_here = lax.dynamic_slice_in_dim(c_rows, iz * cols, cols, 1)
-    share2 = jnp.dot(c_here, place, preferred_element_type=F32)
+    share2 = jnp.dot(c_rows, place, preferred_element_type=F32)
     share = (share2[:, :nf] + share2[:, nf:]) * jnp.exp2(14 - exps[1])
     lane = lax.broadcasted_iota(jnp.int32, (nz * rows, nf), 1)
     marks = jnp.where(lane == 0, exps[0], exps[1])
@@ -142,7 +142,7 @@
 
     every = spread(cross, "x").astype(F32) * scale[None]
     every = every.transpose(0, 2, 1, 3).reshape(cols, ns)
-    diag2 = dot_t(jnp.concatenate(two_parts(every), axis=0), c_rows)
+    diag2 = dot_t(jnp.concatenate(two_parts(every), axis=0), c_turned)
     diag = (diag2[:cols] + diag2[cols:]).reshape(nx, rows, nz * rows)
     diag = lax.all_to_all(diag, "x", 0, 0, tiled=True)
 

time: 131 us -> 142 us (1.084)
  the two profiles are of different devices: /device:TPU:56 before, /device:TPU:16 now
where the time goes in v5:
time: 142 us
  waiting for transfers between devices  54.5 us (38%)
  blocking collectives  25.5 us (18%)
  between operations  15.7 us (11%)
  starting transfers between devices  14.1 us (10%)
  local copies, waits for them, and re-layouts  10.7 us (8%)
  other arithmetic  7.97 us (6%)
  matrix products  7.78 us (5%)
  Pallas kernels  5.28 us (4%)
    all_to_all x2, waiting for transfers between devices, spread(): lax.all_to_all(jnp.broadcast_to(v[None], (n,) + v.shape), axis, 0, 0, til...  38.1 us
    all_to_all x1, blocking collectives, shards(): sent = lax.all_to_all(sent.reshape(nz, rows, -1), 'z', 0, 0, tiled=True)  25.5 us
    all_to_all x2, starting transfers between devices, spread(): lax.all_to_all(jnp.broadcast_to(v[None], (n,) + v.shape), axis, 0, 0, til...  8.7 us
    all_to_all x1, waiting for transfers between devices, shards(): diag = lax.all_to_all(diag, 'x', 0, 0, tiled=True)  8.35 us
    ppermute x1, waiting for transfers between devices, shards(): packed = lax.ppermute(packed, ('y', 'c', 'x', 'z'), route)  7.34 us
    dot_general x4, matrix products, dot_t(): lax.dot_general(a, b, (((1,), (1,)), ((), ())), preferred_element_type=F3...  4.94 us
    all_to_all x1, starting transfers between devices, shards(): diag = lax.all_to_all(diag, 'x', 0, 0, tiled=True)  3.47 us
    unnamed x15, local copies, waits for them, and re-layouts  3.43 us
  transfers between devices with their start and end apart: 5, of which 4 were waited for; matrix products, arithmetic and copies ran while one was open for 8% of the time, Pallas kernels for 4%

profile of v5, /device:TPU:16, one launch (start us, length us, event | category | flops | bytes accessed | tf_op | source)
XLA Modules:
  0.0 141.5 jit_solution(2854867739426861313)
XLA Ops:
  7.9 2.1 %shard_map.85 = bf16[2,64,2176]{2,1,0:T(8,128)(2,1)} custom-call(f32[64,2048]{1,0:T(8,128)} %bitcast.67, f32[64,64]{1,0:T(8,128)} %bitcast.71), custom_call_target="tpu_custom_call" | custom-call | tf_op jit(solution)/shard_map/pallas_call | solution.py:104
  10.0 1.9 %collective-permute-start = (bf16[2,64,2176]{2,1,0:T(8,128)(2,1)}, bf16[2,64,2176]{2,1,0:T(8,128)(2,1)S(1)}, u32[]{:S(2)}, u32[]{:S(2)}) collective-permute-start(bf16[2,64,2176]{2,1,0:T(8,128)(2,1)} %shard_map.85), channel_id=1, source_target_pairs={{32,0},{33,1},{34,2},{35,3},{36,4},{37,5},{38,6},{39,7},{40,8},{41... | collective-permute-start | bytes 1671176 | tf_op jit(solution)/shard_map/ppermute | solution.py:109
  11.9 7.3 %collective-permute-done = bf16[2,64,2176]{2,1,0:T(8,128)(2,1)S(1)} collective-permute-done((bf16[2,64,2176]{2,1,0:T(8,128)(2,1)}, bf16[2,64,2176]{2,1,0:T(8,128)(2,1)S(1)}, u32[]{:S(2)}, u32[]{:S(2)}) %collective-permute-start) | collective-permute-done | bytes 557088 | tf_op jit(solution)/shard_map/ppermute | solution.py:109
  19.3 1.6 %broadcast_in_dim.58 = bf16[4,2,64,2176]{3,2,1,0:T(8,128)(2,1)} broadcast(bf16[2,64,2176]{2,1,0:T(8,128)(2,1)S(1)} %collective-permute-done), dimensions={1,2,3} | broadcast | bytes 2785280 | tf_op jit(solution)/shard_map/broadcast_in_dim | solution.py:29
  20.9 4.5 %all-to-all-start = ((bf16[4,2,64,2176]{3,2,1,0:T(8,128)(2,1)}), bf16[4,2,64,2176]{3,2,1,0:T(8,128)(2,1)}, u32[]{:S(2)}, u32[]{:S(2)}) async-start(bf16[4,2,64,2176]{3,2,1,0:T(8,128)(2,1)} %broadcast_in_dim.58), calls=%async_computation | async-start | bytes 4456448 | tf_op jit(solution)/shard_map/all_to_all | solution.py:29
  25.6 28.3 %all-to-all-done = bf16[4,2,64,2176]{3,2,1,0:T(8,128)(2,1)} async-done(((bf16[4,2,64,2176]{3,2,1,0:T(8,128)(2,1)}), bf16[4,2,64,2176]{3,2,1,0:T(8,128)(2,1)}, u32[]{:S(2)}, u32[]{:S(2)}) %all-to-all-start) | async-done | bytes 2228256 | tf_op jit(solution)/shard_map/all_to_all | solution.py:29
  53.8 1.8 %copy.28 = bf16[4,2,64,2176]{3,2,0,1:T(8,128)(2,1)S(1)} copy(bf16[4,2,64,2176]{3,2,1,0:T(8,128)(2,1)} %all-to-all-done) | data formatting | bytes 4456448 | tf_op jit(solution)/shard_map/all_to_all | solution.py:29
  55.7 1.6 %slice.77 = bf16[2,4,64,2048]{3,2,1,0:T(8,128)(2,1)} slice(bf16[2,4,64,2176]{3,2,1,0:T(8,128)(2,1)S(1)} %bitcast.57), slice={[0:2], [0:4], [0:64], [0:2048]} | slice | bytes 4194304 | tf_op jit(solution)/shard_map/slice | solution.py:112
  59.5 1.1 bitcast_select_fusion
  61.1 1.3 fusion.22
  62.5 2.5 %convolution_bitcast_fusion.1 = f32[512,128]{1,0:T(8,128)S(1)} fusion(bf16[2048,128]{1,0:T(8,128)(2,1)} %bitcast_select_fusion, bf16[1,512,2048]{2,1,0:T(8,128)(2,1)} %all-gather.3.cloned.1.call-done), kind=kOutput, calls=%fused_computation.11 | convolution fusion | flops 268435456 | bytes 2883584 | tf_op jit(solution)/shard_map/dot_general | solution.py:133
  65.2 2.9 %convolution_bitcast_fusion = f32[512,512]{1,0:T(8,128)S(1)} fusion(bf16[512,2048]{1,0:T(8,128)(2,1)} %bitcast.64, bf16[1,512,2048]{2,1,0:T(8,128)(2,1)S(1)} %copy-done.1), kind=kOutput, calls=%fused_computation.10 | convolution fusion | flops 1073741824 | bytes 5242880 | tf_op jit(solution)/shard_map/dot_general | solution.py:19
  68.3 25.5 %all_to_all.20 = f16[8,64,384]{2,1,0:T(8,128)(2,1)S(1)} all-to-all(f16[8,64,384]{2,1,0:T(8,128)(2,1)S(1)} %bitcast.66), channel_id=1, replica_groups=mesh['y'=8,'c'=2,'x'=4,'z'=8] {'z'}, dimensions={0} | all-to-all | bytes 786432 | tf_op jit(solution)/shard_map/all_to_all | solution.py:138
  94.1 1.1 broadcast_in_dim.68
  95.2 4.2 %all-to-all-start.2 = ((f16[4,8,64,256]{3,1,2,0:T(8,128)(2,1)}), f16[4,8,64,256]{3,1,2,0:T(8,128)(2,1)}, u32[]{:S(2)}, u32[]{:S(2)}) async-start(f16[4,8,64,256]{3,1,2,0:T(8,128)(2,1)} %broadcast_in_dim.68), calls=%async_computation.2 | async-start | bytes 2097152 | tf_op jit(solution)/shard_map/all_to_all | solution.py:29
  99.4 1.1 shard_map.86
  100.6 1.3 copy-done.2
  103.1 2.0 %shard_map.87 = f32[64,2048]{1,0:T(8,128)} custom-call(f32[8,64,256]{2,1,0:T(8,128)} %convert_multiply_fusion.1.in_ref), custom_call_target="tpu_custom_call" | custom-call | tf_op jit(solution)/shard_map/pallas_call | solution.py:149
  105.2 9.8 %all-to-all-done.2 = f16[4,8,64,256]{3,1,2,0:T(8,128)(2,1)} async-done(((f16[4,8,64,256]{3,1,2,0:T(8,128)(2,1)}), f16[4,8,64,256]{3,1,2,0:T(8,128)(2,1)}, u32[]{:S(2)}, u32[]{:S(2)}) %all-to-all-start.2) | async-done | bytes 1048608 | tf_op jit(solution)/shard_map/all_to_all | solution.py:29
  115.0 1.5 %convert_multiply_fusion = f32[4,8,64,256]{3,1,2,0:T(8,128)S(1)} fusion(f16[4,8,64,256]{3,1,2,0:T(8,128)(2,1)} %all-to-all-done.2, f32[8]{0:T(128)S(1)} %get-tuple-element.9), kind=kLoop, calls=%fused_computation.9 | loop fusion | flops 1048576 | bytes 3145760 | tf_op jit(solution)/shard_map/mul | solution.py:143
  117.8 1.2 copy-done.3
  119.0 1.3 fusion.1
  121.2 3.5 %all-to-all-start.3 = ((f32[4,64,512]{2,1,0:T(8,128)}), f32[4,64,512]{2,1,0:T(8,128)S(1)}, u32[]{:S(2)}, u32[]{:S(2)}) async-start(f32[4,64,512]{2,1,0:T(8,128)} %bitcast.20), calls=%async_computation.3 | async-start | bytes 1048576 | tf_op jit(solution)/shard_map/all_to_all | solution.py:147
  125.4 8.4 %all-to-all-done.3 = f32[4,64,512]{2,1,0:T(8,128)S(1)} async-done(((f32[4,64,512]{2,1,0:T(8,128)}), f32[4,64,512]{2,1,0:T(8,128)S(1)}, u32[]{:S(2)}, u32[]{:S(2)}) %all-to-all-start.3) | async-done | bytes 524320 | tf_op jit(solution)/shard_map/all_to_all | solution.py:147
  (41 shorter events, 7.9 us)
Async XLA Ops:
  7.2 53.5 %copy-start = (f32[1,2048,64]{1,2,0:T(8,128)S(1)}, f32[1,2048,64]{1,2,0:T(8,128)}, u32[]{:S(2)}) copy-start(f32[1,2048,64]{1,2,0:T(8,128)} %param.7) | copy-start | bytes 1572868
  7.2 55.3 %all-gather.3.cloned.1.call-start = ((), (), s32[]{:S(2)}) async-start(), calls=%async_computation.4 | async-start | bytes 2359296 | tf_op jit(solution)/shard_map/all_gather | solution.py:123
  10.0 9.3 %collective-permute-start = (bf16[2,64,2176]{2,1,0:T(8,128)(2,1)}, bf16[2,64,2176]{2,1,0:T(8,128)(2,1)S(1)}, u32[]{:S(2)}, u32[]{:S(2)}) collective-permute-start(bf16[2,64,2176]{2,1,0:T(8,128)(2,1)} %shard_map.85), channel_id=1, source_target_pairs={{32,0},{33,1},{34,2},{35,3},{36,4},{37,5},{38,6},{39,7},{40,8},{41... | collective-permute-start | bytes 1671176 | tf_op jit(solution)/shard_map/ppermute | solution.py:109
  20.9 32.9 %all-to-all-start = ((bf16[4,2,64,2176]{3,2,1,0:T(8,128)(2,1)}), bf16[4,2,64,2176]{3,2,1,0:T(8,128)(2,1)}, u32[]{:S(2)}, u32[]{:S(2)}) async-start(bf16[4,2,64,2176]{3,2,1,0:T(8,128)(2,1)} %broadcast_in_dim.58), calls=%async_computation | async-start | bytes 4456448 | tf_op jit(solution)/shard_map/all_to_all | solution.py:29
  62.5 2.7 %copy-start.1 = (bf16[1,512,2048]{2,1,0:T(8,128)(2,1)S(1)}, bf16[1,512,2048]{2,1,0:T(8,128)(2,1)}, u32[]{:S(2)}) copy-start(bf16[1,512,2048]{2,1,0:T(8,128)(2,1)} %all-gather.3.cloned.1.call-done) | copy-start | bytes 6291460
  95.2 19.9 %all-to-all-start.2 = ((f16[4,8,64,256]{3,1,2,0:T(8,128)(2,1)}), f16[4,8,64,256]{3,1,2,0:T(8,128)(2,1)}, u32[]{:S(2)}, u32[]{:S(2)}) async-start(f16[4,8,64,256]{3,1,2,0:T(8,128)(2,1)} %broadcast_in_dim.68), calls=%async_computation.2 | async-start | bytes 2097152 | tf_op jit(solution)/shard_map/all_to_all | solution.py:29
  100.6 1.3 copy-start.2
  117.4 1.6 %copy-start.3 = (bf16[512,2048]{1,0:T(8,128)(2,1)S(1)}, bf16[512,2048]{1,0:T(8,128)(2,1)}, u32[]{:S(2)}) copy-start(bf16[512,2048]{1,0:T(8,128)(2,1)} %copy-done.2) | copy-start | bytes 6291460
  120.3 4.4 %copy-start.6 = (f32[64,64]{1,0:T(8,128)S(1)}, f32[64,64]{1,0:T(8,128)}, u32[]{:S(2)}) copy-start(f32[64,64]{1,0:T(8,128)} %param.11) | copy-start | bytes 49156
  120.3 4.7 %copy-start.4 = (f32[1,64,2048]{2,1,0:T(8,128)S(1)}, f32[1,64,2048]{2,1,0:T(8,128)}, u32[]{:S(2)}) copy-start(f32[1,64,2048]{2,1,0:T(8,128)} %param.8) | copy-start | bytes 1572868
  121.2 12.6 %all-to-all-start.3 = ((f32[4,64,512]{2,1,0:T(8,128)}), f32[4,64,512]{2,1,0:T(8,128)S(1)}, u32[]{:S(2)}, u32[]{:S(2)}) async-start(f32[4,64,512]{2,1,0:T(8,128)} %bitcast.20), calls=%async_computation.3 | async-start | bytes 1048576 | tf_op jit(solution)/shard_map/all_to_all | solution.py:147
  125.0 9.7 %copy-start.5 = (f32[64,64]{1,0:T(8,128)}, f32[64,64]{1,0:T(8,128)S(1)}, u32[]{:S(2)}) copy-start(f32[64,64]{1,0:T(8,128)S(1)} %convolution_add_fusion.1) | copy-start | bytes 49156
Sparse Core Ops, SparseCore 0:
  10.1 49.2 all-gather.2

commit v6 on v5

--- a/solution.py
+++ b/solution.py
@@ -19,9 +19,9 @@
     return lax.dot_general(a, b, (((1,), (1,)), ((), ())), preferred_element_type=F32, **kw)
 
 
-def two_parts(v):
-    top = lax.reduce_precision(v, 8, 7)
-    return top.astype(BF16), (v - top).astype(BF16)
+def passed(v, axis, by):
+    n = lax.axis_size(axis)
+    return lax.ppermute(v, axis, [(i, (i + by) % n) for i in range(n)])
 
 
 def spread(v, axis):
@@ -59,23 +59,69 @@
     put(ns, jnp.concatenate([a_own, exps], axis=1))
 
 
-def turn_kernel(nx, nz, in_ref, out_ref):
+def turn_kernel(nx, nz, parts_ref0, parts_ref1, out_ref):
     run = 128
-
-    @pl.loop(0, in_ref.shape[0] // 64)
+    n = parts_ref0.shape[1]
+
+    @pl.loop(0, nz)
+    def _(z):
+        for part, in_ref in enumerate((parts_ref0, parts_ref1)):
+            for q in range(nx // 2):
+                for k in range(nz // 2):
+                    first = (q * nz + k) * run
+                    second = first + nz // 2 * run
+                    pair = halves(
+                        in_ref[z, :, first : first + run].astype(F32),
+                        in_ref[z, :, second : second + run].astype(F32),
+                    )
+                    for h, value in enumerate(pair):
+                        at = ((2 * k + h) * nx // 2 + q) * run
+                        out_ref[z, part * n : (part + 1) * n, at : at + run] = value.astype(BF16)
+
+
+def cross_kernel(nx, nz, iz_ref, exps_ref, c0_ref, c1_ref, s_ref, place_ref, term_ref, out_ref):
+    n, ns = c0_ref.shape[1:]
+    cols, nf = s_ref.shape[0] // 2, place_ref.shape[2] // 2
+    group = 128 // n
+    pair = iz_ref[0] // 2
+    scale = exps_ref[2], exps_ref[3]
+    for part, c_ref in enumerate((c0_ref, c1_ref)):
+
+        @pl.loop(0, nz // group)
+        def _(step):
+            zs = pl.ds(step * group, group)
+            rows = c_ref[zs].reshape(group * n, ns)
+            both = dot_t(rows, s_ref[...])
+            term = term_ref[zs, part * n : (part + 1) * n, :].reshape(group * n, cols)
+            cross = (both[:, :cols] + both[:, cols:] + term) * scale[0]
+            share = jnp.zeros((group * n, 2 * nf), F32)
+            for x in range(nx):
+                at = pl.ds(pl.multiple_of(x * nz * 64 + pair * 128, 128), 128)
+                picked = c_ref[zs, :, at].reshape(group * n, 128)
+                share += jnp.dot(picked, place_ref[x], preferred_element_type=F32)
+            share = (share[:, :nf] + share[:, nf:]) * scale[1]
+            lane = lax.broadcasted_iota(jnp.int32, share.shape, 1)
+            marks = jnp.where(lane == 0, exps_ref[0], exps_ref[1])
+            tail = jnp.concatenate([share, marks], axis=1)
+            here = pl.ds(part * n, n)
+            out_ref[zs, here, :cols] = cross.reshape(group, n, cols)
+            out_ref[zs, here, cols:] = tail.reshape(group, n, 2 * nf)
+
+
+def diag_kernel(v_ref, c_ref, out_ref, parts_ref):
+    nx, nz, rows, cols = v_ref.shape
+    for z in range(nz):
+        value = v_ref[:, z].reshape(nx * rows, cols)
+        top = value.astype(BF16)
+        parts_ref[0, :, z * cols : (z + 1) * cols] = top
+        parts_ref[1, :, z * cols : (z + 1) * cols] = (value - top.astype(F32)).astype(BF16)
+
+    @pl.loop(0, c_ref.shape[0] // 256)
     def _(step):
-        at_rows = pl.ds(pl.multiple_of(step * 64, 64), 64)
-        for q in range(nx // 2):
-            for k in range(nz // 2):
-                first = (q * nz + k) * run
-                second = first + nz // 2 * run
-                pair = halves(
-                    in_ref[at_rows, first : first + run].astype(F32),
-                    in_ref[at_rows, second : second + run].astype(F32),
-                )
-                for h, value in enumerate(pair):
-                    at = ((2 * k + h) * nx // 2 + q) * run
-                    out_ref[at_rows, at : at + run] = value.astype(BF16)
+        at = pl.ds(pl.multiple_of(step * 256, 256), 256)
+        c = c_ref[at, :]
+        both = dot_t(parts_ref[0], c) + dot_t(parts_ref[1], c)
+        out_ref[:, :, at] = both.reshape(nx, rows, 256)
 
 
 def natural_kernel(nx, nz, in_ref, out_ref):
@@ -107,43 +153,55 @@
     )(s_own, a_own)
     route = [(t * group + b, (t - 1) * group + b) for t in range(1, steps) for b in range(group)]
     packed = lax.ppermute(packed, ("y", "c", "x", "z"), route)
-    succ = spread(packed, "x")
-    succ = succ.transpose(1, 0, 2, 3)
-    s_cols = succ[..., :ns].reshape(2 * cols, ns)
-    a_two = succ[..., ns : ns + nf].reshape(2, cols, nf)
-    exps = jnp.max(succ[0, :, :, ns + nf : ns + nf + 2].astype(F32), axis=(0, 1))
+    before, after = passed(packed, "x", 1), passed(packed, "x", -1)
+    far_top, far_low = passed(packed[0], "x", 2), passed(packed[1], "x", -2)
+    far = jnp.stack([far_top, far_low])
+    s_cols = jnp.zeros((2, nx, rows, ns), BF16)
+    tails = jnp.zeros((2, nx, rows, 2 * nf), BF16)
+    for by, block in ((0, packed), (nx - 1, before), (1, after), (2, far)):
+        at = (ix + by) % nx
+        s_cols = lax.dynamic_update_index_in_dim(s_cols, block[..., :ns], at, 1)
+        tails = lax.dynamic_update_index_in_dim(tails, block[..., ns:], at, 1)
+    s_cols = s_cols.reshape(2 * cols, ns)
+    a_two = tails[..., :nf].reshape(2, cols, nf)
+    exps = jnp.max(tails[0, :, :, nf : nf + 2].astype(F32), axis=(0, 1))
+    exps = jnp.concatenate([exps, jnp.exp2(14 - exps)])
 
     link_rows = lax.dynamic_slice_in_dim(link, ix * nz * rows, nz * rows, 0)
-    arrow_term = dot_t(link_rows, a_two[0].astype(F32) + a_two[1].astype(F32), precision=HIGH)
+    term = dot_t(link_rows, a_two[0].astype(F32) + a_two[1].astype(F32), precision=HIGH)
+    term = term.reshape(nz, rows, cols)
     place = jnp.concatenate([a_two[0], a_two[1]], axis=1).reshape(nx, 1, rows, 2 * nf)
-    here = lax.broadcasted_iota(jnp.int32, (1, nz, 1, 1), 1) == iz
-    place = jnp.where(here, place, jnp.zeros((), BF16)).reshape(ns, 2 * nf)
-    s_cols, arrow_term, place = lax.optimization_barrier((s_cols, arrow_term, place))
-
-    c_rows = lax.all_gather(c_own, "z", axis=0, tiled=True)
+    here = lax.broadcasted_iota(jnp.int32, (1, 2, 1, 1), 1) == iz % 2
+    place = jnp.where(here, place, jnp.zeros((), BF16)).reshape(nx, 2 * rows, 2 * nf)
+
+    half = rows // 2
+    c_parts = spread(c_own[:half], "z"), lax.all_gather(c_own[half:], "z", axis=0)
     c_turned = pl.pallas_call(
         functools.partial(turn_kernel, nx, nz),
-        out_shape=jax.ShapeDtypeStruct(c_rows.shape, BF16),
+        out_shape=jax.ShapeDtypeStruct((nz, rows, ns), BF16),
         cost_estimate=pl.CostEstimate(flops=0, bytes_accessed=20 << 20, transcendentals=0),
         compiler_params=pltpu.CompilerParams(vmem_limit_bytes=16 << 20),
-    )(c_rows)
-
-    cross2 = dot_t(c_rows, s_cols)
-    cross = (cross2[:, :cols] + cross2[:, cols:] + arrow_term) * jnp.exp2(14 - exps[0])
-    share2 = jnp.dot(c_rows, place, preferred_element_type=F32)
-    share = (share2[:, :nf] + share2[:, nf:]) * jnp.exp2(14 - exps[1])
-    lane = lax.broadcasted_iota(jnp.int32, (nz * rows, nf), 1)
-    marks = jnp.where(lane == 0, exps[0], exps[1])
-    sent = jnp.concatenate([cross.astype(F16), share.astype(F16), marks.astype(F16)], axis=1)
-    sent = lax.all_to_all(sent.reshape(nz, rows, -1), "z", 0, 0, tiled=True)
+    )(*c_parts)
+    in_smem, in_vmem = pl.BlockSpec(memory_space=pltpu.SMEM), pl.BlockSpec(memory_space=pltpu.VMEM)
+    sent = pl.pallas_call(
+        functools.partial(cross_kernel, nx, nz),
+        out_shape=jax.ShapeDtypeStruct((nz, rows, cols + 2 * nf), F32),
+        in_specs=[in_smem] * 2 + [in_vmem] * 5,
+        compiler_params=pltpu.CompilerParams(vmem_limit_bytes=24 << 20),
+    )(iz.reshape(1), exps, *c_parts, s_cols, place, term)
+    sent = sent.astype(F16)
+    sent = lax.all_to_all(sent, "z", 0, 0, tiled=True)
     cross = sent[..., :cols]
     marks = sent[:, :1, cols + nf : cols + nf + 2].astype(F32)
     scale = jnp.exp2(marks[..., :1] - 14)
 
     every = spread(cross, "x").astype(F32) * scale[None]
-    every = every.transpose(0, 2, 1, 3).reshape(cols, ns)
-    diag2 = dot_t(jnp.concatenate(two_parts(every), axis=0), c_turned)
-    diag = (diag2[:cols] + diag2[cols:]).reshape(nx, rows, nz * rows)
+    diag = pl.pallas_call(
+        diag_kernel,
+        out_shape=jax.ShapeDtypeStruct((nx, rows, nz * rows), F32),
+        scratch_shapes=[pltpu.VMEM((2, cols, ns), BF16)],
+        compiler_params=pltpu.CompilerParams(vmem_limit_bytes=24 << 20),
+    )(every, c_turned.reshape(nz * rows, ns))
     diag = lax.all_to_all(diag, "x", 0, 0, tiled=True)
 
     cross_rows = pl.pallas_call(

time: 142 us -> 137 us (0.965)
  the two profiles are of different devices: /device:TPU:16 before, /device:TPU:56 now
where the time goes in v6:
time: 137 us; the launch traced here: 136 us
  starting transfers between devices  35.7 us (26%)
  waiting for transfers between devices  31.4 us (23%)
  local copies, waits for them, and re-layouts  18.6 us (14%)
  blocking collectives  15.9 us (12%)
  between operations  14.4 us (11%)
  Pallas kernels  13.5 us (10%)
  other arithmetic  5.08 us (4%)
    all_to_all x1, blocking collectives, shards(): sent = lax.all_to_all(sent, 'z', 0, 0, tiled=True)  15.9 us
    all_to_all x2, starting transfers between devices, spread(): lax.all_to_all(jnp.broadcast_to(v[None], (n,) + v.shape), axis, 0, 0, til...  15.2 us
    ppermute x4, starting transfers between devices, passed(): return lax.ppermute(v, axis, [(i, (i + by) % n) for i in range(n)])  14.4 us
    ppermute x4, waiting for transfers between devices, passed(): return lax.ppermute(v, axis, [(i, (i + by) % n) for i in range(n)])  12.4 us
    all_to_all x1, waiting for transfers between devices, shards(): diag = lax.all_to_all(diag, 'x', 0, 0, tiled=True)  7.31 us
    all_gather x1, waiting for transfers between devices, shards(): lax.all_gather(c_own[half:], 'z', axis=0)  5.98 us
    pallas_call x1, Pallas kernels, shards(): pl.pallas_call(functools.partial(cross_kernel, nx, nz), out_shape=jax.Sha...  5.34 us
    all_to_all x2, waiting for transfers between devices, spread(): lax.all_to_all(jnp.broadcast_to(v[None], (n,) + v.shape), axis, 0, 0, til...  5.04 us
  transfers between devices with their start and end apart: 9, of which 5 were waited for; matrix products, arithmetic and copies ran while one was open for 14% of the time, Pallas kernels for 2%

profile of v6, /device:TPU:56, one launch (start us, length us, event | category | flops | bytes accessed | tf_op | source)
XLA Modules:
  0.0 135.7 jit_solution(8685731840800333019)
XLA Ops:
  7.2 2.2 %shard_map.85 = bf16[2,64,2176]{2,1,0:T(8,128)(2,1)} custom-call(f32[64,2048]{1,0:T(8,128)} %bitcast.88, f32[64,64]{1,0:T(8,128)} %bitcast.92), custom_call_target="tpu_custom_call" | custom-call | tf_op jit(solution)/shard_map/pallas_call | solution.py:150
  9.4 2.7 %collective-permute-start = (bf16[2,64,2176]{2,1,0:T(8,128)(2,1)}, bf16[2,64,2176]{2,1,0:T(8,128)(2,1)S(1)}, u32[]{:S(2)}, u32[]{:S(2)}) collective-permute-start(bf16[2,64,2176]{2,1,0:T(8,128)(2,1)} %shard_map.85), channel_id=1, source_target_pairs={{32,0},{33,1},{34,2},{35,3},{36,4},{37,5},{38,6},{39,7},{40,8},{41... | collective-permute-start | bytes 1671176 | tf_op jit(solution)/shard_map/ppermute | solution.py:155
  12.1 1.6 %fusion.19 = (bf16[1,32,2048]{2,1,0:T(8,128)(2,1)}, bf16[32,2048]{1,0:T(8,128)(2,1)S(1)}) fusion(bf16[1,64,2048]{2,1,0:T(8,128)(2,1)} %param.6), kind=kLoop, calls=%fused_computation.47 | loop fusion | bytes 524288 | tf_op jit(solution)/shard_map/slice | solution.py:178
  14.8 10.3 %all-to-all-start = ((bf16[8,32,2048]{2,1,0:T(8,128)(2,1)}), bf16[8,32,2048]{2,1,0:T(8,128)(2,1)S(1)}, u32[]{:S(2)}, u32[]{:S(2)}) async-start(bf16[8,32,2048]{2,1,0:T(8,128)(2,1)} %broadcast_in_dim.90), calls=%async_computation | async-start | bytes 2097152 | tf_op jit(solution)/shard_map/all_to_all | solution.py:29
  26.3 4.9 %collective-permute-start.4 = (bf16[64,2176]{1,0:T(8,128)(2,1)S(1)}, bf16[64,2176]{1,0:T(8,128)(2,1)S(1)}, u32[]{:S(2)}, u32[]{:S(2)}) collective-permute-start(bf16[64,2176]{1,0:T(8,128)(2,1)S(1)} %get-tuple-element.6), channel_id=1, source_target_pairs={{0,16},{8,24},{16,0},{24,8},{1,17},{9,25},{17,1},{25,9},{2,18},{10... | collective-permute-start | bytes 835592 | tf_op jit(solution)/shard_map/ppermute | solution.py:24
  31.2 2.4 %collective-permute-start.3 = (bf16[64,2176]{1,0:T(8,128)(2,1)S(1)}, bf16[64,2176]{1,0:T(8,128)(2,1)S(1)}, u32[]{:S(2)}, u32[]{:S(2)}) collective-permute-start(bf16[64,2176]{1,0:T(8,128)(2,1)S(1)} %get-tuple-element.5), channel_id=1, source_target_pairs={{0,16},{8,24},{16,0},{24,8},{1,17},{9,25},{17,1},{25,9},{2,18},{10... | collective-permute-start | bytes 835592 | tf_op jit(solution)/shard_map/ppermute | solution.py:24
  33.7 3.4 %collective-permute-start.1 = (bf16[2,64,2176]{2,1,0:T(8,128)(2,1)S(1)}, bf16[2,64,2176]{2,1,0:T(8,128)(2,1)}, u32[]{:S(2)}, u32[]{:S(2)}) collective-permute-start(bf16[2,64,2176]{2,1,0:T(8,128)(2,1)S(1)} %collective-permute-done), channel_id=1, source_target_pairs={{0,8},{8,16},{16,24},{24,0},{1,9},{9,17},{17,25},{25,1},{2,10},{10... | collective-permute-start | bytes 1671176 | tf_op jit(solution)/shard_map/ppermute | solution.py:24
  37.1 3.7 %collective-permute-start.2 = (bf16[2,64,2176]{2,1,0:T(8,128)(2,1)S(1)}, bf16[2,64,2176]{2,1,0:T(8,128)(2,1)}, u32[]{:S(2)}, u32[]{:S(2)}) collective-permute-start(bf16[2,64,2176]{2,1,0:T(8,128)(2,1)S(1)} %collective-permute-done), channel_id=1, source_target_pairs={{0,24},{8,0},{16,8},{24,16},{1,25},{9,1},{17,9},{25,17},{2,26},{10... | collective-permute-start | bytes 1671176 | tf_op jit(solution)/shard_map/ppermute | solution.py:24
  40.7 1.6 %broadcast_in_dim.91 = bf16[2,4,64,2048]{3,2,1,0:T(8,128)(2,1)} broadcast(bf16[]{:T(256)} %constant.78.clone.1), dimensions={} | broadcast | bytes 2097154 | tf_op jit(solution)/shard_map/broadcast_in_dim | solution.py:159
  43.2 1.7 %collective-permute-done.3 = bf16[64,2176]{1,0:T(8,128)(2,1)S(1)} collective-permute-done((bf16[64,2176]{1,0:T(8,128)(2,1)S(1)}, bf16[64,2176]{1,0:T(8,128)(2,1)S(1)}, u32[]{:S(2)}, u32[]{:S(2)}) %collective-permute-start.3) | collective-permute-done | bytes 278560 | tf_op jit(solution)/shard_map/ppermute | solution.py:24
  45.1 10.6 %collective-permute-done.1 = bf16[2,64,2176]{2,1,0:T(8,128)(2,1)} collective-permute-done((bf16[2,64,2176]{2,1,0:T(8,128)(2,1)S(1)}, bf16[2,64,2176]{2,1,0:T(8,128)(2,1)}, u32[]{:S(2)}, u32[]{:S(2)}) %collective-permute-start.1) | collective-permute-done | bytes 557088 | tf_op jit(solution)/shard_map/ppermute | solution.py:24
  57.5 3.1 %dynamic_update_slice.29 = bf16[2,4,64,128]{2,1,3,0:T(4,128)(2,1)S(1)} dynamic-update-slice(bf16[2,4,64,128]{2,1,3,0:T(4,128)(2,1)S(1)} %copy.32, bf16[2,1,64,128]{2,1,3,0:T(2,128)(2,1)S(1)} %copy.33, s32[]{:T(128)} %constant.79.clone.1, s32[]{:T(128)S(6)} %select_n.59, s32[]{:T(128)} %constant.79.clone.1, s32[]{:T(128)} %constant.79.clone.1) | dynamic-update-slice | bytes 65540 | tf_op jit(solution)/shard_map/jit(dynamic_update_index_in_dim)/dynamic_update_slice | solution.py:164
  61.6 1.9 %fusion.3 = bf16[2,4,64,2048]{3,2,1,0:T(8,128)(2,1)} fusion(bf16[2,4,64,2048]{3,2,1,0:T(8,128)(2,1)} %fusion.4, s32[]{:T(128)S(6)} %select_n.55, bf16[2,64,2176]{2,1,0:T(8,128)(2,1)} %collective-permute-done.1), kind=kLoop, calls=%fused_computation.9 | loop fusion | bytes 1048580 | tf_op jit(solution)/shard_map/jit(dynamic_update_index_in_dim)/dynamic_update_slice | solution.py:163
  63.4 1.9 %fusion.2 = bf16[2,4,64,2048]{3,2,1,0:T(8,128)(2,1)} fusion(bf16[2,4,64,2048]{3,2,1,0:T(8,128)(2,1)} %fusion.3, s32[]{:T(128)S(6)} %select_n.57, bf16[2,64,2176]{2,1,0:T(8,128)(2,1)} %collective-permute-done.2), kind=kLoop, calls=%fused_computation.7 | loop fusion | bytes 1048580 | tf_op jit(solution)/shard_map/jit(dynamic_update_index_in_dim)/dynamic_update_slice | solution.py:163
  66.6 6.0 %all-gather.2.cloned.1.call-done.c1_ref.parts_ref1 = bf16[8,32,2048]{2,1,0:T(8,128)(2,1)} async-done(((bf16[1,32,2048]{2,1,0:T(8,128)(2,1)}), bf16[8,32,2048]{2,1,0:T(8,128)(2,1)}) %all-gather.2.cloned.1.call-update) | async-done | bytes 1048592 | tf_op jit(solution)/shard_map/all_gather | solution.py:178
  73.8 5.3 %shard_map.86 = f32[8,64,384]{2,1,0:T(8,128)S(1)} custom-call(s32[1]{0:T(128)} %bitcast.1.iz_ref, f32[4]{0:T(128)S(1)} %pad_maximum_fusion.1.exps_ref, bf16[8,32,2048]{2,1,0:T(8,128)(2,1)S(1)} %all-to-all-done.c0_ref.parts_ref0, bf16[8,32,2048]{2,1,0:T(8,128)(2,1)S(1)} %copy-done.3, bf16[512,2048]{1,0:T(8,128)(2,1)} %bitcast.21.s_ref, ...), custom_call_target="tpu_custom_call" | custom-call | tf_op jit(solution)/shard_map/pallas_call | solution.py:186
  79.2 15.9 %all_to_all.20 = f16[8,64,384]{2,1,0:T(8,128)(2,1)S(1)} all-to-all(f16[8,64,384]{2,1,0:T(8,128)(2,1)S(1)} %convert_element_type.26), channel_id=1, replica_groups=mesh['y'=8,'c'=2,'x'=4,'z'=8] {'z'}, dimensions={0} | all-to-all | bytes 786432 | tf_op jit(solution)/shard_map/all_to_all | solution.py:193
  96.3 4.8 %all-to-all-start.2 = ((f16[4,8,64,256]{3,2,1,0:T(8,128)(2,1)}), f16[4,8,64,256]{3,2,1,0:T(8,128)(2,1)}, u32[]{:S(2)}, u32[]{:S(2)}) async-start(f16[4,8,64,256]{3,2,1,0:T(8,128)(2,1)} %broadcast_in_dim.103), calls=%async_computation.2 | async-start | bytes 2097152 | tf_op jit(solution)/shard_map/all_to_all | solution.py:29
  104.8 2.2 %shard_map.89 = f32[64,2048]{1,0:T(8,128)} custom-call(f32[8,64,256]{2,1,0:T(8,128)} %convert_multiply_fusion.1.in_ref), custom_call_target="tpu_custom_call" | custom-call | tf_op jit(solution)/shard_map/pallas_call | solution.py:207
  107.0 5.0 %all-to-all-done.2 = f16[4,8,64,256]{3,2,1,0:T(8,128)(2,1)} async-done(((f16[4,8,64,256]{3,2,1,0:T(8,128)(2,1)}), f16[4,8,64,256]{3,2,1,0:T(8,128)(2,1)}, u32[]{:S(2)}, u32[]{:S(2)}) %all-to-all-start.2) | async-done | bytes 1048608 | tf_op jit(solution)/shard_map/all_to_all | solution.py:29
  112.1 1.6 %convert_multiply_fusion.v_ref = f32[4,8,64,256]{3,2,1,0:T(8,128)S(1)} fusion(f16[4,8,64,256]{3,2,1,0:T(8,128)(2,1)} %all-to-all-done.2, f32[8]{0:T(128)S(1)} %get-tuple-element.3), kind=kLoop, calls=%fused_computation.1 | loop fusion | flops 1048576 | bytes 3145760 | tf_op jit(solution)/shard_map/mul | solution.py:198
  113.7 2.7 %shard_map.88 = f32[4,64,512]{2,1,0:T(8,128)} custom-call(f32[4,8,64,256]{3,2,1,0:T(8,128)S(1)} %convert_multiply_fusion.v_ref, bf16[512,2048]{1,0:T(8,128)(2,1)S(1)} %bitcast.79), custom_call_target="tpu_custom_call" | custom-call | tf_op jit(solution)/shard_map/pallas_call | solution.py:199
  116.4 3.5 %all-to-all-start.3 = ((f32[4,64,512]{2,1,0:T(8,128)}), f32[4,64,512]{2,1,0:T(8,128)S(1)}, u32[]{:S(2)}, u32[]{:S(2)}) async-start(f32[4,64,512]{2,1,0:T(8,128)} %shard_map.88), calls=%async_computation.3 | async-start | bytes 1048576 | tf_op jit(solution)/shard_map/all_to_all | solution.py:205
  120.6 7.3 %all-to-all-done.3 = f32[4,64,512]{2,1,0:T(8,128)S(1)} async-done(((f32[4,64,512]{2,1,0:T(8,128)}), f32[4,64,512]{2,1,0:T(8,128)S(1)}, u32[]{:S(2)}, u32[]{:S(2)}) %all-to-all-start.3) | async-done | bytes 524320 | tf_op jit(solution)/shard_map/all_to_all | solution.py:205
  (63 shorter events, 14.9 us)
Async XLA Ops:
  7.2 18.7 %copy-start = (f32[1,2048,64]{1,2,0:T(8,128)S(1)}, f32[1,2048,64]{1,2,0:T(8,128)}, u32[]{:S(2)}) copy-start(f32[1,2048,64]{1,2,0:T(8,128)} %param.7) | copy-start | bytes 1572868
  9.4 16.9 %collective-permute-start = (bf16[2,64,2176]{2,1,0:T(8,128)(2,1)}, bf16[2,64,2176]{2,1,0:T(8,128)(2,1)S(1)}, u32[]{:S(2)}, u32[]{:S(2)}) collective-permute-start(bf16[2,64,2176]{2,1,0:T(8,128)(2,1)} %shard_map.85), channel_id=1, source_target_pairs={{32,0},{33,1},{34,2},{35,3},{36,4},{37,5},{38,6},{39,7},{40,8},{41... | collective-permute-start | bytes 1671176 | tf_op jit(solution)/shard_map/ppermute | solution.py:155
  14.8 51.7 %all-to-all-start = ((bf16[8,32,2048]{2,1,0:T(8,128)(2,1)}), bf16[8,32,2048]{2,1,0:T(8,128)(2,1)S(1)}, u32[]{:S(2)}, u32[]{:S(2)}) async-start(bf16[8,32,2048]{2,1,0:T(8,128)(2,1)} %broadcast_in_dim.90), calls=%async_computation | async-start | bytes 2097152 | tf_op jit(solution)/shard_map/all_to_all | solution.py:29
  25.1 47.4 %all-gather.2.cloned.1.call-start = ((), (), s32[]{:S(2)}) async-start(), calls=%async_computation.4 | async-start | bytes 1179648 | tf_op jit(solution)/shard_map/all_gather | solution.py:178
  26.3 16.9 %collective-permute-start.4 = (bf16[64,2176]{1,0:T(8,128)(2,1)S(1)}, bf16[64,2176]{1,0:T(8,128)(2,1)S(1)}, u32[]{:S(2)}, u32[]{:S(2)}) collective-permute-start(bf16[64,2176]{1,0:T(8,128)(2,1)S(1)} %get-tuple-element.6), channel_id=1, source_target_pairs={{0,16},{8,24},{16,0},{24,8},{1,17},{9,25},{17,1},{25,9},{2,18},{10... | collective-permute-start | bytes 835592 | tf_op jit(solution)/shard_map/ppermute | solution.py:24
  31.2 13.7 %collective-permute-start.3 = (bf16[64,2176]{1,0:T(8,128)(2,1)S(1)}, bf16[64,2176]{1,0:T(8,128)(2,1)S(1)}, u32[]{:S(2)}, u32[]{:S(2)}) collective-permute-start(bf16[64,2176]{1,0:T(8,128)(2,1)S(1)} %get-tuple-element.5), channel_id=1, source_target_pairs={{0,16},{8,24},{16,0},{24,8},{1,17},{9,25},{17,1},{25,9},{2,18},{10... | collective-permute-start | bytes 835592 | tf_op jit(solution)/shard_map/ppermute | solution.py:24
  33.7 22.1 %collective-permute-start.1 = (bf16[2,64,2176]{2,1,0:T(8,128)(2,1)S(1)}, bf16[2,64,2176]{2,1,0:T(8,128)(2,1)}, u32[]{:S(2)}, u32[]{:S(2)}) collective-permute-start(bf16[2,64,2176]{2,1,0:T(8,128)(2,1)S(1)} %collective-permute-done), channel_id=1, source_target_pairs={{0,8},{8,16},{16,24},{24,0},{1,9},{9,17},{17,25},{25,1},{2,10},{10... | collective-permute-start | bytes 1671176 | tf_op jit(solution)/shard_map/ppermute | solution.py:24
  37.1 19.4 %collective-permute-start.2 = (bf16[2,64,2176]{2,1,0:T(8,128)(2,1)S(1)}, bf16[2,64,2176]{2,1,0:T(8,128)(2,1)}, u32[]{:S(2)}, u32[]{:S(2)}) collective-permute-start(bf16[2,64,2176]{2,1,0:T(8,128)(2,1)S(1)} %collective-permute-done), channel_id=1, source_target_pairs={{0,24},{8,0},{16,8},{24,16},{1,25},{9,1},{17,9},{25,17},{2,26},{10... | collective-permute-start | bytes 1671176 | tf_op jit(solution)/shard_map/ppermute | solution.py:24
  72.5 1.2 copy-start.3
  95.1 6.0 %copy-start.4 = (bf16[8,32,2048]{2,1,0:T(8,128)(2,1)S(1)}, bf16[8,32,2048]{2,1,0:T(8,128)(2,1)}, u32[]{:S(2)}) copy-start(bf16[8,32,2048]{2,1,0:T(8,128)(2,1)} %all-gather.2.cloned.1.call-done.c1_ref.parts_ref1) | copy-start | bytes 3145732
  96.3 15.8 %all-to-all-start.2 = ((f16[4,8,64,256]{3,2,1,0:T(8,128)(2,1)}), f16[4,8,64,256]{3,2,1,0:T(8,128)(2,1)}, u32[]{:S(2)}, u32[]{:S(2)}) async-start(f16[4,8,64,256]{3,2,1,0:T(8,128)(2,1)} %broadcast_in_dim.103), calls=%async_computation.2 | async-start | bytes 2097152 | tf_op jit(solution)/shard_map/all_to_all | solution.py:29
  102.2 1.3 copy-start.1
  104.8 8.9 %copy-start.2 = (bf16[8,64,2048]{2,1,0:T(8,128)(2,1)S(1)}, bf16[8,64,2048]{2,1,0:T(8,128)(2,1)}, u32[]{:S(2)}) copy-start(bf16[8,64,2048]{2,1,0:T(8,128)(2,1)} %copy-done.1) | copy-start | bytes 6291460
  113.7 6.2 %copy-start.7 = (f32[64,64]{1,0:T(8,128)S(1)}, f32[64,64]{1,0:T(8,128)}, u32[]{:S(2)}) copy-start(f32[64,64]{1,0:T(8,128)} %param.11) | copy-start | bytes 49156
  113.7 6.5 %copy-start.5 = (f32[1,64,2048]{2,1,0:T(8,128)S(1)}, f32[1,64,2048]{2,1,0:T(8,128)}, u32[]{:S(2)}) copy-start(f32[1,64,2048]{2,1,0:T(8,128)} %param.8) | copy-start | bytes 1572868
  116.4 11.5 %all-to-all-start.3 = ((f32[4,64,512]{2,1,0:T(8,128)}), f32[4,64,512]{2,1,0:T(8,128)S(1)}, u32[]{:S(2)}, u32[]{:S(2)}) async-start(f32[4,64,512]{2,1,0:T(8,128)} %shard_map.88), calls=%async_computation.3 | async-start | bytes 1048576 | tf_op jit(solution)/shard_map/all_to_all | solution.py:205
  120.2 8.6 %copy-start.6 = (f32[64,64]{1,0:T(8,128)}, f32[64,64]{1,0:T(8,128)S(1)}, u32[]{:S(2)}) copy-start(f32[64,64]{1,0:T(8,128)S(1)} %convolution_add_fusion.1) | copy-start | bytes 49156
Sparse Core Ops, SparseCore 0:
  28.6 43.8 all-gather.1

commit v7 on v5

--- a/solution.py
+++ b/solution.py
@@ -17,11 +17,6 @@
 
 def dot_t(a, b, **kw):
     return lax.dot_general(a, b, (((1,), (1,)), ((), ())), preferred_element_type=F32, **kw)
-
-
-def two_parts(v):
-    top = lax.reduce_precision(v, 8, 7)
-    return top.astype(BF16), (v - top).astype(BF16)
 
 
 def spread(v, axis):
@@ -78,6 +73,43 @@
                     out_ref[at_rows, at : at + run] = value.astype(BF16)
 
 
+def cross_kernel(nz, iz_ref, exps_ref, c_ref, s_ref, place_ref, term_ref, out_ref):
+    nx, _, rows, _ = s_ref.shape
+    all_rows, ns = c_ref.shape
+    nf = place_ref.shape[2] // 2
+    run = 2 * rows
+    lane = lax.broadcasted_iota(jnp.int32, (all_rows, run), 1)
+    for q in range(nx // 2):
+        block = s_ref[2 * q : 2 * q + 2, :, :, :ns].reshape(2 * run, ns)
+        both = dot_t(c_ref[...], block)
+        first, second = both[:, :run], both[:, run:]
+        first = first + pltpu.roll(first, rows, 1)
+        second = second + pltpu.roll(second, rows, 1)
+        cross = jnp.where(lane < rows, first, second)
+        at = slice(q * run, (q + 1) * run)
+        out_ref[:, at] = (cross + term_ref[:, at]) * exps_ref[2]
+    pair = iz_ref[0] // 2
+    share = jnp.zeros((all_rows, 2 * nf), F32)
+    for x in range(nx):
+        at = pl.ds(pl.multiple_of(x * nz * rows + pair * run, run), run)
+        share += jnp.dot(c_ref[:, at], place_ref[x], preferred_element_type=F32)
+    share = (share + pltpu.roll(share, nf, 1)) * exps_ref[3]
+    marks = jnp.where(lane == nf, exps_ref[0], exps_ref[1])
+    out_ref[:, nx * rows :] = jnp.where(lane < nf, share, marks)
+
+
+def diag_kernel(top_ref, low_ref, c_ref, out_ref, parts_ref):
+    nx, nz, rows, cols = top_ref.shape
+    for part, v_ref in enumerate((top_ref, low_ref)):
+        for z in range(nz):
+            value = v_ref[:, z].reshape(nx * rows, cols)
+            parts_ref[part, :, z * cols : (z + 1) * cols] = value
+    for at in range(0, c_ref.shape[0], 256):
+        c = c_ref[at : at + 256, :]
+        both = dot_t(parts_ref[0], c) + dot_t(parts_ref[1], c)
+        out_ref[:, :, at : at + 256] = both.reshape(nx, rows, 256)
+
+
 def natural_kernel(nx, nz, in_ref, out_ref):
     rows = out_ref.shape[0]
     run = 2 * rows
@@ -108,17 +140,17 @@
     route = [(t * group + b, (t - 1) * group + b) for t in range(1, steps) for b in range(group)]
     packed = lax.ppermute(packed, ("y", "c", "x", "z"), route)
     succ = spread(packed, "x")
-    succ = succ.transpose(1, 0, 2, 3)
-    s_cols = succ[..., :ns].reshape(2 * cols, ns)
-    a_two = succ[..., ns : ns + nf].reshape(2, cols, nf)
-    exps = jnp.max(succ[0, :, :, ns + nf : ns + nf + 2].astype(F32), axis=(0, 1))
+    tails = succ[..., ns:]
+    a_two = tails[..., :nf]
+    exps = jnp.max(tails[:, 0, :, nf : nf + 2].astype(F32), axis=(0, 1))
+    exps = jnp.concatenate([exps, jnp.exp2(14 - exps)])
 
     link_rows = lax.dynamic_slice_in_dim(link, ix * nz * rows, nz * rows, 0)
-    arrow_term = dot_t(link_rows, a_two[0].astype(F32) + a_two[1].astype(F32), precision=HIGH)
-    place = jnp.concatenate([a_two[0], a_two[1]], axis=1).reshape(nx, 1, rows, 2 * nf)
-    here = lax.broadcasted_iota(jnp.int32, (1, nz, 1, 1), 1) == iz
-    place = jnp.where(here, place, jnp.zeros((), BF16)).reshape(ns, 2 * nf)
-    s_cols, arrow_term, place = lax.optimization_barrier((s_cols, arrow_term, place))
+    a_cols = a_two[:, 0].astype(F32) + a_two[:, 1].astype(F32)
+    term = dot_t(link_rows, a_cols.reshape(cols, nf), precision=HIGH)
+    place = jnp.concatenate([a_two[:, 0], a_two[:, 1]], axis=2)[:, None]
+    here = lax.broadcasted_iota(jnp.int32, (1, 2, 1, 1), 1) == iz % 2
+    place = jnp.where(here, place, jnp.zeros((), BF16)).reshape(nx, 2 * rows, 2 * nf)
 
     c_rows = lax.all_gather(c_own, "z", axis=0, tiled=True)
     c_turned = pl.pallas_call(
@@ -127,23 +159,29 @@
         cost_estimate=pl.CostEstimate(flops=0, bytes_accessed=20 << 20, transcendentals=0),
         compiler_params=pltpu.CompilerParams(vmem_limit_bytes=16 << 20),
     )(c_rows)
-
-    cross2 = dot_t(c_rows, s_cols)
-    cross = (cross2[:, :cols] + cross2[:, cols:] + arrow_term) * jnp.exp2(14 - exps[0])
-    share2 = jnp.dot(c_rows, place, preferred_element_type=F32)
-    share = (share2[:, :nf] + share2[:, nf:]) * jnp.exp2(14 - exps[1])
-    lane = lax.broadcasted_iota(jnp.int32, (nz * rows, nf), 1)
-    marks = jnp.where(lane == 0, exps[0], exps[1])
-    sent = jnp.concatenate([cross.astype(F16), share.astype(F16), marks.astype(F16)], axis=1)
-    sent = lax.all_to_all(sent.reshape(nz, rows, -1), "z", 0, 0, tiled=True)
+    in_smem, in_vmem = pl.BlockSpec(memory_space=pltpu.SMEM), pl.BlockSpec(memory_space=pltpu.VMEM)
+    sent = pl.pallas_call(
+        functools.partial(cross_kernel, nz),
+        out_shape=jax.ShapeDtypeStruct((nz * rows, cols + 2 * nf), F32),
+        in_specs=[in_smem] * 2 + [in_vmem] * 4,
+        compiler_params=pltpu.CompilerParams(vmem_limit_bytes=24 << 20),
+    )(iz.reshape(1), exps, c_rows, succ, place, term)
+    sent = sent.reshape(nz, rows, cols + 2 * nf)
+    sent = sent.astype(F16)
+    sent = lax.all_to_all(sent, "z", 0, 0, tiled=True)
     cross = sent[..., :cols]
     marks = sent[:, :1, cols + nf : cols + nf + 2].astype(F32)
     scale = jnp.exp2(marks[..., :1] - 14)
 
     every = spread(cross, "x").astype(F32) * scale[None]
-    every = every.transpose(0, 2, 1, 3).reshape(cols, ns)
-    diag2 = dot_t(jnp.concatenate(two_parts(every), axis=0), c_turned)
-    diag = (diag2[:cols] + diag2[cols:]).reshape(nx, rows, nz * rows)
+    every_top = lax.reduce_precision(every, 8, 7)
+    every_low = (every - every_top).astype(BF16)
+    diag = pl.pallas_call(
+        diag_kernel,
+        out_shape=jax.ShapeDtypeStruct((nx, rows, nz * rows), F32),
+        scratch_shapes=[pltpu.VMEM((2, cols, ns), BF16)],
+        compiler_params=pltpu.CompilerParams(vmem_limit_bytes=24 << 20),
+    )(every_top.astype(BF16), every_low, c_turned)
     diag = lax.all_to_all(diag, "x", 0, 0, tiled=True)
 
     cross_rows = pl.pallas_call(

time: 142 us -> 129 us (0.908)
  the two profiles are of different devices: /device:TPU:16 before, /device:TPU:24 now
where the time goes in v7:
time: 129 us
  waiting for transfers between devices  58.4 us (45%)
  blocking collectives  20.6 us (16%)
  between operations  14.3 us (11%)
  starting transfers between devices  14 us (11%)
  Pallas kernels  9.65 us (7%)
  local copies, waits for them, and re-layouts  6 us (5%)
  other arithmetic  5.02 us (4%)
    all_to_all x2, waiting for transfers between devices, spread(): lax.all_to_all(jnp.broadcast_to(v[None], (n,) + v.shape), axis, 0, 0, til...  36.3 us
    all_to_all x1, blocking collectives, shards(): sent = lax.all_to_all(sent, 'z', 0, 0, tiled=True)  20.6 us
    all_to_all x2, starting transfers between devices, spread(): lax.all_to_all(jnp.broadcast_to(v[None], (n,) + v.shape), axis, 0, 0, til...  8.53 us
    all_to_all x1, waiting for transfers between devices, shards(): diag = lax.all_to_all(diag, 'x', 0, 0, tiled=True)  8.43 us
    ppermute x1, waiting for transfers between devices, shards(): packed = lax.ppermute(packed, ('y', 'c', 'x', 'z'), route)  7.34 us
    all_gather x1, waiting for transfers between devices, shards(): c_rows = lax.all_gather(c_own, 'z', axis=0, tiled=True)  5.64 us
    all_to_all x1, starting transfers between devices, shards(): diag = lax.all_to_all(diag, 'x', 0, 0, tiled=True)  3.47 us
    unnamed x18, local copies, waits for them, and re-layouts  2.96 us
  transfers between devices with their start and end apart: 5, of which 5 were waited for; matrix products, arithmetic and copies ran while one was open for 4% of the time, Pallas kernels for 4%

profile of v7, /device:TPU:24, one launch (start us, length us, event | category | flops | bytes accessed | tf_op | source)
XLA Modules:
  0.0 129.0 jit_solution(15251915852392223319)
XLA Ops:
  7.2 0.7 all-gather.3.cloned.1.call-update
  7.9 2.1 %shard_map.85 = bf16[2,64,2176]{2,1,0:T(8,128)(2,1)} custom-call(f32[64,2048]{1,0:T(8,128)} %bitcast.38, f32[64,64]{1,0:T(8,128)} %bitcast.42), custom_call_target="tpu_custom_call" | custom-call | tf_op jit(solution)/shard_map/pallas_call | solution.py:136
  10.0 1.9 %collective-permute-start = (bf16[2,64,2176]{2,1,0:T(8,128)(2,1)}, bf16[2,64,2176]{2,1,0:T(8,128)(2,1)S(1)}, u32[]{:S(2)}, u32[]{:S(2)}) collective-permute-start(bf16[2,64,2176]{2,1,0:T(8,128)(2,1)} %shard_map.85), channel_id=1, source_target_pairs={{32,0},{33,1},{34,2},{35,3},{36,4},{37,5},{38,6},{39,7},{40,8},{41... | collective-permute-start | bytes 1671176 | tf_op jit(solution)/shard_map/ppermute | solution.py:141
  12.0 7.3 %collective-permute-done = bf16[2,64,2176]{2,1,0:T(8,128)(2,1)S(1)} collective-permute-done((bf16[2,64,2176]{2,1,0:T(8,128)(2,1)}, bf16[2,64,2176]{2,1,0:T(8,128)(2,1)S(1)}, u32[]{:S(2)}, u32[]{:S(2)}) %collective-permute-start) | collective-permute-done | bytes 557088 | tf_op jit(solution)/shard_map/ppermute | solution.py:141
  19.3 1.6 %broadcast_in_dim.49 = bf16[4,2,64,2176]{3,2,1,0:T(8,128)(2,1)} broadcast(bf16[2,64,2176]{2,1,0:T(8,128)(2,1)S(1)} %collective-permute-done), dimensions={1,2,3} | broadcast | bytes 2785280 | tf_op jit(solution)/shard_map/broadcast_in_dim | solution.py:24
  21.0 4.3 %all-to-all-start = ((bf16[4,2,64,2176]{3,2,1,0:T(8,128)(2,1)}), bf16[4,2,64,2176]{3,2,1,0:T(8,128)(2,1)S(1)}, u32[]{:S(2)}, u32[]{:S(2)}) async-start(bf16[4,2,64,2176]{3,2,1,0:T(8,128)(2,1)} %broadcast_in_dim.49), calls=%async_computation | async-start | bytes 4456448 | tf_op jit(solution)/shard_map/all_to_all | solution.py:24
  25.4 27.2 %all-to-all-done.s_ref = bf16[4,2,64,2176]{3,2,1,0:T(8,128)(2,1)S(1)} async-done(((bf16[4,2,64,2176]{3,2,1,0:T(8,128)(2,1)}), bf16[4,2,64,2176]{3,2,1,0:T(8,128)(2,1)S(1)}, u32[]{:S(2)}, u32[]{:S(2)}) %all-to-all-start) | async-done | bytes 2228256 | tf_op jit(solution)/shard_map/all_to_all | solution.py:24
  53.5 5.6 %all-gather.3.cloned.1.call-done = bf16[1,512,2048]{2,1,0:T(8,128)(2,1)} async-done(((bf16[1,64,2048]{2,1,0:T(8,128)(2,1)}), bf16[1,512,2048]{2,1,0:T(8,128)(2,1)}) %all-gather.3.cloned.1.call-update) | async-done | bytes 2097168 | tf_op jit(solution)/shard_map/all_gather | solution.py:155
  59.2 1.6 %copy-done.1 = bf16[1,512,2048]{2,1,0:T(8,128)(2,1)S(1)} copy-done((bf16[1,512,2048]{2,1,0:T(8,128)(2,1)S(1)}, bf16[1,512,2048]{2,1,0:T(8,128)(2,1)}, u32[]{:S(2)}) %copy-start.1) | copy-done | bytes 2097176
  60.8 2.1 %shard_map.86 = f32[512,384]{1,0:T(8,128)S(1)} custom-call(s32[1]{0:T(128)} %bitcast.1.iz_ref, f32[4]{0:T(128)S(1)} %pad_maximum_fusion.1.exps_ref, bf16[512,2048]{1,0:T(8,128)(2,1)S(1)} %bitcast.33, bf16[4,2,64,2176]{3,2,1,0:T(8,128)(2,1)S(1)} %all-to-all-done.s_ref, bf16[4,128,128]{2,1,0:T(8,128)(2,1)S(1)} %bitcast_select_fusion.place_ref, ...), custom_call_target="tpu_custom_call" | custom-call | tf_op jit(solution)/shard_map/pallas_call | solution.py:163
  62.9 20.6 %all_to_all.20 = f16[8,64,384]{2,1,0:T(8,128)(2,1)S(1)} all-to-all(f16[8,64,384]{2,1,0:T(8,128)(2,1)S(1)} %bitcast.37), channel_id=1, replica_groups=mesh['y'=8,'c'=2,'x'=4,'z'=8] {'z'}, dimensions={0} | all-to-all | bytes 786432 | tf_op jit(solution)/shard_map/all_to_all | solution.py:171
  83.6 1.1 broadcast_in_dim.56
  84.7 4.2 %all-to-all-start.2 = ((f16[4,8,64,256]{3,2,1,0:T(8,128)(2,1)}), f16[4,8,64,256]{3,2,1,0:T(8,128)(2,1)}, u32[]{:S(2)}, u32[]{:S(2)}) async-start(f16[4,8,64,256]{3,2,1,0:T(8,128)(2,1)} %broadcast_in_dim.56), calls=%async_computation.2 | async-start | bytes 2097152 | tf_op jit(solution)/shard_map/all_to_all | solution.py:24
  89.0 1.1 shard_map.87.c_ref
  90.1 1.3 %copy-done.3 = bf16[512,2048]{1,0:T(8,128)(2,1)} copy-done((bf16[512,2048]{1,0:T(8,128)(2,1)}, bf16[512,2048]{1,0:T(8,128)(2,1)S(1)}, u32[]{:S(2)}) %copy-start.3) | copy-done | bytes 2097176
  91.8 0.9 convert_multiply_fusion.1.in_ref
  92.7 2.2 %shard_map.89 = f32[64,2048]{1,0:T(8,128)} custom-call(f32[8,64,256]{2,1,0:T(8,128)} %convert_multiply_fusion.1.in_ref), custom_call_target="tpu_custom_call" | custom-call | tf_op jit(solution)/shard_map/pallas_call | solution.py:187
  94.8 0.7 multiply_reduce_fusion
  95.6 9.1 %all-to-all-done.2 = f16[4,8,64,256]{3,2,1,0:T(8,128)(2,1)} async-done(((f16[4,8,64,256]{3,2,1,0:T(8,128)(2,1)}), f16[4,8,64,256]{3,2,1,0:T(8,128)(2,1)}, u32[]{:S(2)}, u32[]{:S(2)}) %all-to-all-start.2) | async-done | bytes 1048608 | tf_op jit(solution)/shard_map/all_to_all | solution.py:24
  104.7 1.8 %fusion = (bf16[4,8,64,256]{3,2,1,0:T(8,128)(2,1)S(1)}, bf16[4,8,64,256]{3,2,1,0:T(8,128)(2,1)S(1)}) fusion(f16[4,8,64,256]{3,2,1,0:T(8,128)(2,1)} %all-to-all-done.2, f32[8]{0:T(128)S(1)} %get-tuple-element.3), kind=kLoop, calls=%fused_computation.3 | loop fusion | flops 3145728 | bytes 3145760 | tf_op jit(solution)/shard_map/convert_element_type | solution.py:178
  106.5 2.1 %shard_map.88 = f32[4,64,512]{2,1,0:T(8,128)} custom-call(bf16[4,8,64,256]{3,2,1,0:T(8,128)(2,1)S(1)} %get-tuple-element.8.top_ref, bf16[4,8,64,256]{3,2,1,0:T(8,128)(2,1)S(1)} %get-tuple-element.7.low_ref, bf16[512,2048]{1,0:T(8,128)(2,1)S(1)} %copy-done.4), custom_call_target="tpu_custom_call" | custom-call | tf_op jit(solution)/shard_map/pallas_call | solution.py:179
  108.6 3.5 %all-to-all-start.3 = ((f32[4,64,512]{2,1,0:T(8,128)}), f32[4,64,512]{2,1,0:T(8,128)S(1)}, u32[]{:S(2)}, u32[]{:S(2)}) async-start(f32[4,64,512]{2,1,0:T(8,128)} %shard_map.88), calls=%async_computation.3 | async-start | bytes 1048576 | tf_op jit(solution)/shard_map/all_to_all | solution.py:185
  112.8 8.4 %all-to-all-done.3 = f32[4,64,512]{2,1,0:T(8,128)S(1)} async-done(((f32[4,64,512]{2,1,0:T(8,128)}), f32[4,64,512]{2,1,0:T(8,128)S(1)}, u32[]{:S(2)}, u32[]{:S(2)}) %all-to-all-start.3) | async-done | bytes 524320 | tf_op jit(solution)/shard_map/all_to_all | solution.py:185
  121.3 0.9 add_bitcast_fusion
  (36 shorter events, 2.2 us)
Async XLA Ops:
  7.2 45.9 %copy-start = (f32[1,2048,64]{1,2,0:T(8,128)S(1)}, f32[1,2048,64]{1,2,0:T(8,128)}, u32[]{:S(2)}) copy-start(f32[1,2048,64]{1,2,0:T(8,128)} %param.7) | copy-start | bytes 1572868
  7.2 52.0 %all-gather.3.cloned.1.call-start = ((), (), s32[]{:S(2)}) async-start(), calls=%async_computation.4 | async-start | bytes 2359296 | tf_op jit(solution)/shard_map/all_gather | solution.py:155
  10.0 9.3 %collective-permute-start = (bf16[2,64,2176]{2,1,0:T(8,128)(2,1)}, bf16[2,64,2176]{2,1,0:T(8,128)(2,1)S(1)}, u32[]{:S(2)}, u32[]{:S(2)}) collective-permute-start(bf16[2,64,2176]{2,1,0:T(8,128)(2,1)} %shard_map.85), channel_id=1, source_target_pairs={{32,0},{33,1},{34,2},{35,3},{36,4},{37,5},{38,6},{39,7},{40,8},{41... | collective-permute-start | bytes 1671176 | tf_op jit(solution)/shard_map/ppermute | solution.py:141
  21.0 31.7 %all-to-all-start = ((bf16[4,2,64,2176]{3,2,1,0:T(8,128)(2,1)}), bf16[4,2,64,2176]{3,2,1,0:T(8,128)(2,1)S(1)}, u32[]{:S(2)}, u32[]{:S(2)}) async-start(bf16[4,2,64,2176]{3,2,1,0:T(8,128)(2,1)} %broadcast_in_dim.49), calls=%async_computation | async-start | bytes 4456448 | tf_op jit(solution)/shard_map/all_to_all | solution.py:24
  59.2 1.6 %copy-start.1 = (bf16[1,512,2048]{2,1,0:T(8,128)(2,1)S(1)}, bf16[1,512,2048]{2,1,0:T(8,128)(2,1)}, u32[]{:S(2)}) copy-start(bf16[1,512,2048]{2,1,0:T(8,128)(2,1)} %all-gather.3.cloned.1.call-done) | copy-start | bytes 6291460
  83.5 5.4 %copy-start.2 = (bf16[1,512,2048]{2,1,0:T(8,128)(2,1)S(1)}, bf16[1,512,2048]{2,1,0:T(8,128)(2,1)}, u32[]{:S(2)}) copy-start(bf16[1,512,2048]{2,1,0:T(8,128)(2,1)} %all-gather.3.cloned.1.call-done) | copy-start | bytes 6291460
  84.7 20.0 %all-to-all-start.2 = ((f16[4,8,64,256]{3,2,1,0:T(8,128)(2,1)}), f16[4,8,64,256]{3,2,1,0:T(8,128)(2,1)}, u32[]{:S(2)}, u32[]{:S(2)}) async-start(f16[4,8,64,256]{3,2,1,0:T(8,128)(2,1)} %broadcast_in_dim.56), calls=%async_computation.2 | async-start | bytes 2097152 | tf_op jit(solution)/shard_map/all_to_all | solution.py:24
  90.1 1.3 %copy-start.3 = (bf16[512,2048]{1,0:T(8,128)(2,1)}, bf16[512,2048]{1,0:T(8,128)(2,1)S(1)}, u32[]{:S(2)}) copy-start(bf16[512,2048]{1,0:T(8,128)(2,1)S(1)} %shard_map.87.c_ref) | copy-start | bytes 6291460
  92.7 13.8 %copy-start.4 = (bf16[512,2048]{1,0:T(8,128)(2,1)S(1)}, bf16[512,2048]{1,0:T(8,128)(2,1)}, u32[]{:S(2)}) copy-start(bf16[512,2048]{1,0:T(8,128)(2,1)} %copy-done.3) | copy-start | bytes 6291460
  106.5 5.6 %copy-start.6 = (f32[64,64]{1,0:T(8,128)S(1)}, f32[64,64]{1,0:T(8,128)}, u32[]{:S(2)}) copy-start(f32[64,64]{1,0:T(8,128)} %multiply_reduce_fusion) | copy-start | bytes 49156
  106.5 5.6 %copy-start.8 = (f32[64,64]{1,0:T(8,128)S(1)}, f32[64,64]{1,0:T(8,128)}, u32[]{:S(2)}) copy-start(f32[64,64]{1,0:T(8,128)} %param.11) | copy-start | bytes 49156
  106.5 5.9 %copy-start.5 = (f32[1,64,2048]{2,1,0:T(8,128)S(1)}, f32[1,64,2048]{2,1,0:T(8,128)}, u32[]{:S(2)}) copy-start(f32[1,64,2048]{2,1,0:T(8,128)} %param.8) | copy-start | bytes 1572868
  108.6 12.6 %all-to-all-start.3 = ((f32[4,64,512]{2,1,0:T(8,128)}), f32[4,64,512]{2,1,0:T(8,128)S(1)}, u32[]{:S(2)}, u32[]{:S(2)}) async-start(f32[4,64,512]{2,1,0:T(8,128)} %shard_map.88), calls=%async_computation.3 | async-start | bytes 1048576 | tf_op jit(solution)/shard_map/all_to_all | solution.py:185
  112.4 9.7 %copy-start.7 = (f32[64,64]{1,0:T(8,128)}, f32[64,64]{1,0:T(8,128)S(1)}, u32[]{:S(2)}) copy-start(f32[64,64]{1,0:T(8,128)S(1)} %convolution_add_fusion.1) | copy-start | bytes 49156
Sparse Core Ops, SparseCore 0:
  10.1 49.0 all-gather.2

commit v8 on v7

--- a/solution.py
+++ b/solution.py
@@ -17,6 +17,11 @@
 
 def dot_t(a, b, **kw):
     return lax.dot_general(a, b, (((1,), (1,)), ((), ())), preferred_element_type=F32, **kw)
+
+
+def passed(v, axis, by):
+    n = lax.axis_size(axis)
+    return lax.ppermute(v, axis, [(i, (i + by) % n) for i in range(n)])
 
 
 def spread(v, axis):
@@ -73,8 +78,25 @@
                     out_ref[at_rows, at : at + run] = value.astype(BF16)
 
 
-def cross_kernel(nz, iz_ref, exps_ref, c_ref, s_ref, place_ref, term_ref, out_ref):
+def place_kernel(iz_ref, tails_ref, out_ref):
+    rows, run = tails_ref.shape[2:]
+    lane = lax.broadcasted_iota(jnp.int32, (rows, run), 1)
+    odd = lax.rem(iz_ref[0], 2)
+    for x in range(tails_ref.shape[0]):
+        top = tails_ref[x, 0].astype(F32)
+        low = pltpu.roll(tails_ref[x, 1].astype(F32), run // 2, 1)
+        both = jnp.where(lane < run // 2, top, low)
+        out_ref[x, :rows] = jnp.where(odd == 0, both, 0.0).astype(BF16)
+        out_ref[x, rows:] = jnp.where(odd == 1, both, 0.0).astype(BF16)
+
+
+def cross_kernel(order, iz_ref, exps_ref, s_ref, place_ref, term_ref, *refs):
+    block_refs, (out_ref, c_ref) = refs[:-2], refs[-2:]
     nx, _, rows, _ = s_ref.shape
+    nz = len(order)
+    for by, block_ref in zip(order, block_refs):
+        at = lax.rem(iz_ref[0] + by + nz, nz) * rows
+        c_ref[pl.ds(pl.multiple_of(at, rows), rows), :] = block_ref[...]
     all_rows, ns = c_ref.shape
     nf = place_ref.shape[2] // 2
     run = 2 * rows
@@ -148,24 +170,31 @@
     link_rows = lax.dynamic_slice_in_dim(link, ix * nz * rows, nz * rows, 0)
     a_cols = a_two[:, 0].astype(F32) + a_two[:, 1].astype(F32)
     term = dot_t(link_rows, a_cols.reshape(cols, nf), precision=HIGH)
-    place = jnp.concatenate([a_two[:, 0], a_two[:, 1]], axis=2)[:, None]
-    here = lax.broadcasted_iota(jnp.int32, (1, 2, 1, 1), 1) == iz % 2
-    place = jnp.where(here, place, jnp.zeros((), BF16)).reshape(nx, 2 * rows, 2 * nf)
-
-    c_rows = lax.all_gather(c_own, "z", axis=0, tiled=True)
+    in_smem, in_vmem = pl.BlockSpec(memory_space=pltpu.SMEM), pl.BlockSpec(memory_space=pltpu.VMEM)
+    place = pl.pallas_call(
+        place_kernel,
+        out_shape=jax.ShapeDtypeStruct((nx, 2 * rows, 2 * nf), BF16),
+        in_specs=[in_smem, in_vmem],
+        cost_estimate=pl.CostEstimate(flops=10**11, bytes_accessed=1 << 20, transcendentals=0),
+    )(iz.reshape(1), tails)
+
+    c_blocks = [c_own] + [passed(c_own, "z", -by) for by in (1, -1, 2, -2, 4)]
+    c_blocks += [passed(c_blocks[3], "z", -1), passed(c_blocks[4], "z", 1)]
+    sent, c_rows = pl.pallas_call(
+        functools.partial(cross_kernel, (0, 1, -1, 2, -2, 4, 3, -3)),
+        out_shape=(
+            jax.ShapeDtypeStruct((nz * rows, cols + 2 * nf), F32),
+            jax.ShapeDtypeStruct((nz * rows, ns), BF16),
+        ),
+        in_specs=[in_smem] * 2 + [in_vmem] * (3 + len(c_blocks)),
+        compiler_params=pltpu.CompilerParams(vmem_limit_bytes=16 << 20),
+    )(iz.reshape(1), exps, succ, place, term, *c_blocks)
     c_turned = pl.pallas_call(
         functools.partial(turn_kernel, nx, nz),
         out_shape=jax.ShapeDtypeStruct(c_rows.shape, BF16),
         cost_estimate=pl.CostEstimate(flops=0, bytes_accessed=20 << 20, transcendentals=0),
-        compiler_params=pltpu.CompilerParams(vmem_limit_bytes=16 << 20),
+        compiler_params=pltpu.CompilerParams(vmem_limit_bytes=8 << 20),
     )(c_rows)
-    in_smem, in_vmem = pl.BlockSpec(memory_space=pltpu.SMEM), pl.BlockSpec(memory_space=pltpu.VMEM)
-    sent = pl.pallas_call(
-        functools.partial(cross_kernel, nz),
-        out_shape=jax.ShapeDtypeStruct((nz * rows, cols + 2 * nf), F32),
-        in_specs=[in_smem] * 2 + [in_vmem] * 4,
-        compiler_params=pltpu.CompilerParams(vmem_limit_bytes=24 << 20),
-    )(iz.reshape(1), exps, c_rows, succ, place, term)
     sent = sent.reshape(nz, rows, cols + 2 * nf)
     sent = sent.astype(F16)
     sent = lax.all_to_all(sent, "z", 0, 0, tiled=True)
@@ -180,7 +209,7 @@
         diag_kernel,
         out_shape=jax.ShapeDtypeStruct((nx, rows, nz * rows), F32),
         scratch_shapes=[pltpu.VMEM((2, cols, ns), BF16)],
-        compiler_params=pltpu.CompilerParams(vmem_limit_bytes=24 << 20),
+        compiler_params=pltpu.CompilerParams(vmem_limit_bytes=12 << 20),
     )(every_top.astype(BF16), every_low, c_turned)
     diag = lax.all_to_all(diag, "x", 0, 0, tiled=True)
 

time: 129 us -> 130 us (level)
  the two profiles are of different devices: /device:TPU:24 before, /device:TPU:8 now
where the time goes in v8:
time: 130 us; the launch traced here: 129 us
  starting transfers between devices  47.5 us (37%)
  waiting for transfers between devices  34.4 us (26%)
  blocking collectives  21.1 us (16%)
  Pallas kernels  12.1 us (9%)
  local copies, waits for them, and re-layouts  7.4 us (6%)
  other arithmetic  4.78 us (4%)
    ppermute x7, starting transfers between devices, passed(): return lax.ppermute(v, axis, [(i, (i + by) % n) for i in range(n)])  33 us
    all_to_all x1, blocking collectives, shards(): sent = lax.all_to_all(sent, 'z', 0, 0, tiled=True)  21.1 us
    ppermute x7, waiting for transfers between devices, passed(): return lax.ppermute(v, axis, [(i, (i + by) % n) for i in range(n)])  12.5 us
    all_to_all x2, starting transfers between devices, spread(): lax.all_to_all(jnp.broadcast_to(v[None], (n,) + v.shape), axis, 0, 0, til...  9.12 us
    ppermute x1, waiting for transfers between devices, shards(): packed = lax.ppermute(packed, ('y', 'c', 'x', 'z'), route)  7.34 us
    all_to_all x1, waiting for transfers between devices, shards(): diag = lax.all_to_all(diag, 'x', 0, 0, tiled=True)  7.31 us
    all_to_all x2, waiting for transfers between devices, spread(): lax.all_to_all(jnp.broadcast_to(v[None], (n,) + v.shape), axis, 0, 0, til...  7.28 us
    unnamed x18, local copies, waits for them, and re-layouts  3.87 us
  transfers between devices with their start and end apart: 11, of which 8 were waited for; matrix products, arithmetic and copies ran while one was open for 3% of the time, Pallas kernels for 4%

profile of v8, /device:TPU:8, one launch (start us, length us, event | category | flops | bytes accessed | tf_op | source)
XLA Modules:
  0.0 129.2 jit_solution(5709353836389600800)
XLA Ops:
  0.6 2.2 %shard_map.85 = bf16[2,64,2176]{2,1,0:T(8,128)(2,1)} custom-call(f32[64,2048]{1,0:T(8,128)} %bitcast.36, f32[64,64]{1,0:T(8,128)} %bitcast.40), custom_call_target="tpu_custom_call" | custom-call | tf_op jit(solution)/shard_map/pallas_call | solution.py:158
  2.8 1.9 %collective-permute-start = (bf16[2,64,2176]{2,1,0:T(8,128)(2,1)}, bf16[2,64,2176]{2,1,0:T(8,128)(2,1)S(1)}, u32[]{:S(2)}, u32[]{:S(2)}) collective-permute-start(bf16[2,64,2176]{2,1,0:T(8,128)(2,1)} %shard_map.85), channel_id=1, source_target_pairs={{32,0},{33,1},{34,2},{35,3},{36,4},{37,5},{38,6},{39,7},{40,8},{41... | collective-permute-start | bytes 1671176 | tf_op jit(solution)/shard_map/ppermute | solution.py:163
  4.7 7.3 %collective-permute-done = bf16[2,64,2176]{2,1,0:T(8,128)(2,1)S(1)} collective-permute-done((bf16[2,64,2176]{2,1,0:T(8,128)(2,1)}, bf16[2,64,2176]{2,1,0:T(8,128)(2,1)S(1)}, u32[]{:S(2)}, u32[]{:S(2)}) %collective-permute-start) | collective-permute-done | bytes 557088 | tf_op jit(solution)/shard_map/ppermute | solution.py:163
  12.1 1.6 %broadcast_in_dim.10 = bf16[4,2,64,2176]{3,2,1,0:T(8,128)(2,1)} broadcast(bf16[2,64,2176]{2,1,0:T(8,128)(2,1)S(1)} %collective-permute-done), dimensions={1,2,3} | broadcast | bytes 2785280 | tf_op jit(solution)/shard_map/broadcast_in_dim | solution.py:29
  13.7 4.4 %all-to-all-start = ((bf16[4,2,64,2176]{3,2,1,0:T(8,128)(2,1)}), bf16[4,2,64,2176]{3,2,1,0:T(8,128)(2,1)S(1)}, u32[]{:S(2)}, u32[]{:S(2)}) async-start(bf16[4,2,64,2176]{3,2,1,0:T(8,128)(2,1)} %broadcast_in_dim.10), calls=%async_computation | async-start | bytes 4456448 | tf_op jit(solution)/shard_map/all_to_all | solution.py:29
  18.2 6.1 %collective-permute-start.4 = (bf16[64,2048]{1,0:T(8,128)(2,1)S(1)}, bf16[64,2048]{1,0:T(8,128)(2,1)S(1)}, u32[]{:S(2)}, u32[]{:S(2)}) collective-permute-start(bf16[64,2048]{1,0:T(8,128)(2,1)S(1)} %bitcast.27), channel_id=1, source_target_pairs={{0,2},{1,3},{2,4},{3,5},{4,6},{5,7},{6,0},{7,1},{8,10},{9,11},{10,... | collective-permute-start | bytes 786440 | tf_op jit(solution)/shard_map/ppermute | solution.py:24
  24.2 6.8 %collective-permute-start.3 = (bf16[64,2048]{1,0:T(8,128)(2,1)S(1)}, bf16[64,2048]{1,0:T(8,128)(2,1)S(1)}, u32[]{:S(2)}, u32[]{:S(2)}) collective-permute-start(bf16[64,2048]{1,0:T(8,128)(2,1)S(1)} %bitcast.28), channel_id=1, source_target_pairs={{0,6},{1,7},{2,0},{3,1},{4,2},{5,3},{6,4},{7,5},{8,14},{9,15},{10,... | collective-permute-start | bytes 786440 | tf_op jit(solution)/shard_map/ppermute | solution.py:24
  31.0 6.0 %collective-permute-start.5 = (bf16[64,2048]{1,0:T(8,128)(2,1)S(1)}, bf16[64,2048]{1,0:T(8,128)(2,1)}, u32[]{:S(2)}, u32[]{:S(2)}) collective-permute-start(bf16[64,2048]{1,0:T(8,128)(2,1)S(1)} %bitcast.29), channel_id=1, source_target_pairs={{0,4},{1,5},{2,6},{3,7},{4,0},{5,1},{6,2},{7,3},{8,12},{9,13},{10,... | collective-permute-start | bytes 786440 | tf_op jit(solution)/shard_map/ppermute | solution.py:24
  37.0 3.4 %collective-permute-start.2 = (bf16[64,2048]{1,0:T(8,128)(2,1)S(1)}, bf16[64,2048]{1,0:T(8,128)(2,1)}, u32[]{:S(2)}, u32[]{:S(2)}) collective-permute-start(bf16[64,2048]{1,0:T(8,128)(2,1)S(1)} %bitcast.30), channel_id=1, source_target_pairs={{0,1},{1,2},{2,3},{3,4},{4,5},{5,6},{6,7},{7,0},{8,9},{9,10},{10,1... | collective-permute-start | bytes 786440 | tf_op jit(solution)/shard_map/ppermute | solution.py:24
  40.4 3.7 %collective-permute-start.1 = (bf16[64,2048]{1,0:T(8,128)(2,1)S(1)}, bf16[64,2048]{1,0:T(8,128)(2,1)}, u32[]{:S(2)}, u32[]{:S(2)}) collective-permute-start(bf16[64,2048]{1,0:T(8,128)(2,1)S(1)} %bitcast.31), channel_id=1, source_target_pairs={{0,7},{1,0},{2,1},{3,2},{4,3},{5,4},{6,5},{7,6},{8,15},{9,8},{10,9... | collective-permute-start | bytes 786440 | tf_op jit(solution)/shard_map/ppermute | solution.py:24
  44.1 2.2 %collective-permute-start.7 = (bf16[64,2048]{1,0:T(8,128)(2,1)S(1)}, bf16[64,2048]{1,0:T(8,128)(2,1)}, u32[]{:S(2)}, u32[]{:S(2)}) collective-permute-start(bf16[64,2048]{1,0:T(8,128)(2,1)S(1)} %collective-permute-done.4.refs_4_), channel_id=1, source_target_pairs={{0,1},{1,2},{2,3},{3,4},{4,5},{5,6},{6,7},{7,0},{8,9},{9,10},{10,1... | collective-permute-start | bytes 786440 | tf_op jit(solution)/shard_map/ppermute | solution.py:24
  46.3 4.9 %collective-permute-start.6 = (bf16[64,2048]{1,0:T(8,128)(2,1)S(1)}, bf16[64,2048]{1,0:T(8,128)(2,1)}, u32[]{:S(2)}, u32[]{:S(2)}) collective-permute-start(bf16[64,2048]{1,0:T(8,128)(2,1)S(1)} %collective-permute-done.3.refs_3_), channel_id=1, source_target_pairs={{0,7},{1,0},{2,1},{3,2},{4,3},{5,4},{6,5},{7,6},{8,15},{9,8},{10,9... | collective-permute-start | bytes 786440 | tf_op jit(solution)/shard_map/ppermute | solution.py:24
  52.0 1.7 %shard_map.86.place_ref = bf16[4,128,128]{2,1,0:T(8,128)(2,1)} custom-call(s32[1]{0:T(128)} %bitcast.1.iz_ref, bf16[4,2,64,128]{3,2,1,0:T(8,128)(2,1)} %slice.42.tails_ref), custom_call_target="tpu_custom_call" | custom-call | flops 99999997952 | bytes 1048576 | tf_op jit(solution)/shard_map/pallas_call | solution.py:174
  55.3 4.3 %collective-permute-done.2.refs_2_ = bf16[64,2048]{1,0:T(8,128)(2,1)} collective-permute-done((bf16[64,2048]{1,0:T(8,128)(2,1)S(1)}, bf16[64,2048]{1,0:T(8,128)(2,1)}, u32[]{:S(2)}, u32[]{:S(2)}) %collective-permute-start.2) | collective-permute-done | bytes 262176 | tf_op jit(solution)/shard_map/ppermute | solution.py:24
  61.1 4.1 %collective-permute-done.7.refs_7_ = bf16[64,2048]{1,0:T(8,128)(2,1)} collective-permute-done((bf16[64,2048]{1,0:T(8,128)(2,1)S(1)}, bf16[64,2048]{1,0:T(8,128)(2,1)}, u32[]{:S(2)}, u32[]{:S(2)}) %collective-permute-start.7) | collective-permute-done | bytes 262176 | tf_op jit(solution)/shard_map/ppermute | solution.py:24
  67.6 3.0 %shard_map.87 = (f32[512,384]{1,0:T(8,128)S(1)}, bf16[512,2048]{1,0:T(8,128)(2,1)S(1)}) custom-call(s32[1]{0:T(128)} %bitcast.1.iz_ref, f32[4]{0:T(128)S(1)} %pad_maximum_fusion.exps_ref, bf16[4,2,64,2176]{3,2,1,0:T(8,128)(2,1)S(1)} %all-to-all-done.s_ref, bf16[4,128,128]{2,1,0:T(8,128)(2,1)S(1)} %copy-done.4, f32[512,256]{1,0:T(8,128)S(1)} %fusion.2.term_ref, ...), custom_call_target="tpu_custom_call" | custom-call | tf_op jit(solution)/shard_map/pallas_call | solution.py:183
  72.0 21.1 %all_to_all.20 = f16[8,64,384]{2,1,0:T(8,128)(2,1)S(1)} all-to-all(f16[8,64,384]{2,1,0:T(8,128)(2,1)S(1)} %bitcast.35), channel_id=1, replica_groups=mesh['y'=8,'c'=2,'x'=4,'z'=8] {'z'}, dimensions={0} | all-to-all | bytes 786432 | tf_op jit(solution)/shard_map/all_to_all | solution.py:200
  94.2 4.7 %all-to-all-start.2 = ((f16[4,8,64,256]{3,2,1,0:T(8,128)(2,1)}), f16[4,8,64,256]{3,2,1,0:T(8,128)(2,1)}, u32[]{:S(2)}, u32[]{:S(2)}) async-start(f16[4,8,64,256]{3,2,1,0:T(8,128)(2,1)} %broadcast_in_dim.11), calls=%async_computation.2 | async-start | bytes 2097152 | tf_op jit(solution)/shard_map/all_to_all | solution.py:29
  102.8 2.0 %shard_map.90 = f32[64,2048]{1,0:T(8,128)} custom-call(f32[8,64,256]{2,1,0:T(8,128)} %convert_multiply_fusion.1.in_ref), custom_call_target="tpu_custom_call" | custom-call | tf_op jit(solution)/shard_map/pallas_call | solution.py:216
  105.6 7.3 %all-to-all-done.2 = f16[4,8,64,256]{3,2,1,0:T(8,128)(2,1)} async-done(((f16[4,8,64,256]{3,2,1,0:T(8,128)(2,1)}), f16[4,8,64,256]{3,2,1,0:T(8,128)(2,1)}, u32[]{:S(2)}, u32[]{:S(2)}) %all-to-all-start.2) | async-done | bytes 1048608 | tf_op jit(solution)/shard_map/all_to_all | solution.py:29
  112.9 1.7 %fusion = (bf16[4,8,64,256]{3,2,1,0:T(8,128)(2,1)S(1)}, bf16[4,8,64,256]{3,2,1,0:T(8,128)(2,1)S(1)}) fusion(f16[4,8,64,256]{3,2,1,0:T(8,128)(2,1)} %all-to-all-done.2, f32[8]{0:T(128)S(1)} %get-tuple-element.7), kind=kLoop, calls=%fused_computation.3 | loop fusion | flops 3145728 | bytes 3145760 | tf_op jit(solution)/shard_map/convert_element_type | solution.py:207
  114.6 2.1 %shard_map.89 = f32[4,64,512]{2,1,0:T(8,128)} custom-call(bf16[4,8,64,256]{3,2,1,0:T(8,128)(2,1)S(1)} %get-tuple-element.10.top_ref, bf16[4,8,64,256]{3,2,1,0:T(8,128)(2,1)S(1)} %get-tuple-element.9.low_ref, bf16[512,2048]{1,0:T(8,128)(2,1)S(1)} %shard_map.88.c_ref), custom_call_target="tpu_custom_call" | custom-call | tf_op jit(solution)/shard_map/pallas_call | solution.py:208
  116.7 3.5 %all-to-all-start.3 = ((f32[4,64,512]{2,1,0:T(8,128)}), f32[4,64,512]{2,1,0:T(8,128)S(1)}, u32[]{:S(2)}, u32[]{:S(2)}) async-start(f32[4,64,512]{2,1,0:T(8,128)} %shard_map.89), calls=%async_computation.3 | async-start | bytes 1048576 | tf_op jit(solution)/shard_map/all_to_all | solution.py:214
  121.0 7.3 %all-to-all-done.3 = f32[4,64,512]{2,1,0:T(8,128)S(1)} async-done(((f32[4,64,512]{2,1,0:T(8,128)}), f32[4,64,512]{2,1,0:T(8,128)S(1)}, u32[]{:S(2)}, u32[]{:S(2)}) %all-to-all-start.3) | async-done | bytes 524320 | tf_op jit(solution)/shard_map/all_to_all | solution.py:214
  (43 shorter events, 15.1 us)
Async XLA Ops:
  0.6 53.2 %copy-start = (f32[1,2048,64]{1,2,0:T(8,128)S(1)}, f32[1,2048,64]{1,2,0:T(8,128)}, u32[]{:S(2)}) copy-start(f32[1,2048,64]{1,2,0:T(8,128)} %param.7) | copy-start | bytes 1572868
  2.8 9.3 %collective-permute-start = (bf16[2,64,2176]{2,1,0:T(8,128)(2,1)}, bf16[2,64,2176]{2,1,0:T(8,128)(2,1)S(1)}, u32[]{:S(2)}, u32[]{:S(2)}) collective-permute-start(bf16[2,64,2176]{2,1,0:T(8,128)(2,1)} %shard_map.85), channel_id=1, source_target_pairs={{32,0},{33,1},{34,2},{35,3},{36,4},{37,5},{38,6},{39,7},{40,8},{41... | collective-permute-start | bytes 1671176 | tf_op jit(solution)/shard_map/ppermute | solution.py:163
  13.7 4.4 %copy-start.3 = (bf16[1,64,2048]{2,1,0:T(8,128)(2,1)S(1)}, bf16[1,64,2048]{2,1,0:T(8,128)(2,1)}, u32[]{:S(2)}) copy-start(bf16[1,64,2048]{2,1,0:T(8,128)(2,1)} %param.6) | copy-start | bytes 786436
  13.7 37.5 %all-to-all-start = ((bf16[4,2,64,2176]{3,2,1,0:T(8,128)(2,1)}), bf16[4,2,64,2176]{3,2,1,0:T(8,128)(2,1)S(1)}, u32[]{:S(2)}, u32[]{:S(2)}) async-start(bf16[4,2,64,2176]{3,2,1,0:T(8,128)(2,1)} %broadcast_in_dim.10), calls=%async_computation | async-start | bytes 4456448 | tf_op jit(solution)/shard_map/all_to_all | solution.py:29
  18.2 26.0 %collective-permute-start.4 = (bf16[64,2048]{1,0:T(8,128)(2,1)S(1)}, bf16[64,2048]{1,0:T(8,128)(2,1)S(1)}, u32[]{:S(2)}, u32[]{:S(2)}) collective-permute-start(bf16[64,2048]{1,0:T(8,128)(2,1)S(1)} %bitcast.27), channel_id=1, source_target_pairs={{0,2},{1,3},{2,4},{3,5},{4,6},{5,7},{6,0},{7,1},{8,10},{9,11},{10,... | collective-permute-start | bytes 786440 | tf_op jit(solution)/shard_map/ppermute | solution.py:24
  24.2 22.1 %collective-permute-start.3 = (bf16[64,2048]{1,0:T(8,128)(2,1)S(1)}, bf16[64,2048]{1,0:T(8,128)(2,1)S(1)}, u32[]{:S(2)}, u32[]{:S(2)}) collective-permute-start(bf16[64,2048]{1,0:T(8,128)(2,1)S(1)} %bitcast.28), channel_id=1, source_target_pairs={{0,6},{1,7},{2,0},{3,1},{4,2},{5,3},{6,4},{7,5},{8,14},{9,15},{10,... | collective-permute-start | bytes 786440 | tf_op jit(solution)/shard_map/ppermute | solution.py:24
  31.0 24.3 %collective-permute-start.5 = (bf16[64,2048]{1,0:T(8,128)(2,1)S(1)}, bf16[64,2048]{1,0:T(8,128)(2,1)}, u32[]{:S(2)}, u32[]{:S(2)}) collective-permute-start(bf16[64,2048]{1,0:T(8,128)(2,1)S(1)} %bitcast.29), channel_id=1, source_target_pairs={{0,4},{1,5},{2,6},{3,7},{4,0},{5,1},{6,2},{7,3},{8,12},{9,13},{10,... | collective-permute-start | bytes 786440 | tf_op jit(solution)/shard_map/ppermute | solution.py:24
  37.0 22.6 %collective-permute-start.2 = (bf16[64,2048]{1,0:T(8,128)(2,1)S(1)}, bf16[64,2048]{1,0:T(8,128)(2,1)}, u32[]{:S(2)}, u32[]{:S(2)}) collective-permute-start(bf16[64,2048]{1,0:T(8,128)(2,1)S(1)} %bitcast.30), channel_id=1, source_target_pairs={{0,1},{1,2},{2,3},{3,4},{4,5},{5,6},{6,7},{7,0},{8,9},{9,10},{10,1... | collective-permute-start | bytes 786440 | tf_op jit(solution)/shard_map/ppermute | solution.py:24
  40.4 20.6 %collective-permute-start.1 = (bf16[64,2048]{1,0:T(8,128)(2,1)S(1)}, bf16[64,2048]{1,0:T(8,128)(2,1)}, u32[]{:S(2)}, u32[]{:S(2)}) collective-permute-start(bf16[64,2048]{1,0:T(8,128)(2,1)S(1)} %bitcast.31), channel_id=1, source_target_pairs={{0,7},{1,0},{2,1},{3,2},{4,3},{5,4},{6,5},{7,6},{8,15},{9,8},{10,9... | collective-permute-start | bytes 786440 | tf_op jit(solution)/shard_map/ppermute | solution.py:24
  44.1 21.1 %collective-permute-start.7 = (bf16[64,2048]{1,0:T(8,128)(2,1)S(1)}, bf16[64,2048]{1,0:T(8,128)(2,1)}, u32[]{:S(2)}, u32[]{:S(2)}) collective-permute-start(bf16[64,2048]{1,0:T(8,128)(2,1)S(1)} %collective-permute-done.4.refs_4_), channel_id=1, source_target_pairs={{0,1},{1,2},{2,3},{3,4},{4,5},{5,6},{6,7},{7,0},{8,9},{9,10},{10,1... | collective-permute-start | bytes 786440 | tf_op jit(solution)/shard_map/ppermute | solution.py:24
  46.3 20.4 %collective-permute-start.6 = (bf16[64,2048]{1,0:T(8,128)(2,1)S(1)}, bf16[64,2048]{1,0:T(8,128)(2,1)}, u32[]{:S(2)}, u32[]{:S(2)}) collective-permute-start(bf16[64,2048]{1,0:T(8,128)(2,1)S(1)} %collective-permute-done.3.refs_3_), channel_id=1, source_target_pairs={{0,7},{1,0},{2,1},{3,2},{4,3},{5,4},{6,5},{7,6},{8,15},{9,8},{10,9... | collective-permute-start | bytes 786440 | tf_op jit(solution)/shard_map/ppermute | solution.py:24
  66.7 0.9 copy-start.4
  70.6 1.3 %copy-start.1 = (bf16[512,2048]{1,0:T(8,128)(2,1)}, bf16[512,2048]{1,0:T(8,128)(2,1)S(1)}, u32[]{:S(2)}) copy-start(bf16[512,2048]{1,0:T(8,128)(2,1)S(1)} %get-tuple-element.6.in_ref) | copy-start | bytes 6291460
  94.2 18.6 %all-to-all-start.2 = ((f16[4,8,64,256]{3,2,1,0:T(8,128)(2,1)}), f16[4,8,64,256]{3,2,1,0:T(8,128)(2,1)}, u32[]{:S(2)}, u32[]{:S(2)}) async-start(f16[4,8,64,256]{3,2,1,0:T(8,128)(2,1)} %broadcast_in_dim.11), calls=%async_computation.2 | async-start | bytes 2097152 | tf_op jit(solution)/shard_map/all_to_all | solution.py:29
  98.9 1.6 %copy-start.2 = (bf16[512,2048]{1,0:T(8,128)(2,1)S(1)}, bf16[512,2048]{1,0:T(8,128)(2,1)}, u32[]{:S(2)}) copy-start(bf16[512,2048]{1,0:T(8,128)(2,1)} %copy-done.1) | copy-start | bytes 6291460
  114.6 5.6 %copy-start.6 = (f32[64,64]{1,0:T(8,128)S(1)}, f32[64,64]{1,0:T(8,128)}, u32[]{:S(2)}) copy-start(f32[64,64]{1,0:T(8,128)} %multiply_reduce_fusion) | copy-start | bytes 49156
  114.6 5.6 %copy-start.8 = (f32[64,64]{1,0:T(8,128)S(1)}, f32[64,64]{1,0:T(8,128)}, u32[]{:S(2)}) copy-start(f32[64,64]{1,0:T(8,128)} %param.11) | copy-start | bytes 49156
  114.6 5.9 %copy-start.5 = (f32[1,64,2048]{2,1,0:T(8,128)S(1)}, f32[1,64,2048]{2,1,0:T(8,128)}, u32[]{:S(2)}) copy-start(f32[1,64,2048]{2,1,0:T(8,128)} %param.8) | copy-start | bytes 1572868
  116.7 11.5 %all-to-all-start.3 = ((f32[4,64,512]{2,1,0:T(8,128)}), f32[4,64,512]{2,1,0:T(8,128)S(1)}, u32[]{:S(2)}, u32[]{:S(2)}) async-start(f32[4,64,512]{2,1,0:T(8,128)} %shard_map.89), calls=%async_computation.3 | async-start | bytes 1048576 | tf_op jit(solution)/shard_map/all_to_all | solution.py:214
  120.6 8.6 %copy-start.7 = (f32[64,64]{1,0:T(8,128)}, f32[64,64]{1,0:T(8,128)S(1)}, u32[]{:S(2)}) copy-start(f32[64,64]{1,0:T(8,128)S(1)} %convolution_add_fusion.1) | copy-start | bytes 49156

commit v9 on v8

--- a/solution.py
+++ b/solution.py
@@ -17,11 +17,6 @@
 
 def dot_t(a, b, **kw):
     return lax.dot_general(a, b, (((1,), (1,)), ((), ())), preferred_element_type=F32, **kw)
-
-
-def passed(v, axis, by):
-    n = lax.axis_size(axis)
-    return lax.ppermute(v, axis, [(i, (i + by) % n) for i in range(n)])
 
 
 def spread(v, axis):
@@ -90,13 +85,8 @@
         out_ref[x, rows:] = jnp.where(odd == 1, both, 0.0).astype(BF16)
 
 
-def cross_kernel(order, iz_ref, exps_ref, s_ref, place_ref, term_ref, *refs):
-    block_refs, (out_ref, c_ref) = refs[:-2], refs[-2:]
+def cross_kernel(nz, iz_ref, exps_ref, c_ref, s_ref, place_ref, term_ref, out_ref):
     nx, _, rows, _ = s_ref.shape
-    nz = len(order)
-    for by, block_ref in zip(order, block_refs):
-        at = lax.rem(iz_ref[0] + by + nz, nz) * rows
-        c_ref[pl.ds(pl.multiple_of(at, rows), rows), :] = block_ref[...]
     all_rows, ns = c_ref.shape
     nf = place_ref.shape[2] // 2
     run = 2 * rows
@@ -155,13 +145,16 @@
     cols = nx * rows
     ix, iz = lax.axis_index("x"), lax.axis_index("z")
 
+    route = [(t * group + b, (t - 1) * group + b) for t in range(1, steps) for b in range(group)]
+    s_own, a_own = lax.ppermute((s_own, a_own), ("y", "c", "x", "z"), route)
     packed = pl.pallas_call(
         functools.partial(pack_kernel, cols),
         out_shape=jax.ShapeDtypeStruct((2, rows, ns + 2 * nf), BF16),
     )(s_own, a_own)
-    route = [(t * group + b, (t - 1) * group + b) for t in range(1, steps) for b in range(group)]
-    packed = lax.ppermute(packed, ("y", "c", "x", "z"), route)
-    succ = spread(packed, "x")
+    succ = jnp.zeros((nx,) + packed.shape, BF16)
+    for by in range(nx):
+        block = lax.ppermute(packed, "x", [((i + by) % nx, i) for i in range(nx)]) if by else packed
+        succ = lax.dynamic_update_index_in_dim(succ, block, (ix + by) % nx, 0)
     tails = succ[..., ns:]
     a_two = tails[..., :nf]
     exps = jnp.max(tails[:, 0, :, nf : nf + 2].astype(F32), axis=(0, 1))
@@ -175,20 +168,15 @@
         place_kernel,
         out_shape=jax.ShapeDtypeStruct((nx, 2 * rows, 2 * nf), BF16),
         in_specs=[in_smem, in_vmem],
-        cost_estimate=pl.CostEstimate(flops=10**11, bytes_accessed=1 << 20, transcendentals=0),
     )(iz.reshape(1), tails)
 
-    c_blocks = [c_own] + [passed(c_own, "z", -by) for by in (1, -1, 2, -2, 4)]
-    c_blocks += [passed(c_blocks[3], "z", -1), passed(c_blocks[4], "z", 1)]
-    sent, c_rows = pl.pallas_call(
-        functools.partial(cross_kernel, (0, 1, -1, 2, -2, 4, 3, -3)),
-        out_shape=(
-            jax.ShapeDtypeStruct((nz * rows, cols + 2 * nf), F32),
-            jax.ShapeDtypeStruct((nz * rows, ns), BF16),
-        ),
-        in_specs=[in_smem] * 2 + [in_vmem] * (3 + len(c_blocks)),
-        compiler_params=pltpu.CompilerParams(vmem_limit_bytes=16 << 20),
-    )(iz.reshape(1), exps, succ, place, term, *c_blocks)
+    c_rows = spread(c_own, "z").reshape(nz * rows, ns)
+    sent = pl.pallas_call(
+        functools.partial(cross_kernel, nz),
+        out_shape=jax.ShapeDtypeStruct((nz * rows, cols + 2 * nf), F32),
+        in_specs=[in_smem] * 2 + [in_vmem] * 4,
+        compiler_params=pltpu.CompilerParams(vmem_limit_bytes=12 << 20),
+    )(iz.reshape(1), exps, c_rows, succ, place, term)
     c_turned = pl.pallas_call(
         functools.partial(turn_kernel, nx, nz),
         out_shape=jax.ShapeDtypeStruct(c_rows.shape, BF16),

time: 130 us -> 129 us (level)
  the two profiles are of different devices: /device:TPU:8 before, /device:TPU:2 now
where the time goes in v9:
time: 129 us
  waiting for transfers between devices  48.3 us (37%)
  starting transfers between devices  33.4 us (26%)
  blocking collectives  17.6 us (14%)
  Pallas kernels  11.3 us (9%)
  local copies, waits for them, and re-layouts  10.9 us (8%)
  other arithmetic  5.02 us (4%)
    ppermute x3, waiting for transfers between devices, shards(): lax.ppermute(packed, 'x', [((i + by) % nx, i) for i in range(nx)])  22.4 us
    all_to_all x2, waiting for transfers between devices, spread(): lax.all_to_all(jnp.broadcast_to(v[None], (n,) + v.shape), axis, 0, 0, til...  19.1 us
    all_to_all x1, blocking collectives, shards(): sent = lax.all_to_all(sent, 'z', 0, 0, tiled=True)  17.6 us
    all_to_all x2, starting transfers between devices, spread(): lax.all_to_all(jnp.broadcast_to(v[None], (n,) + v.shape), axis, 0, 0, til...  15.1 us
    ppermute x3, starting transfers between devices, shards(): lax.ppermute(packed, 'x', [((i + by) % nx, i) for i in range(nx)])  10.6 us
    all_to_all x1, waiting for transfers between devices, shards(): diag = lax.all_to_all(diag, 'x', 0, 0, tiled=True)  6.81 us
    unnamed x24, local copies, waits for them, and re-layouts  5.94 us
    all_to_all x1, starting transfers between devices, shards(): diag = lax.all_to_all(diag, 'x', 0, 0, tiled=True)  4.9 us
  transfers between devices with their start and end apart: 8, of which 6 were waited for; matrix products, arithmetic and copies ran while one was open for 6% of the time, Pallas kernels for 6%

profile of v9, /device:TPU:2, one launch (start us, length us, event | category | flops | bytes accessed | tf_op | source)
XLA Modules:
  0.0 128.5 jit_solution(14037044409561060197)
XLA Ops:
  0.6 1.4 %collective-permute-start = (f32[64,2048]{1,0:T(8,128)}, f32[64,2048]{1,0:T(8,128)S(1)}, u32[]{:S(2)}, u32[]{:S(2)}) collective-permute-start(f32[64,2048]{1,0:T(8,128)} %bitcast.45), channel_id=1, source_target_pairs={{32,0},{33,1},{34,2},{35,3},{36,4},{37,5},{38,6},{39,7},{40,8},{41... | collective-permute-start | bytes 1572872 | tf_op jit(solution)/shard_map/ppermute | solution.py:149
  2.1 1.3 %collective-permute-start.1 = (f32[64,64]{1,0:T(8,128)}, f32[64,64]{1,0:T(8,128)S(1)}, u32[]{:S(2)}, u32[]{:S(2)}) collective-permute-start(f32[64,64]{1,0:T(8,128)} %bitcast.46), channel_id=1, source_target_pairs={{32,0},{33,1},{34,2},{35,3},{36,4},{37,5},{38,6},{39,7},{40,8},{41... | collective-permute-start | bytes 49160 | tf_op jit(solution)/shard_map/ppermute | solution.py:149
  3.4 2.5 %broadcast_in_dim.45 = bf16[8,64,2048]{2,1,0:T(8,128)(2,1)} broadcast(bf16[64,2048]{1,0:T(8,128)(2,1)} %bitcast.43), dimensions={1,2} | broadcast | bytes 2359296 | tf_op jit(solution)/shard_map/broadcast_in_dim | solution.py:24
  5.9 10.3 %all-to-all-start = ((bf16[8,64,2048]{2,1,0:T(8,128)(2,1)}), bf16[8,64,2048]{2,1,0:T(8,128)(2,1)S(1)}, u32[]{:S(2)}, u32[]{:S(2)}) async-start(bf16[8,64,2048]{2,1,0:T(8,128)(2,1)} %broadcast_in_dim.45), calls=%async_computation | async-start | bytes 4194304 | tf_op jit(solution)/shard_map/all_to_all | solution.py:24
  17.6 2.1 %shard_map.85 = bf16[2,64,2176]{2,1,0:T(8,128)(2,1)} custom-call(f32[64,2048]{1,0:T(8,128)} %copy-done.8, f32[64,64]{1,0:T(8,128)} %copy-done.10), custom_call_target="tpu_custom_call" | custom-call | tf_op jit(solution)/shard_map/pallas_call | solution.py:150
  19.7 2.6 %collective-permute-start.2 = (bf16[2,64,2176]{2,1,0:T(8,128)(2,1)}, bf16[2,64,2176]{2,1,0:T(8,128)(2,1)S(1)}, u32[]{:S(2)}, u32[]{:S(2)}) collective-permute-start(bf16[2,64,2176]{2,1,0:T(8,128)(2,1)} %shard_map.85), channel_id=1, source_target_pairs={{8,0},{16,8},{24,16},{0,24},{9,1},{17,9},{25,17},{1,25},{10,2},{18... | collective-permute-start | bytes 1671176 | tf_op jit(solution)/shard_map/ppermute | solution.py:156
  22.3 4.3 %collective-permute-start.3 = (bf16[2,64,2176]{2,1,0:T(8,128)(2,1)}, bf16[2,64,2176]{2,1,0:T(8,128)(2,1)S(1)}, u32[]{:S(2)}, u32[]{:S(2)}) collective-permute-start(bf16[2,64,2176]{2,1,0:T(8,128)(2,1)} %shard_map.85), channel_id=1, source_target_pairs={{16,0},{24,8},{0,16},{8,24},{17,1},{25,9},{1,17},{9,25},{18,2},{26... | collective-permute-start | bytes 1671176 | tf_op jit(solution)/shard_map/ppermute | solution.py:156
  26.6 3.7 %collective-permute-start.4 = (bf16[2,64,2176]{2,1,0:T(8,128)(2,1)}, bf16[2,64,2176]{2,1,0:T(8,128)(2,1)S(1)}, u32[]{:S(2)}, u32[]{:S(2)}) collective-permute-start(bf16[2,64,2176]{2,1,0:T(8,128)(2,1)} %shard_map.85), channel_id=1, source_target_pairs={{24,0},{0,8},{8,16},{16,24},{25,1},{1,9},{9,17},{17,25},{26,2},{2,... | collective-permute-start | bytes 1671176 | tf_op jit(solution)/shard_map/ppermute | solution.py:156
  30.7 6.3 %collective-permute-done.2 = bf16[2,64,2176]{2,1,0:T(8,128)(2,1)S(1)} collective-permute-done((bf16[2,64,2176]{2,1,0:T(8,128)(2,1)}, bf16[2,64,2176]{2,1,0:T(8,128)(2,1)S(1)}, u32[]{:S(2)}, u32[]{:S(2)}) %collective-permute-start.2) | collective-permute-done | bytes 557088 | tf_op jit(solution)/shard_map/ppermute | solution.py:156
  37.1 12.8 %collective-permute-done.3 = bf16[2,64,2176]{2,1,0:T(8,128)(2,1)S(1)} collective-permute-done((bf16[2,64,2176]{2,1,0:T(8,128)(2,1)}, bf16[2,64,2176]{2,1,0:T(8,128)(2,1)S(1)}, u32[]{:S(2)}, u32[]{:S(2)}) %collective-permute-start.3) | collective-permute-done | bytes 557088 | tf_op jit(solution)/shard_map/ppermute | solution.py:156
  50.0 3.2 %collective-permute-done.4 = bf16[2,64,2176]{2,1,0:T(8,128)(2,1)S(1)} collective-permute-done((bf16[2,64,2176]{2,1,0:T(8,128)(2,1)}, bf16[2,64,2176]{2,1,0:T(8,128)(2,1)S(1)}, u32[]{:S(2)}, u32[]{:S(2)}) %collective-permute-start.4) | collective-permute-done | bytes 557088 | tf_op jit(solution)/shard_map/ppermute | solution.py:156
  54.8 1.7 %shard_map.86.place_ref = bf16[4,128,128]{2,1,0:T(8,128)(2,1)} custom-call(s32[1]{0:T(128)} %bitcast.1.iz_ref, bf16[4,2,64,128]{3,2,1,0:T(8,128)(2,1)} %slice.42.tails_ref), custom_call_target="tpu_custom_call" | custom-call | tf_op jit(solution)/shard_map/pallas_call | solution.py:167
  57.9 11.0 %all-to-all-done = bf16[8,64,2048]{2,1,0:T(8,128)(2,1)S(1)} async-done(((bf16[8,64,2048]{2,1,0:T(8,128)(2,1)}), bf16[8,64,2048]{2,1,0:T(8,128)(2,1)S(1)}, u32[]{:S(2)}, u32[]{:S(2)}) %all-to-all-start) | async-done | bytes 2097184 | tf_op jit(solution)/shard_map/all_to_all | solution.py:24
  68.8 1.6 %copy-done.2 = bf16[4,2,64,2176]{3,2,1,0:T(8,128)(2,1)S(1)} copy-done((bf16[4,2,64,2176]{3,2,1,0:T(8,128)(2,1)S(1)}, bf16[4,2,64,2176]{3,2,1,0:T(8,128)(2,1)}, u32[]{:S(2)}) %copy-start.2) | copy-done | bytes 2228248
  71.4 2.1 %shard_map.87 = f32[512,384]{1,0:T(8,128)S(1)} custom-call(s32[1]{0:T(128)} %bitcast.1.iz_ref, f32[4]{0:T(128)S(1)} %pad_maximum_fusion.exps_ref, bf16[512,2048]{1,0:T(8,128)(2,1)S(1)} %bitcast.36, bf16[4,2,64,2176]{3,2,1,0:T(8,128)(2,1)S(1)} %copy-done.2, bf16[4,128,128]{2,1,0:T(8,128)(2,1)S(1)} %copy-done.5, f32[512,256]{1,0:T(8,128)S(1)} %fusion.2.term_ref), custom_call_target="tpu_custom_call" | custom-call | tf_op jit(solution)/shard_map/pallas_call | solution.py:174
  73.6 17.6 %all_to_all.20 = f16[8,64,384]{2,1,0:T(8,128)(2,1)S(1)} all-to-all(f16[8,64,384]{2,1,0:T(8,128)(2,1)S(1)} %bitcast.40), channel_id=1, replica_groups=mesh['y'=8,'c'=2,'x'=4,'z'=8] {'z'}, dimensions={0} | all-to-all | bytes 786432 | tf_op jit(solution)/shard_map/all_to_all | solution.py:188
  92.4 4.8 %all-to-all-start.2 = ((f16[4,8,64,256]{3,2,1,0:T(8,128)(2,1)}), f16[4,8,64,256]{3,2,1,0:T(8,128)(2,1)}, u32[]{:S(2)}, u32[]{:S(2)}) async-start(f16[4,8,64,256]{3,2,1,0:T(8,128)(2,1)} %broadcast_in_dim.46), calls=%async_computation.2 | async-start | bytes 2097152 | tf_op jit(solution)/shard_map/all_to_all | solution.py:24
  98.4 1.3 %copy-done.3 = bf16[512,2048]{1,0:T(8,128)(2,1)} copy-done((bf16[512,2048]{1,0:T(8,128)(2,1)}, bf16[512,2048]{1,0:T(8,128)(2,1)S(1)}, u32[]{:S(2)}) %copy-start.3) | copy-done | bytes 2097176
  100.9 2.2 %shard_map.90 = f32[64,2048]{1,0:T(8,128)} custom-call(f32[8,64,256]{2,1,0:T(8,128)} %convert_multiply_fusion.1.in_ref), custom_call_target="tpu_custom_call" | custom-call | tf_op jit(solution)/shard_map/pallas_call | solution.py:204
  103.2 8.2 %all-to-all-done.2 = f16[4,8,64,256]{3,2,1,0:T(8,128)(2,1)} async-done(((f16[4,8,64,256]{3,2,1,0:T(8,128)(2,1)}), f16[4,8,64,256]{3,2,1,0:T(8,128)(2,1)}, u32[]{:S(2)}, u32[]{:S(2)}) %all-to-all-start.2) | async-done | bytes 1048608 | tf_op jit(solution)/shard_map/all_to_all | solution.py:24
  111.3 1.7 %fusion = (bf16[4,8,64,256]{3,2,1,0:T(8,128)(2,1)S(1)}, bf16[4,8,64,256]{3,2,1,0:T(8,128)(2,1)S(1)}) fusion(f16[4,8,64,256]{3,2,1,0:T(8,128)(2,1)} %all-to-all-done.2, f32[8]{0:T(128)S(1)} %get-tuple-element.3), kind=kLoop, calls=%fused_computation.3 | loop fusion | flops 3145728 | bytes 3145760 | tf_op jit(solution)/shard_map/convert_element_type | solution.py:195
  113.1 2.1 %shard_map.89 = f32[4,64,512]{2,1,0:T(8,128)} custom-call(bf16[4,8,64,256]{3,2,1,0:T(8,128)(2,1)S(1)} %get-tuple-element.6.top_ref, bf16[4,8,64,256]{3,2,1,0:T(8,128)(2,1)S(1)} %get-tuple-element.5.low_ref, bf16[512,2048]{1,0:T(8,128)(2,1)S(1)} %copy-done.4), custom_call_target="tpu_custom_call" | custom-call | tf_op jit(solution)/shard_map/pallas_call | solution.py:196
  115.2 4.9 %all-to-all-start.3 = ((f32[4,64,512]{2,1,0:T(8,128)}), f32[4,64,512]{2,1,0:T(8,128)S(1)}, u32[]{:S(2)}, u32[]{:S(2)}) async-start(f32[4,64,512]{2,1,0:T(8,128)} %shard_map.89), calls=%async_computation.3 | async-start | bytes 1048576 | tf_op jit(solution)/shard_map/all_to_all | solution.py:202
  120.8 6.8 %all-to-all-done.3 = f32[4,64,512]{2,1,0:T(8,128)S(1)} async-done(((f32[4,64,512]{2,1,0:T(8,128)}), f32[4,64,512]{2,1,0:T(8,128)S(1)}, u32[]{:S(2)}, u32[]{:S(2)}) %all-to-all-start.3) | async-done | bytes 524320 | tf_op jit(solution)/shard_map/all_to_all | solution.py:202
  (48 shorter events, 11.0 us)
Async XLA Ops:
  0.6 56.8 %copy-start = (f32[1,2048,64]{1,2,0:T(8,128)S(1)}, f32[1,2048,64]{1,2,0:T(8,128)}, u32[]{:S(2)}) copy-start(f32[1,2048,64]{1,2,0:T(8,128)} %param.7) | copy-start | bytes 1572868
  0.6 15.6 %collective-permute-start = (f32[64,2048]{1,0:T(8,128)}, f32[64,2048]{1,0:T(8,128)S(1)}, u32[]{:S(2)}, u32[]{:S(2)}) collective-permute-start(f32[64,2048]{1,0:T(8,128)} %bitcast.45), channel_id=1, source_target_pairs={{32,0},{33,1},{34,2},{35,3},{36,4},{37,5},{38,6},{39,7},{40,8},{41... | collective-permute-start | bytes 1572872 | tf_op jit(solution)/shard_map/ppermute | solution.py:149
  2.1 14.1 %collective-permute-start.1 = (f32[64,64]{1,0:T(8,128)}, f32[64,64]{1,0:T(8,128)S(1)}, u32[]{:S(2)}, u32[]{:S(2)}) collective-permute-start(f32[64,64]{1,0:T(8,128)} %bitcast.46), channel_id=1, source_target_pairs={{32,0},{33,1},{34,2},{35,3},{36,4},{37,5},{38,6},{39,7},{40,8},{41... | collective-permute-start | bytes 49160 | tf_op jit(solution)/shard_map/ppermute | solution.py:149
  5.9 63.0 %all-to-all-start = ((bf16[8,64,2048]{2,1,0:T(8,128)(2,1)}), bf16[8,64,2048]{2,1,0:T(8,128)(2,1)S(1)}, u32[]{:S(2)}, u32[]{:S(2)}) async-start(bf16[8,64,2048]{2,1,0:T(8,128)(2,1)} %broadcast_in_dim.45), calls=%async_computation | async-start | bytes 4194304 | tf_op jit(solution)/shard_map/all_to_all | solution.py:24
  16.2 0.6 copy-start.10
  16.8 0.8 copy-start.8
  19.7 10.9 %copy-start.6 = (bf16[2,64,2176]{2,1,0:T(8,128)(2,1)S(1)}, bf16[2,64,2176]{2,1,0:T(8,128)(2,1)}, u32[]{:S(2)}) copy-start(bf16[2,64,2176]{2,1,0:T(8,128)(2,1)} %shard_map.85) | copy-start | bytes 1671172
  19.7 17.3 %collective-permute-start.2 = (bf16[2,64,2176]{2,1,0:T(8,128)(2,1)}, bf16[2,64,2176]{2,1,0:T(8,128)(2,1)S(1)}, u32[]{:S(2)}, u32[]{:S(2)}) collective-permute-start(bf16[2,64,2176]{2,1,0:T(8,128)(2,1)} %shard_map.85), channel_id=1, source_target_pairs={{8,0},{16,8},{24,16},{0,24},{9,1},{17,9},{25,17},{1,25},{10,2},{18... | collective-permute-start | bytes 1671176 | tf_op jit(solution)/shard_map/ppermute | solution.py:156
  22.3 27.6 %collective-permute-start.3 = (bf16[2,64,2176]{2,1,0:T(8,128)(2,1)}, bf16[2,64,2176]{2,1,0:T(8,128)(2,1)S(1)}, u32[]{:S(2)}, u32[]{:S(2)}) collective-permute-start(bf16[2,64,2176]{2,1,0:T(8,128)(2,1)} %shard_map.85), channel_id=1, source_target_pairs={{16,0},{24,8},{0,16},{8,24},{17,1},{25,9},{1,17},{9,25},{18,2},{26... | collective-permute-start | bytes 1671176 | tf_op jit(solution)/shard_map/ppermute | solution.py:156
  26.6 26.6 %collective-permute-start.4 = (bf16[2,64,2176]{2,1,0:T(8,128)(2,1)}, bf16[2,64,2176]{2,1,0:T(8,128)(2,1)S(1)}, u32[]{:S(2)}, u32[]{:S(2)}) collective-permute-start(bf16[2,64,2176]{2,1,0:T(8,128)(2,1)} %shard_map.85), channel_id=1, source_target_pairs={{24,0},{0,8},{8,16},{16,24},{25,1},{1,9},{9,17},{17,25},{26,2},{2,... | collective-permute-start | bytes 1671176 | tf_op jit(solution)/shard_map/ppermute | solution.py:156
  53.3 1.4 %copy-start.1 = (bf16[4,2,64,2176]{3,2,1,0:T(8,128)(2,1)}, bf16[4,2,64,2176]{3,2,1,0:T(8,128)(2,1)S(1)}, u32[]{:S(2)}) copy-start(bf16[4,2,64,2176]{3,2,1,0:T(8,128)(2,1)S(1)} %bitcast_dynamic-update-slice_fusion.s_ref) | copy-start | bytes 6684676
  68.8 1.6 %copy-start.2 = (bf16[4,2,64,2176]{3,2,1,0:T(8,128)(2,1)S(1)}, bf16[4,2,64,2176]{3,2,1,0:T(8,128)(2,1)}, u32[]{:S(2)}) copy-start(bf16[4,2,64,2176]{3,2,1,0:T(8,128)(2,1)} %copy-done.1) | copy-start | bytes 6684676
  70.5 0.9 copy-start.5
  92.4 18.9 %all-to-all-start.2 = ((f16[4,8,64,256]{3,2,1,0:T(8,128)(2,1)}), f16[4,8,64,256]{3,2,1,0:T(8,128)(2,1)}, u32[]{:S(2)}, u32[]{:S(2)}) async-start(f16[4,8,64,256]{3,2,1,0:T(8,128)(2,1)} %broadcast_in_dim.46), calls=%async_computation.2 | async-start | bytes 2097152 | tf_op jit(solution)/shard_map/all_to_all | solution.py:24
  98.3 1.3 %copy-start.3 = (bf16[512,2048]{1,0:T(8,128)(2,1)}, bf16[512,2048]{1,0:T(8,128)(2,1)S(1)}, u32[]{:S(2)}) copy-start(bf16[512,2048]{1,0:T(8,128)(2,1)S(1)} %shard_map.88.c_ref) | copy-start | bytes 6291460
  100.9 12.2 %copy-start.4 = (bf16[512,2048]{1,0:T(8,128)(2,1)S(1)}, bf16[512,2048]{1,0:T(8,128)(2,1)}, u32[]{:S(2)}) copy-start(bf16[512,2048]{1,0:T(8,128)(2,1)} %copy-done.3) | copy-start | bytes 6291460
  113.1 7.0 %copy-start.11 = (f32[64,64]{1,0:T(8,128)S(1)}, f32[64,64]{1,0:T(8,128)}, u32[]{:S(2)}) copy-start(f32[64,64]{1,0:T(8,128)} %param.11) | copy-start | bytes 49156
  113.1 7.3 %copy-start.7 = (f32[1,64,2048]{2,1,0:T(8,128)S(1)}, f32[1,64,2048]{2,1,0:T(8,128)}, u32[]{:S(2)}) copy-start(f32[1,64,2048]{2,1,0:T(8,128)} %param.8) | copy-start | bytes 1572868
  115.2 12.4 %all-to-all-start.3 = ((f32[4,64,512]{2,1,0:T(8,128)}), f32[4,64,512]{2,1,0:T(8,128)S(1)}, u32[]{:S(2)}, u32[]{:S(2)}) async-start(f32[4,64,512]{2,1,0:T(8,128)} %shard_map.89), calls=%async_computation.3 | async-start | bytes 1048576 | tf_op jit(solution)/shard_map/all_to_all | solution.py:202
  120.4 8.1 %copy-start.9 = (f32[64,64]{1,0:T(8,128)}, f32[64,64]{1,0:T(8,128)S(1)}, u32[]{:S(2)}) copy-start(f32[64,64]{1,0:T(8,128)S(1)} %convolution_add_fusion.1) | copy-start | bytes 49156

commit v10 on v9

--- a/solution.py
+++ b/solution.py
@@ -31,7 +31,7 @@
     return low, high
 
 
-def pack_kernel(cols, s_ref, a_ref, packed_ref):
+def pack_kernel(s_ref, a_ref, packed_ref):
     rows, ns = s_ref.shape
     nf = a_ref.shape[1]
 
@@ -49,8 +49,7 @@
     a_own = a_ref[...]
     bound_a = jnp.max(jnp.abs(a_own), axis=1, keepdims=True)
     bound = 0.125 * jnp.sum(total, axis=1, keepdims=True) + 0.75 * nf * bound_a
-    lane = lax.broadcasted_iota(jnp.int32, (rows, nf), 1)
-    exps = jnp.where(lane == 0, exponent(bound), exponent(0.125 * cols * bound_a)) + 2
+    exps = jnp.broadcast_to(exponent(bound) + 2, a_own.shape)
     put(ns, jnp.concatenate([a_own, exps], axis=1))
 
 
@@ -85,7 +84,7 @@
         out_ref[x, rows:] = jnp.where(odd == 1, both, 0.0).astype(BF16)
 
 
-def cross_kernel(nz, iz_ref, exps_ref, c_ref, s_ref, place_ref, term_ref, out_ref):
+def cross_kernel(nz, iz_ref, exps_ref, c_ref, s_ref, place_ref, term_ref, out_ref, share_ref):
     nx, _, rows, _ = s_ref.shape
     all_rows, ns = c_ref.shape
     nf = place_ref.shape[2] // 2
@@ -99,15 +98,14 @@
         second = second + pltpu.roll(second, rows, 1)
         cross = jnp.where(lane < rows, first, second)
         at = slice(q * run, (q + 1) * run)
-        out_ref[:, at] = (cross + term_ref[:, at]) * exps_ref[2]
+        out_ref[:, at] = (cross + term_ref[:, at]) * exps_ref[1]
     pair = iz_ref[0] // 2
     share = jnp.zeros((all_rows, 2 * nf), F32)
     for x in range(nx):
         at = pl.ds(pl.multiple_of(x * nz * rows + pair * run, run), run)
         share += jnp.dot(c_ref[:, at], place_ref[x], preferred_element_type=F32)
-    share = (share + pltpu.roll(share, nf, 1)) * exps_ref[3]
-    marks = jnp.where(lane == nf, exps_ref[0], exps_ref[1])
-    out_ref[:, nx * rows :] = jnp.where(lane < nf, share, marks)
+    share = share + pltpu.roll(share, nf, 1)
+    share_ref[...] = jnp.where(lane < nf, share, exps_ref[0])
 
 
 def diag_kernel(top_ref, low_ref, c_ref, out_ref, parts_ref):
@@ -148,7 +146,7 @@
     route = [(t * group + b, (t - 1) * group + b) for t in range(1, steps) for b in range(group)]
     s_own, a_own = lax.ppermute((s_own, a_own), ("y", "c", "x", "z"), route)
     packed = pl.pallas_call(
-        functools.partial(pack_kernel, cols),
+        pack_kernel,
         out_shape=jax.ShapeDtypeStruct((2, rows, ns + 2 * nf), BF16),
     )(s_own, a_own)
     succ = jnp.zeros((nx,) + packed.shape, BF16)
@@ -157,8 +155,8 @@
         succ = lax.dynamic_update_index_in_dim(succ, block, (ix + by) % nx, 0)
     tails = succ[..., ns:]
     a_two = tails[..., :nf]
-    exps = jnp.max(tails[:, 0, :, nf : nf + 2].astype(F32), axis=(0, 1))
-    exps = jnp.concatenate([exps, jnp.exp2(14 - exps)])
+    exp_own = jnp.max(tails[:, 0, :, nf].astype(F32))
+    exps = jnp.stack([exp_own, jnp.exp2(14 - exp_own)])
 
     link_rows = lax.dynamic_slice_in_dim(link, ix * nz * rows, nz * rows, 0)
     a_cols = a_two[:, 0].astype(F32) + a_two[:, 1].astype(F32)
@@ -171,9 +169,12 @@
     )(iz.reshape(1), tails)
 
     c_rows = spread(c_own, "z").reshape(nz * rows, ns)
-    sent = pl.pallas_call(
+    sent, share = pl.pallas_call(
         functools.partial(cross_kernel, nz),
-        out_shape=jax.ShapeDtypeStruct((nz * rows, cols + 2 * nf), F32),
+        out_shape=(
+            jax.ShapeDtypeStruct((nz * rows, cols), F32),
+            jax.ShapeDtypeStruct((nz * rows, 2 * nf), F32),
+        ),
         in_specs=[in_smem] * 2 + [in_vmem] * 4,
         compiler_params=pltpu.CompilerParams(vmem_limit_bytes=12 << 20),
     )(iz.reshape(1), exps, c_rows, succ, place, term)
@@ -183,14 +184,22 @@
         cost_estimate=pl.CostEstimate(flops=0, bytes_accessed=20 << 20, transcendentals=0),
         compiler_params=pltpu.CompilerParams(vmem_limit_bytes=8 << 20),
     )(c_rows)
-    sent = sent.reshape(nz, rows, cols + 2 * nf)
-    sent = sent.astype(F16)
-    sent = lax.all_to_all(sent, "z", 0, 0, tiled=True)
-    cross = sent[..., :cols]
-    marks = sent[:, :1, cols + nf : cols + nf + 2].astype(F32)
-    scale = jnp.exp2(marks[..., :1] - 14)
-
-    every = spread(cross, "x").astype(F32) * scale[None]
+    sent = sent.astype(F16).reshape(nz, rows, cols)
+    sent = jnp.broadcast_to(sent[None], (nx, nz, rows, cols)).reshape(group, rows, cols)
+    every = lax.all_to_all(sent, ("x", "z"), 0, 0, tiled=True).reshape(nx, nz, rows, cols)
+
+    share = share.reshape(nz, rows, 2 * nf)
+    arrow = jnp.zeros((rows, nf), F32)
+    exp_z = jnp.zeros((nz,), F32)
+    for by in range(nz):
+        part = lax.dynamic_index_in_dim(share, (iz + by) % nz, 0, keepdims=False)
+        part = lax.ppermute(part, "z", [(i, (i + by) % nz) for i in range(nz)]) if by else part
+        arrow = arrow + part[:, :nf]
+        exp_z = jnp.where(jnp.arange(nz) == (iz - by) % nz, part[0, nf], exp_z)
+    scale = jnp.exp2(exp_z - 14)[:, None, None]
+    cross = lax.dynamic_index_in_dim(every, ix, 0, keepdims=False)
+
+    every = every.astype(F32) * scale[None]
     every_top = lax.reduce_precision(every, 8, 7)
     every_low = (every - every_top).astype(BF16)
     diag = pl.pallas_call(
@@ -205,10 +214,8 @@
         functools.partial(natural_kernel, nx, nz),
         out_shape=jax.ShapeDtypeStruct((rows, ns), F32),
     )(cross.astype(F32) * scale)
-    share = sent[..., cols : cols + nf].astype(F32) * jnp.exp2(marks[..., 1:] - 14)
     link_own = lax.dynamic_slice_in_dim(link, (ix * nz + iz) * rows, rows, 0)
-    arrow = jnp.dot(link_own, fixed_cov, precision=lax.Precision.HIGHEST)
-    arrow = jnp.sum(share, axis=0) + arrow
+    arrow = arrow + jnp.dot(link_own, fixed_cov, precision=lax.Precision.HIGHEST)
     local = lax.optimization_barrier(local + dot_t(arrow, link, precision=HIGH))
     diag_rows = local + diag.transpose(1, 0, 2).reshape(rows, ns)
     return (diag_rows[None], cross_rows[None], arrow[None])

time: 129 us -> 146 us (1.13)
  the two profiles are of different devices: /device:TPU:2 before, /device:TPU:56 now
where the time goes in v10:
time: 146 us; the launch traced here: 144 us
  starting transfers between devices  62.5 us (43%)
  waiting for transfers between devices  39.2 us (27%)
  local copies, waits for them, and re-layouts  15.7 us (11%)
  Pallas kernels  11.1 us (8%)
  other arithmetic  11.1 us (8%)
  between operations  2.62 us (2%)
    ppermute x7, starting transfers between devices, shards(): lax.ppermute(part, 'z', [(i, (i + by) % nz) for i in range(nz)])  28.4 us
    ppermute x3, waiting for transfers between devices, shards(): lax.ppermute(packed, 'x', [((i + by) % nx, i) for i in range(nx)])  23.2 us
    all_to_all x1, starting transfers between devices, spread(): lax.all_to_all(jnp.broadcast_to(v[None], (n,) + v.shape), axis, 0, 0, til...  10.4 us
    ppermute x3, starting transfers between devices, shards(): lax.ppermute(packed, 'x', [((i + by) % nx, i) for i in range(nx)])  10.3 us
    ppermute x7, waiting for transfers between devices, shards(): lax.ppermute(part, 'z', [(i, (i + by) % nz) for i in range(nz)])  7.64 us
    unnamed x26, local copies, waits for them, and re-layouts  6.01 us
    ppermute x2, starting transfers between devices, shards(): s_own, a_own = lax.ppermute((s_own, a_own), ('y', 'c', 'x', 'z'), route)  5.13 us
    exp2 x1, other arithmetic, shards(): scale = jnp.exp2(exp_z - 14)[:, None, None]  4.98 us
  transfers between devices with their start and end apart: 15, of which 6 were waited for; matrix products, arithmetic and copies ran while one was open for 13% of the time, Pallas kernels for 5%

profile of v10, /device:TPU:56, one launch (start us, length us, event | category | flops | bytes accessed | tf_op | source)
XLA Modules:
  0.0 143.5 jit_solution(1917584038877542183)
XLA Ops:
  0.6 2.8 %collective-permute-start = (f32[64,2048]{1,0:T(8,128)}, f32[64,2048]{1,0:T(8,128)S(1)}, u32[]{:S(2)}, u32[]{:S(2)}) collective-permute-start(f32[64,2048]{1,0:T(8,128)} %bitcast.81), channel_id=1, source_target_pairs={{32,0},{33,1},{34,2},{35,3},{36,4},{37,5},{38,6},{39,7},{40,8},{41... | collective-permute-start | bytes 1572872 | tf_op jit(solution)/shard_map/ppermute | solution.py:147
  3.5 2.5 %broadcast_in_dim.71 = bf16[8,64,2048]{2,1,0:T(8,128)(2,1)} broadcast(bf16[64,2048]{1,0:T(8,128)(2,1)} %bitcast.79), dimensions={1,2} | broadcast | bytes 2359296 | tf_op jit(solution)/shard_map/broadcast_in_dim | solution.py:24
  6.0 10.4 %all-to-all-start = ((bf16[8,64,2048]{2,1,0:T(8,128)(2,1)}), bf16[8,64,2048]{2,1,0:T(8,128)(2,1)S(1)}, u32[]{:S(2)}, u32[]{:S(2)}) async-start(bf16[8,64,2048]{2,1,0:T(8,128)(2,1)} %broadcast_in_dim.71), calls=%async_computation | async-start | bytes 4194304 | tf_op jit(solution)/shard_map/all_to_all | solution.py:24
  16.5 2.3 %collective-permute-start.1 = (f32[64,64]{1,0:T(8,128)S(1)}, f32[64,64]{1,0:T(8,128)S(1)}, u32[]{:S(2)}, u32[]{:S(2)}) collective-permute-start(f32[64,64]{1,0:T(8,128)S(1)} %bitcast.82), channel_id=1, source_target_pairs={{32,0},{33,1},{34,2},{35,3},{36,4},{37,5},{38,6},{39,7},{40,8},{41... | collective-permute-start | bytes 49160 | tf_op jit(solution)/shard_map/ppermute | solution.py:147
  23.8 4.8 %collective-permute-start.2 = (bf16[2,64,2176]{2,1,0:T(8,128)(2,1)}, bf16[2,64,2176]{2,1,0:T(8,128)(2,1)S(1)}, u32[]{:S(2)}, u32[]{:S(2)}) collective-permute-start(bf16[2,64,2176]{2,1,0:T(8,128)(2,1)} %shard_map.85), channel_id=1, source_target_pairs={{8,0},{16,8},{24,16},{0,24},{9,1},{17,9},{25,17},{1,25},{10,2},{18... | collective-permute-start | bytes 1671176 | tf_op jit(solution)/shard_map/ppermute | solution.py:154
  28.6 2.7 %collective-permute-start.3 = (bf16[2,64,2176]{2,1,0:T(8,128)(2,1)}, bf16[2,64,2176]{2,1,0:T(8,128)(2,1)S(1)}, u32[]{:S(2)}, u32[]{:S(2)}) collective-permute-start(bf16[2,64,2176]{2,1,0:T(8,128)(2,1)} %shard_map.85), channel_id=1, source_target_pairs={{16,0},{24,8},{0,16},{8,24},{17,1},{25,9},{1,17},{9,25},{18,2},{26... | collective-permute-start | bytes 1671176 | tf_op jit(solution)/shard_map/ppermute | solution.py:154
  31.3 2.8 %collective-permute-start.4 = (bf16[2,64,2176]{2,1,0:T(8,128)(2,1)}, bf16[2,64,2176]{2,1,0:T(8,128)(2,1)S(1)}, u32[]{:S(2)}, u32[]{:S(2)}) collective-permute-start(bf16[2,64,2176]{2,1,0:T(8,128)(2,1)} %shard_map.85), channel_id=1, source_target_pairs={{24,0},{0,8},{8,16},{16,24},{25,1},{1,9},{9,17},{17,25},{26,2},{2,... | collective-permute-start | bytes 1671176 | tf_op jit(solution)/shard_map/ppermute | solution.py:154
  34.5 17.8 %collective-permute-done.2 = bf16[2,64,2176]{2,1,0:T(8,128)(2,1)S(1)} collective-permute-done((bf16[2,64,2176]{2,1,0:T(8,128)(2,1)}, bf16[2,64,2176]{2,1,0:T(8,128)(2,1)S(1)}, u32[]{:S(2)}, u32[]{:S(2)}) %collective-permute-start.2) | collective-permute-done | bytes 557088 | tf_op jit(solution)/shard_map/ppermute | solution.py:154
  52.4 5.3 %collective-permute-done.4 = bf16[2,64,2176]{2,1,0:T(8,128)(2,1)S(1)} collective-permute-done((bf16[2,64,2176]{2,1,0:T(8,128)(2,1)}, bf16[2,64,2176]{2,1,0:T(8,128)(2,1)S(1)}, u32[]{:S(2)}, u32[]{:S(2)}) %collective-permute-start.4) | collective-permute-done | bytes 557088 | tf_op jit(solution)/shard_map/ppermute | solution.py:154
  64.4 3.2 %all-to-all-done = bf16[8,64,2048]{2,1,0:T(8,128)(2,1)S(1)} async-done(((bf16[8,64,2048]{2,1,0:T(8,128)(2,1)}), bf16[8,64,2048]{2,1,0:T(8,128)(2,1)S(1)}, u32[]{:S(2)}, u32[]{:S(2)}) %all-to-all-start) | async-done | bytes 2097184 | tf_op jit(solution)/shard_map/all_to_all | solution.py:24
  70.1 2.1 %shard_map.87 = (f32[512,256]{1,0:T(8,128)S(1)}, f32[512,128]{1,0:T(8,128)S(1)}) custom-call(s32[1]{0:T(128)} %bitcast.1.iz_ref, f32[2]{0:T(128)S(1)} %pad_maximum_fusion.exps_ref, bf16[512,2048]{1,0:T(8,128)(2,1)S(1)} %bitcast.70, bf16[4,2,64,2176]{3,2,1,0:T(8,128)(2,1)S(1)} %copy-done.2, bf16[4,128,128]{2,1,0:T(8,128)(2,1)S(1)} %copy-done.5, ...), custom_call_target="tpu_custom_call" | custom-call | tf_op jit(solution)/shard_map/pallas_call | solution.py:172
  73.4 4.8 %all-to-all-start.1 = ((f16[32,64,256]{2,1,0:T(8,128)(2,1)}), f16[32,64,256]{2,1,0:T(8,128)(2,1)}, u32[]{:S(2)}, u32[]{:S(2)}) async-start(f16[32,64,256]{2,1,0:T(8,128)(2,1)} %bitcast.73), calls=%async_computation.1 | async-start | bytes 2097152 | tf_op jit(solution)/shard_map/all_to_all | solution.py:189
  78.4 4.8 %collective-permute-start.11 = (f32[64,128]{1,0:T(8,128)S(1)}, f32[64,128]{1,0:T(8,128)S(1)}, u32[]{:S(2)}, u32[]{:S(2)}) collective-permute-start(f32[64,128]{1,0:T(8,128)S(1)} %get-tuple-element.10), channel_id=1, source_target_pairs={{0,7},{1,0},{2,1},{3,2},{4,3},{5,4},{6,5},{7,6},{8,15},{9,8},{10,9... | collective-permute-start | bytes 98312 | tf_op jit(solution)/shard_map/ppermute | solution.py:196
  83.2 4.3 %collective-permute-start.10 = (f32[64,128]{1,0:T(8,128)S(1)}, f32[64,128]{1,0:T(8,128)S(1)}, u32[]{:S(2)}, u32[]{:S(2)}) collective-permute-start(f32[64,128]{1,0:T(8,128)S(1)} %get-tuple-element.11), channel_id=1, source_target_pairs={{0,6},{1,7},{2,0},{3,1},{4,2},{5,3},{6,4},{7,5},{8,14},{9,15},{10,... | collective-permute-start | bytes 98312 | tf_op jit(solution)/shard_map/ppermute | solution.py:196
  87.5 3.4 %collective-permute-start.9 = (f32[64,128]{1,0:T(8,128)S(1)}, f32[64,128]{1,0:T(8,128)S(1)}, u32[]{:S(2)}, u32[]{:S(2)}) collective-permute-start(f32[64,128]{1,0:T(8,128)S(1)} %get-tuple-element.12), channel_id=1, source_target_pairs={{0,5},{1,6},{2,7},{3,0},{4,1},{5,2},{6,3},{7,4},{8,13},{9,14},{10,... | collective-permute-start | bytes 98312 | tf_op jit(solution)/shard_map/ppermute | solution.py:196
  90.9 5.5 %collective-permute-start.8 = (f32[64,128]{1,0:T(8,128)S(1)}, f32[64,128]{1,0:T(8,128)S(1)}, u32[]{:S(2)}, u32[]{:S(2)}) collective-permute-start(f32[64,128]{1,0:T(8,128)S(1)} %get-tuple-element.13), channel_id=1, source_target_pairs={{0,4},{1,5},{2,6},{3,7},{4,0},{5,1},{6,2},{7,3},{8,12},{9,13},{10,... | collective-permute-start | bytes 98312 | tf_op jit(solution)/shard_map/ppermute | solution.py:196
  96.4 2.2 %collective-permute-start.7 = (f32[64,128]{1,0:T(8,128)S(1)}, f32[64,128]{1,0:T(8,128)S(1)}, u32[]{:S(2)}, u32[]{:S(2)}) collective-permute-start(f32[64,128]{1,0:T(8,128)S(1)} %get-tuple-element.14), channel_id=1, source_target_pairs={{0,3},{1,4},{2,5},{3,6},{4,7},{5,0},{6,1},{7,2},{8,11},{9,12},{10,... | collective-permute-start | bytes 98312 | tf_op jit(solution)/shard_map/ppermute | solution.py:196
  98.6 7.6 %collective-permute-done.11 = f32[64,128]{1,0:T(8,128)S(1)} collective-permute-done((f32[64,128]{1,0:T(8,128)S(1)}, f32[64,128]{1,0:T(8,128)S(1)}, u32[]{:S(2)}, u32[]{:S(2)}) %collective-permute-start.11) | collective-permute-done | bytes 32800 | tf_op jit(solution)/shard_map/ppermute | solution.py:196
  106.2 2.6 %collective-permute-start.6 = (f32[64,128]{1,0:T(8,128)S(1)}, f32[64,128]{1,0:T(8,128)S(1)}, u32[]{:S(2)}, u32[]{:S(2)}) collective-permute-start(f32[64,128]{1,0:T(8,128)S(1)} %get-tuple-element.15), channel_id=1, source_target_pairs={{0,2},{1,3},{2,4},{3,5},{4,6},{5,7},{6,0},{7,1},{8,10},{9,11},{10,... | collective-permute-start | bytes 98312 | tf_op jit(solution)/shard_map/ppermute | solution.py:196
  108.8 5.7 %collective-permute-start.5 = (f32[64,128]{1,0:T(8,128)S(1)}, f32[64,128]{1,0:T(8,128)S(1)}, u32[]{:S(2)}, u32[]{:S(2)}) collective-permute-start(f32[64,128]{1,0:T(8,128)S(1)} %get-tuple-element.16), channel_id=1, source_target_pairs={{0,1},{1,2},{2,3},{3,4},{4,5},{5,6},{6,7},{7,0},{8,9},{9,10},{10,1... | collective-permute-start | bytes 98312 | tf_op jit(solution)/shard_map/ppermute | solution.py:196
  121.9 5.0 %multiply_exponential_fusion = f32[8]{0:T(128)S(1)} fusion(f32[]{:T(128)} %bitcast.35, s32[]{:T(128)S(6)} %select_n.227, f32[]{:T(128)} %bitcast.34, s32[]{:T(128)S(6)} %select_n.250, f32[]{:T(128)} %bitcast.33, s32[]{:T(128)S(6)} %select_n.249, f32[]{:T(128)} %bitcast.32, s32[]{:T(128)S(6)} %select_n.248, f32[]{:T(128)} %bitcast.31, s32[]{:T(128)S(6)} %select_n.247, ...), kind=kLoop, calls=%fused_computation.48 | loop fusion | flops 144 | bytes 96 | tf_op jit(solution)/shard_map/exp2 | solution.py:199
  129.0 2.1 %shard_map.89 = f32[4,64,512]{2,1,0:T(8,128)} custom-call(bf16[4,8,64,256]{3,2,1,0:T(8,128)(2,1)S(1)} %get-tuple-element.8.top_ref, bf16[4,8,64,256]{3,2,1,0:T(8,128)(2,1)S(1)} %get-tuple-element.7.low_ref, bf16[512,2048]{1,0:T(8,128)(2,1)S(1)} %copy-done.4), custom_call_target="tpu_custom_call" | custom-call | tf_op jit(solution)/shard_map/pallas_call | solution.py:205
  131.1 3.5 %all-to-all-start.2 = ((f32[4,64,512]{2,1,0:T(8,128)}), f32[4,64,512]{2,1,0:T(8,128)S(1)}, u32[]{:S(2)}, u32[]{:S(2)}) async-start(f32[4,64,512]{2,1,0:T(8,128)} %shard_map.89), calls=%async_computation.2 | async-start | bytes 1048576 | tf_op jit(solution)/shard_map/all_to_all | solution.py:211
  138.9 3.7 %all-to-all-done.2 = f32[4,64,512]{2,1,0:T(8,128)S(1)} async-done(((f32[4,64,512]{2,1,0:T(8,128)}), f32[4,64,512]{2,1,0:T(8,128)S(1)}, u32[]{:S(2)}, u32[]{:S(2)}) %all-to-all-start.2) | async-done | bytes 524320 | tf_op jit(solution)/shard_map/all_to_all | solution.py:211
  (67 shorter events, 28.9 us)
Async XLA Ops:
  0.6 63.3 %copy-start = (f32[1,2048,64]{1,2,0:T(8,128)S(1)}, f32[1,2048,64]{1,2,0:T(8,128)}, u32[]{:S(2)}) copy-start(f32[1,2048,64]{1,2,0:T(8,128)} %param.7) | copy-start | bytes 1572868
  0.6 19.7 %collective-permute-start = (f32[64,2048]{1,0:T(8,128)}, f32[64,2048]{1,0:T(8,128)S(1)}, u32[]{:S(2)}, u32[]{:S(2)}) collective-permute-start(f32[64,2048]{1,0:T(8,128)} %bitcast.81), channel_id=1, source_target_pairs={{32,0},{33,1},{34,2},{35,3},{36,4},{37,5},{38,6},{39,7},{40,8},{41... | collective-permute-start | bytes 1572872 | tf_op jit(solution)/shard_map/ppermute | solution.py:147
  6.0 10.5 %copy-start.12 = (f32[1,64,64]{2,1,0:T(8,128)S(1)}, f32[1,64,64]{2,1,0:T(8,128)}, u32[]{:S(2)}) copy-start(f32[1,64,64]{2,1,0:T(8,128)} %param.10) | copy-start | bytes 49156
  6.0 61.6 %all-to-all-start = ((bf16[8,64,2048]{2,1,0:T(8,128)(2,1)}), bf16[8,64,2048]{2,1,0:T(8,128)(2,1)S(1)}, u32[]{:S(2)}, u32[]{:S(2)}) async-start(bf16[8,64,2048]{2,1,0:T(8,128)(2,1)} %broadcast_in_dim.71), calls=%async_computation | async-start | bytes 4194304 | tf_op jit(solution)/shard_map/all_to_all | solution.py:24
  16.5 3.9 %collective-permute-start.1 = (f32[64,64]{1,0:T(8,128)S(1)}, f32[64,64]{1,0:T(8,128)S(1)}, u32[]{:S(2)}, u32[]{:S(2)}) collective-permute-start(f32[64,64]{1,0:T(8,128)S(1)} %bitcast.82), channel_id=1, source_target_pairs={{32,0},{33,1},{34,2},{35,3},{36,4},{37,5},{38,6},{39,7},{40,8},{41... | collective-permute-start | bytes 49160 | tf_op jit(solution)/shard_map/ppermute | solution.py:147
  23.8 10.6 %copy-start.6 = (bf16[2,64,2176]{2,1,0:T(8,128)(2,1)S(1)}, bf16[2,64,2176]{2,1,0:T(8,128)(2,1)}, u32[]{:S(2)}) copy-start(bf16[2,64,2176]{2,1,0:T(8,128)(2,1)} %shard_map.85) | copy-start | bytes 1671172
  23.8 28.5 %collective-permute-start.2 = (bf16[2,64,2176]{2,1,0:T(8,128)(2,1)}, bf16[2,64,2176]{2,1,0:T(8,128)(2,1)S(1)}, u32[]{:S(2)}, u32[]{:S(2)}) collective-permute-start(bf16[2,64,2176]{2,1,0:T(8,128)(2,1)} %shard_map.85), channel_id=1, source_target_pairs={{8,0},{16,8},{24,16},{0,24},{9,1},{17,9},{25,17},{1,25},{10,2},{18... | collective-permute-start | bytes 1671176 | tf_op jit(solution)/shard_map/ppermute | solution.py:154
  28.6 23.8 %collective-permute-start.3 = (bf16[2,64,2176]{2,1,0:T(8,128)(2,1)}, bf16[2,64,2176]{2,1,0:T(8,128)(2,1)S(1)}, u32[]{:S(2)}, u32[]{:S(2)}) collective-permute-start(bf16[2,64,2176]{2,1,0:T(8,128)(2,1)} %shard_map.85), channel_id=1, source_target_pairs={{16,0},{24,8},{0,16},{8,24},{17,1},{25,9},{1,17},{9,25},{18,2},{26... | collective-permute-start | bytes 1671176 | tf_op jit(solution)/shard_map/ppermute | solution.py:154
  31.3 26.5 %collective-permute-start.4 = (bf16[2,64,2176]{2,1,0:T(8,128)(2,1)}, bf16[2,64,2176]{2,1,0:T(8,128)(2,1)S(1)}, u32[]{:S(2)}, u32[]{:S(2)}) collective-permute-start(bf16[2,64,2176]{2,1,0:T(8,128)(2,1)} %shard_map.85), channel_id=1, source_target_pairs={{24,0},{0,8},{8,16},{16,24},{25,1},{1,9},{9,17},{17,25},{26,2},{2,... | collective-permute-start | bytes 1671176 | tf_op jit(solution)/shard_map/ppermute | solution.py:154
  57.9 1.4 %copy-start.1 = (bf16[4,2,64,2176]{3,2,1,0:T(8,128)(2,1)}, bf16[4,2,64,2176]{3,2,1,0:T(8,128)(2,1)S(1)}, u32[]{:S(2)}) copy-start(bf16[4,2,64,2176]{3,2,1,0:T(8,128)(2,1)S(1)} %bitcast_dynamic-update-slice_fusion.s_ref) | copy-start | bytes 6684676
  67.6 1.6 %copy-start.2 = (bf16[4,2,64,2176]{3,2,1,0:T(8,128)(2,1)S(1)}, bf16[4,2,64,2176]{3,2,1,0:T(8,128)(2,1)}, u32[]{:S(2)}) copy-start(bf16[4,2,64,2176]{3,2,1,0:T(8,128)(2,1)} %copy-done.1) | copy-start | bytes 6684676
  73.4 53.8 %all-to-all-start.1 = ((f16[32,64,256]{2,1,0:T(8,128)(2,1)}), f16[32,64,256]{2,1,0:T(8,128)(2,1)}, u32[]{:S(2)}, u32[]{:S(2)}) async-start(f16[32,64,256]{2,1,0:T(8,128)(2,1)} %bitcast.73), calls=%async_computation.1 | async-start | bytes 2097152 | tf_op jit(solution)/shard_map/all_to_all | solution.py:189
  78.4 48.5 %copy-start.11 = (f32[64,64]{1,0:T(8,128)S(1)}, f32[64,64]{1,0:T(8,128)}, u32[]{:S(2)}) copy-start(f32[64,64]{1,0:T(8,128)} %param.11) | copy-start | bytes 49156
  78.4 27.8 %collective-permute-start.11 = (f32[64,128]{1,0:T(8,128)S(1)}, f32[64,128]{1,0:T(8,128)S(1)}, u32[]{:S(2)}, u32[]{:S(2)}) collective-permute-start(f32[64,128]{1,0:T(8,128)S(1)} %get-tuple-element.10), channel_id=1, source_target_pairs={{0,7},{1,0},{2,1},{3,2},{4,3},{5,4},{6,5},{7,6},{8,15},{9,8},{10,9... | collective-permute-start | bytes 98312 | tf_op jit(solution)/shard_map/ppermute | solution.py:196
  83.2 25.5 %collective-permute-start.10 = (f32[64,128]{1,0:T(8,128)S(1)}, f32[64,128]{1,0:T(8,128)S(1)}, u32[]{:S(2)}, u32[]{:S(2)}) collective-permute-start(f32[64,128]{1,0:T(8,128)S(1)} %get-tuple-element.11), channel_id=1, source_target_pairs={{0,6},{1,7},{2,0},{3,1},{4,2},{5,3},{6,4},{7,5},{8,14},{9,15},{10,... | collective-permute-start | bytes 98312 | tf_op jit(solution)/shard_map/ppermute | solution.py:196
  87.5 31.3 %collective-permute-start.9 = (f32[64,128]{1,0:T(8,128)S(1)}, f32[64,128]{1,0:T(8,128)S(1)}, u32[]{:S(2)}, u32[]{:S(2)}) collective-permute-start(f32[64,128]{1,0:T(8,128)S(1)} %get-tuple-element.12), channel_id=1, source_target_pairs={{0,5},{1,6},{2,7},{3,0},{4,1},{5,2},{6,3},{7,4},{8,13},{9,14},{10,... | collective-permute-start | bytes 98312 | tf_op jit(solution)/shard_map/ppermute | solution.py:196
  90.9 28.6 %collective-permute-start.8 = (f32[64,128]{1,0:T(8,128)S(1)}, f32[64,128]{1,0:T(8,128)S(1)}, u32[]{:S(2)}, u32[]{:S(2)}) collective-permute-start(f32[64,128]{1,0:T(8,128)S(1)} %get-tuple-element.13), channel_id=1, source_target_pairs={{0,4},{1,5},{2,6},{3,7},{4,0},{5,1},{6,2},{7,3},{8,12},{9,13},{10,... | collective-permute-start | bytes 98312 | tf_op jit(solution)/shard_map/ppermute | solution.py:196
  96.4 23.8 %collective-permute-start.7 = (f32[64,128]{1,0:T(8,128)S(1)}, f32[64,128]{1,0:T(8,128)S(1)}, u32[]{:S(2)}, u32[]{:S(2)}) collective-permute-start(f32[64,128]{1,0:T(8,128)S(1)} %get-tuple-element.14), channel_id=1, source_target_pairs={{0,3},{1,4},{2,5},{3,6},{4,7},{5,0},{6,1},{7,2},{8,11},{9,12},{10,... | collective-permute-start | bytes 98312 | tf_op jit(solution)/shard_map/ppermute | solution.py:196
  106.2 14.5 %collective-permute-start.6 = (f32[64,128]{1,0:T(8,128)S(1)}, f32[64,128]{1,0:T(8,128)S(1)}, u32[]{:S(2)}, u32[]{:S(2)}) collective-permute-start(f32[64,128]{1,0:T(8,128)S(1)} %get-tuple-element.15), channel_id=1, source_target_pairs={{0,2},{1,3},{2,4},{3,5},{4,6},{5,7},{6,0},{7,1},{8,10},{9,11},{10,... | collective-permute-start | bytes 98312 | tf_op jit(solution)/shard_map/ppermute | solution.py:196
  108.8 12.5 %collective-permute-start.5 = (f32[64,128]{1,0:T(8,128)S(1)}, f32[64,128]{1,0:T(8,128)S(1)}, u32[]{:S(2)}, u32[]{:S(2)}) collective-permute-start(f32[64,128]{1,0:T(8,128)S(1)} %get-tuple-element.16), channel_id=1, source_target_pairs={{0,1},{1,2},{2,3},{3,4},{4,5},{5,6},{6,7},{7,0},{8,9},{9,10},{10,1... | collective-permute-start | bytes 98312 | tf_op jit(solution)/shard_map/ppermute | solution.py:196
  117.1 11.9 %copy-start.4 = (bf16[512,2048]{1,0:T(8,128)(2,1)S(1)}, bf16[512,2048]{1,0:T(8,128)(2,1)}, u32[]{:S(2)}) copy-start(bf16[512,2048]{1,0:T(8,128)(2,1)} %copy-done.3) | copy-start | bytes 6291460
  127.2 7.4 %copy-start.9 = (f32[64,64]{1,0:T(8,128)}, f32[64,64]{1,0:T(8,128)S(1)}, u32[]{:S(2)}) copy-start(f32[64,64]{1,0:T(8,128)S(1)} %fusion.5) | copy-start | bytes 49156
  129.0 5.6 %copy-start.7 = (f32[1,64,2048]{2,1,0:T(8,128)S(1)}, f32[1,64,2048]{2,1,0:T(8,128)}, u32[]{:S(2)}) copy-start(f32[1,64,2048]{2,1,0:T(8,128)} %param.8) | copy-start | bytes 1572868
  131.1 11.5 %all-to-all-start.2 = ((f32[4,64,512]{2,1,0:T(8,128)}), f32[4,64,512]{2,1,0:T(8,128)S(1)}, u32[]{:S(2)}, u32[]{:S(2)}) async-start(f32[4,64,512]{2,1,0:T(8,128)} %shard_map.89), calls=%async_computation.2 | async-start | bytes 1048576 | tf_op jit(solution)/shard_map/all_to_all | solution.py:211
  (4 other events, 3.7 us)

commit v11 on v9

--- a/solution.py
+++ b/solution.py
@@ -85,14 +85,17 @@
         out_ref[x, rows:] = jnp.where(odd == 1, both, 0.0).astype(BF16)
 
 
-def cross_kernel(nz, iz_ref, exps_ref, c_ref, s_ref, place_ref, term_ref, out_ref):
-    nx, _, rows, _ = s_ref.shape
-    all_rows, ns = c_ref.shape
+def cross_kernel(nx, nz, at_ref, exps_ref, c_ref, place_ref, term_ref, *refs):
+    block_refs, (out_ref, s_ref) = refs[:nx], refs[nx:]
+    rows, ns = s_ref.shape[2:]
+    for by, block_ref in enumerate(block_refs):
+        s_ref[lax.rem(at_ref[0] + by, nx)] = block_ref[:, :, :ns]
+    all_rows = c_ref.shape[0]
     nf = place_ref.shape[2] // 2
     run = 2 * rows
     lane = lax.broadcasted_iota(jnp.int32, (all_rows, run), 1)
     for q in range(nx // 2):
-        block = s_ref[2 * q : 2 * q + 2, :, :, :ns].reshape(2 * run, ns)
+        block = s_ref[2 * q : 2 * q + 2].reshape(2 * run, ns)
         both = dot_t(c_ref[...], block)
         first, second = both[:, :run], both[:, run:]
         first = first + pltpu.roll(first, rows, 1)
@@ -100,7 +103,7 @@
         cross = jnp.where(lane < rows, first, second)
         at = slice(q * run, (q + 1) * run)
         out_ref[:, at] = (cross + term_ref[:, at]) * exps_ref[2]
-    pair = iz_ref[0] // 2
+    pair = at_ref[1] // 2
     share = jnp.zeros((all_rows, 2 * nf), F32)
     for x in range(nx):
         at = pl.ds(pl.multiple_of(x * nz * rows + pair * run, run), run)
@@ -150,12 +153,13 @@
     packed = pl.pallas_call(
         functools.partial(pack_kernel, cols),
         out_shape=jax.ShapeDtypeStruct((2, rows, ns + 2 * nf), BF16),
+        compiler_params=pltpu.CompilerParams(vmem_limit_bytes=4 << 20),
     )(s_own, a_own)
-    succ = jnp.zeros((nx,) + packed.shape, BF16)
-    for by in range(nx):
-        block = lax.ppermute(packed, "x", [((i + by) % nx, i) for i in range(nx)]) if by else packed
-        succ = lax.dynamic_update_index_in_dim(succ, block, (ix + by) % nx, 0)
-    tails = succ[..., ns:]
+    blocks = [packed]
+    for by in range(1, nx):
+        blocks.append(lax.ppermute(packed, "x", [((i + by) % nx, i) for i in range(nx)]))
+    tails = jnp.stack([block[..., ns:] for block in blocks] * 2)
+    tails = lax.dynamic_slice_in_dim(tails, (nx - ix) % nx, nx, 0)
     a_two = tails[..., :nf]
     exps = jnp.max(tails[:, 0, :, nf : nf + 2].astype(F32), axis=(0, 1))
     exps = jnp.concatenate([exps, jnp.exp2(14 - exps)])
@@ -168,20 +172,22 @@
         place_kernel,
         out_shape=jax.ShapeDtypeStruct((nx, 2 * rows, 2 * nf), BF16),
         in_specs=[in_smem, in_vmem],
+        compiler_params=pltpu.CompilerParams(vmem_limit_bytes=2 << 20),
     )(iz.reshape(1), tails)
 
     c_rows = spread(c_own, "z").reshape(nz * rows, ns)
     sent = pl.pallas_call(
-        functools.partial(cross_kernel, nz),
+        functools.partial(cross_kernel, nx, nz),
         out_shape=jax.ShapeDtypeStruct((nz * rows, cols + 2 * nf), F32),
-        in_specs=[in_smem] * 2 + [in_vmem] * 4,
+        in_specs=[in_smem] * 2 + [in_vmem] * (3 + nx),
+        scratch_shapes=[pltpu.VMEM((nx, 2, rows, ns), BF16)],
         compiler_params=pltpu.CompilerParams(vmem_limit_bytes=12 << 20),
-    )(iz.reshape(1), exps, c_rows, succ, place, term)
+    )(jnp.stack([ix, iz]), exps, c_rows, place, term, *blocks)
     c_turned = pl.pallas_call(
         functools.partial(turn_kernel, nx, nz),
         out_shape=jax.ShapeDtypeStruct(c_rows.shape, BF16),
         cost_estimate=pl.CostEstimate(flops=0, bytes_accessed=20 << 20, transcendentals=0),
-        compiler_params=pltpu.CompilerParams(vmem_limit_bytes=8 << 20),
+        compiler_params=pltpu.CompilerParams(vmem_limit_bytes=6 << 20),
     )(c_rows)
     sent = sent.reshape(nz, rows, cols + 2 * nf)
     sent = sent.astype(F16)
@@ -197,13 +203,14 @@
         diag_kernel,
         out_shape=jax.ShapeDtypeStruct((nx, rows, nz * rows), F32),
         scratch_shapes=[pltpu.VMEM((2, cols, ns), BF16)],
-        compiler_params=pltpu.CompilerParams(vmem_limit_bytes=12 << 20),
+        compiler_params=pltpu.CompilerParams(vmem_limit_bytes=10 << 20),
     )(every_top.astype(BF16), every_low, c_turned)
     diag = lax.all_to_all(diag, "x", 0, 0, tiled=True)
 
     cross_rows = pl.pallas_call(
         functools.partial(natural_kernel, nx, nz),
         out_shape=jax.ShapeDtypeStruct((rows, ns), F32),
+        compiler_params=pltpu.CompilerParams(vmem_limit_bytes=4 << 20),
     )(cross.astype(F32) * scale)
     share = sent[..., cols : cols + nf].astype(F32) * jnp.exp2(marks[..., 1:] - 14)
     link_own = lax.dynamic_slice_in_dim(link, (ix * nz + iz) * rows, rows, 0)

time: 129 us -> 126 us (0.977)
  the two profiles are of different devices: /device:TPU:2 before, /device:TPU:24 now
where the time goes in v11:
time: 126 us; the launch traced here: 125 us
  waiting for transfers between devices  50.9 us (40%)
  starting transfers between devices  32.7 us (26%)
  blocking collectives  18 us (14%)
  local copies, waits for them, and re-layouts  9.98 us (8%)
  Pallas kernels  7.34 us (6%)
  other arithmetic  3.43 us (3%)
  matrix products  1.92 us (2%)
    ppermute x3, waiting for transfers between devices, shards(): lax.ppermute(packed, 'x', [((i + by) % nx, i) for i in range(nx)])  24.4 us
    all_to_all x1, blocking collectives, shards(): sent = lax.all_to_all(sent, 'z', 0, 0, tiled=True)  18 us
    all_to_all x2, starting transfers between devices, spread(): lax.all_to_all(jnp.broadcast_to(v[None], (n,) + v.shape), axis, 0, 0, til...  14.7 us
    all_to_all x2, waiting for transfers between devices, spread(): lax.all_to_all(jnp.broadcast_to(v[None], (n,) + v.shape), axis, 0, 0, til...  14.6 us
    ppermute x3, starting transfers between devices, shards(): lax.ppermute(packed, 'x', [((i + by) % nx, i) for i in range(nx)])  10.2 us
    all_to_all x1, waiting for transfers between devices, shards(): diag = lax.all_to_all(diag, 'x', 0, 0, tiled=True)  7.31 us
    unnamed x33, local copies, waits for them, and re-layouts  6.14 us
    ppermute x2, waiting for transfers between devices, shards(): s_own, a_own = lax.ppermute((s_own, a_own), ('y', 'c', 'x', 'z'), route)  4.55 us
  transfers between devices with their start and end apart: 8, of which 7 were waited for; matrix products, arithmetic and copies ran while one was open for 3% of the time, Pallas kernels for 2%

profile of v11, /device:TPU:24, one launch (start us, length us, event | category | flops | bytes accessed | tf_op | source)
XLA Modules:
  0.0 125.2 jit_solution(10407791366967077073)
XLA Ops:
  0.6 2.6 %broadcast_in_dim.24 = bf16[8,64,2048]{2,1,0:T(8,128)(2,1)} broadcast(bf16[64,2048]{1,0:T(8,128)(2,1)} %bitcast.60), dimensions={1,2} | broadcast | bytes 2359296 | tf_op jit(solution)/shard_map/broadcast_in_dim | solution.py:24
  3.2 10.4 %all-to-all-start = ((bf16[8,64,2048]{2,1,0:T(8,128)(2,1)}), bf16[8,64,2048]{2,1,0:T(8,128)(2,1)S(1)}, u32[]{:S(2)}, u32[]{:S(2)}) async-start(bf16[8,64,2048]{2,1,0:T(8,128)(2,1)} %broadcast_in_dim.24), calls=%async_computation | async-start | bytes 4194304 | tf_op jit(solution)/shard_map/all_to_all | solution.py:24
  13.7 1.9 %collective-permute-start = (f32[64,2048]{1,0:T(8,128)S(1)}, f32[64,2048]{1,0:T(8,128)S(1)}, u32[]{:S(2)}, u32[]{:S(2)}) collective-permute-start(f32[64,2048]{1,0:T(8,128)S(1)} %bitcast.62), channel_id=1, source_target_pairs={{32,0},{33,1},{34,2},{35,3},{36,4},{37,5},{38,6},{39,7},{40,8},{41... | collective-permute-start | bytes 1572872 | tf_op jit(solution)/shard_map/ppermute | solution.py:152
  15.6 2.5 %collective-permute-start.1 = (f32[64,64]{1,0:T(8,128)S(1)}, f32[64,64]{1,0:T(8,128)S(1)}, u32[]{:S(2)}, u32[]{:S(2)}) collective-permute-start(f32[64,64]{1,0:T(8,128)S(1)} %bitcast.63), channel_id=1, source_target_pairs={{32,0},{33,1},{34,2},{35,3},{36,4},{37,5},{38,6},{39,7},{40,8},{41... | collective-permute-start | bytes 49160 | tf_op jit(solution)/shard_map/ppermute | solution.py:152
  18.1 4.5 %collective-permute-done.1.a_ref = f32[64,64]{1,0:T(8,128)S(1)} collective-permute-done((f32[64,64]{1,0:T(8,128)S(1)}, f32[64,64]{1,0:T(8,128)S(1)}, u32[]{:S(2)}, u32[]{:S(2)}) %collective-permute-start.1) | collective-permute-done | bytes 16416 | tf_op jit(solution)/shard_map/ppermute | solution.py:152
  22.9 4.7 %collective-permute-start.2 = (bf16[2,64,2176]{2,1,0:T(8,128)(2,1)S(1)}, bf16[2,64,2176]{2,1,0:T(8,128)(2,1)}, u32[]{:S(2)}, u32[]{:S(2)}) collective-permute-start(bf16[2,64,2176]{2,1,0:T(8,128)(2,1)S(1)} %shard_map.85.refs_0_), channel_id=1, source_target_pairs={{8,0},{16,8},{24,16},{0,24},{9,1},{17,9},{25,17},{1,25},{10,2},{18... | collective-permute-start | bytes 1671176 | tf_op jit(solution)/shard_map/ppermute | solution.py:160
  27.6 2.7 %collective-permute-start.3 = (bf16[2,64,2176]{2,1,0:T(8,128)(2,1)S(1)}, bf16[2,64,2176]{2,1,0:T(8,128)(2,1)S(1)}, u32[]{:S(2)}, u32[]{:S(2)}) collective-permute-start(bf16[2,64,2176]{2,1,0:T(8,128)(2,1)S(1)} %shard_map.85.refs_0_), channel_id=1, source_target_pairs={{16,0},{24,8},{0,16},{8,24},{17,1},{25,9},{1,17},{9,25},{18,2},{26... | collective-permute-start | bytes 1671176 | tf_op jit(solution)/shard_map/ppermute | solution.py:160
  30.4 2.8 %collective-permute-start.4 = (bf16[2,64,2176]{2,1,0:T(8,128)(2,1)S(1)}, bf16[2,64,2176]{2,1,0:T(8,128)(2,1)S(1)}, u32[]{:S(2)}, u32[]{:S(2)}) collective-permute-start(bf16[2,64,2176]{2,1,0:T(8,128)(2,1)S(1)} %shard_map.85.refs_0_), channel_id=1, source_target_pairs={{24,0},{0,8},{8,16},{16,24},{25,1},{1,9},{9,17},{17,25},{26,2},{2,... | collective-permute-start | bytes 1671176 | tf_op jit(solution)/shard_map/ppermute | solution.py:160
  33.2 5.7 %collective-permute-done.2.refs_1_ = bf16[2,64,2176]{2,1,0:T(8,128)(2,1)} collective-permute-done((bf16[2,64,2176]{2,1,0:T(8,128)(2,1)S(1)}, bf16[2,64,2176]{2,1,0:T(8,128)(2,1)}, u32[]{:S(2)}, u32[]{:S(2)}) %collective-permute-start.2) | collective-permute-done | bytes 557088 | tf_op jit(solution)/shard_map/ppermute | solution.py:160
  39.7 4.7 %collective-permute-done.3.refs_2_ = bf16[2,64,2176]{2,1,0:T(8,128)(2,1)S(1)} collective-permute-done((bf16[2,64,2176]{2,1,0:T(8,128)(2,1)S(1)}, bf16[2,64,2176]{2,1,0:T(8,128)(2,1)S(1)}, u32[]{:S(2)}, u32[]{:S(2)}) %collective-permute-start.3) | collective-permute-done | bytes 557088 | tf_op jit(solution)/shard_map/ppermute | solution.py:160
  44.5 13.9 %collective-permute-done.4.refs_3_ = bf16[2,64,2176]{2,1,0:T(8,128)(2,1)S(1)} collective-permute-done((bf16[2,64,2176]{2,1,0:T(8,128)(2,1)S(1)}, bf16[2,64,2176]{2,1,0:T(8,128)(2,1)S(1)}, u32[]{:S(2)}, u32[]{:S(2)}) %collective-permute-start.4) | collective-permute-done | bytes 557088 | tf_op jit(solution)/shard_map/ppermute | solution.py:160
  59.6 1.2 fusion.2.term_ref
  60.9 4.0 %all-to-all-done = bf16[8,64,2048]{2,1,0:T(8,128)(2,1)S(1)} async-done(((bf16[8,64,2048]{2,1,0:T(8,128)(2,1)}), bf16[8,64,2048]{2,1,0:T(8,128)(2,1)S(1)}, u32[]{:S(2)}, u32[]{:S(2)}) %all-to-all-start) | async-done | bytes 2097184 | tf_op jit(solution)/shard_map/all_to_all | solution.py:24
  68.0 2.7 %shard_map.87 = f32[512,384]{1,0:T(8,128)S(1)} custom-call(s32[2]{0:T(128)S(1)} %pad_add_fusion.at_ref, f32[4]{0:T(128)S(1)} %pad_maximum_fusion.exps_ref, bf16[512,2048]{1,0:T(8,128)(2,1)S(1)} %bitcast.53, bf16[4,128,128]{2,1,0:T(8,128)(2,1)S(1)} %shard_map.86.place_ref, f32[512,256]{1,0:T(8,128)S(1)} %copy-done.3, ...), custom_call_target="tpu_custom_call" | custom-call | tf_op jit(solution)/shard_map/pallas_call | solution.py:179
  70.9 18.0 %all_to_all.20 = f16[8,64,384]{2,1,0:T(8,128)(2,1)S(1)} all-to-all(f16[8,64,384]{2,1,0:T(8,128)(2,1)S(1)} %bitcast.57), channel_id=1, replica_groups=mesh['y'=8,'c'=2,'x'=4,'z'=8] {'z'}, dimensions={0} | all-to-all | bytes 786432 | tf_op jit(solution)/shard_map/all_to_all | solution.py:194
  88.9 1.1 broadcast_in_dim.25
  90.1 4.3 %all-to-all-start.2 = ((f16[4,8,64,256]{3,2,1,0:T(8,128)(2,1)}), f16[4,8,64,256]{3,2,1,0:T(8,128)(2,1)}, u32[]{:S(2)}, u32[]{:S(2)}) async-start(f16[4,8,64,256]{3,2,1,0:T(8,128)(2,1)} %broadcast_in_dim.25), calls=%async_computation.2 | async-start | bytes 2097152 | tf_op jit(solution)/shard_map/all_to_all | solution.py:24
  94.3 1.1 shard_map.88.c_ref
  95.5 1.3 %copy-done.1 = bf16[512,2048]{1,0:T(8,128)(2,1)} copy-done((bf16[512,2048]{1,0:T(8,128)(2,1)}, bf16[512,2048]{1,0:T(8,128)(2,1)S(1)}, u32[]{:S(2)}) %copy-start.1) | copy-done | bytes 2097176
  98.3 10.6 %all-to-all-done.2 = f16[4,8,64,256]{3,2,1,0:T(8,128)(2,1)} async-done(((f16[4,8,64,256]{3,2,1,0:T(8,128)(2,1)}), f16[4,8,64,256]{3,2,1,0:T(8,128)(2,1)}, u32[]{:S(2)}, u32[]{:S(2)}) %all-to-all-start.2) | async-done | bytes 1048608 | tf_op jit(solution)/shard_map/all_to_all | solution.py:24
  108.9 1.7 %fusion = (bf16[4,8,64,256]{3,2,1,0:T(8,128)(2,1)S(1)}, bf16[4,8,64,256]{3,2,1,0:T(8,128)(2,1)S(1)}) fusion(f16[4,8,64,256]{3,2,1,0:T(8,128)(2,1)} %all-to-all-done.2, f32[8]{0:T(128)S(1)} %get-tuple-element.3), kind=kLoop, calls=%fused_computation.3 | loop fusion | flops 3145728 | bytes 3145760 | tf_op jit(solution)/shard_map/convert_element_type | solution.py:201
  110.7 2.1 %shard_map.89 = f32[4,64,512]{2,1,0:T(8,128)} custom-call(bf16[4,8,64,256]{3,2,1,0:T(8,128)(2,1)S(1)} %get-tuple-element.6.top_ref, bf16[4,8,64,256]{3,2,1,0:T(8,128)(2,1)S(1)} %get-tuple-element.5.low_ref, bf16[512,2048]{1,0:T(8,128)(2,1)S(1)} %copy-done.2), custom_call_target="tpu_custom_call" | custom-call | tf_op jit(solution)/shard_map/pallas_call | solution.py:202
  112.8 3.5 %all-to-all-start.3 = ((f32[4,64,512]{2,1,0:T(8,128)}), f32[4,64,512]{2,1,0:T(8,128)S(1)}, u32[]{:S(2)}, u32[]{:S(2)}) async-start(f32[4,64,512]{2,1,0:T(8,128)} %shard_map.89), calls=%async_computation.3 | async-start | bytes 1048576 | tf_op jit(solution)/shard_map/all_to_all | solution.py:208
  117.0 7.3 %all-to-all-done.3 = f32[4,64,512]{2,1,0:T(8,128)S(1)} async-done(((f32[4,64,512]{2,1,0:T(8,128)}), f32[4,64,512]{2,1,0:T(8,128)S(1)}, u32[]{:S(2)}, u32[]{:S(2)}) %all-to-all-start.3) | async-done | bytes 524320 | tf_op jit(solution)/shard_map/all_to_all | solution.py:208
  (54 shorter events, 8.7 us)
Async XLA Ops:
  0.6 59.0 %copy-start = (f32[1,2048,64]{1,2,0:T(8,128)S(1)}, f32[1,2048,64]{1,2,0:T(8,128)}, u32[]{:S(2)}) copy-start(f32[1,2048,64]{1,2,0:T(8,128)} %param.7) | copy-start | bytes 1572868
  3.2 10.5 %copy-start.11 = (f32[1,64,2048]{2,1,0:T(8,128)S(1)}, f32[1,64,2048]{2,1,0:T(8,128)}, u32[]{:S(2)}) copy-start(f32[1,64,2048]{2,1,0:T(8,128)} %param.9) | copy-start | bytes 1572868
  3.2 12.4 %copy-start.12 = (f32[1,64,64]{2,1,0:T(8,128)S(1)}, f32[1,64,64]{2,1,0:T(8,128)}, u32[]{:S(2)}) copy-start(f32[1,64,64]{2,1,0:T(8,128)} %param.10) | copy-start | bytes 49156
  3.2 61.6 %all-to-all-start = ((bf16[8,64,2048]{2,1,0:T(8,128)(2,1)}), bf16[8,64,2048]{2,1,0:T(8,128)(2,1)S(1)}, u32[]{:S(2)}, u32[]{:S(2)}) async-start(bf16[8,64,2048]{2,1,0:T(8,128)(2,1)} %broadcast_in_dim.24), calls=%async_computation | async-start | bytes 4194304 | tf_op jit(solution)/shard_map/all_to_all | solution.py:24
  13.7 9.0 %collective-permute-start = (f32[64,2048]{1,0:T(8,128)S(1)}, f32[64,2048]{1,0:T(8,128)S(1)}, u32[]{:S(2)}, u32[]{:S(2)}) collective-permute-start(f32[64,2048]{1,0:T(8,128)S(1)} %bitcast.62), channel_id=1, source_target_pairs={{32,0},{33,1},{34,2},{35,3},{36,4},{37,5},{38,6},{39,7},{40,8},{41... | collective-permute-start | bytes 1572872 | tf_op jit(solution)/shard_map/ppermute | solution.py:152
  15.6 7.0 %collective-permute-start.1 = (f32[64,64]{1,0:T(8,128)S(1)}, f32[64,64]{1,0:T(8,128)S(1)}, u32[]{:S(2)}, u32[]{:S(2)}) collective-permute-start(f32[64,64]{1,0:T(8,128)S(1)} %bitcast.63), channel_id=1, source_target_pairs={{32,0},{33,1},{34,2},{35,3},{36,4},{37,5},{38,6},{39,7},{40,8},{41... | collective-permute-start | bytes 49160 | tf_op jit(solution)/shard_map/ppermute | solution.py:152
  22.9 16.0 %collective-permute-start.2 = (bf16[2,64,2176]{2,1,0:T(8,128)(2,1)S(1)}, bf16[2,64,2176]{2,1,0:T(8,128)(2,1)}, u32[]{:S(2)}, u32[]{:S(2)}) collective-permute-start(bf16[2,64,2176]{2,1,0:T(8,128)(2,1)S(1)} %shard_map.85.refs_0_), channel_id=1, source_target_pairs={{8,0},{16,8},{24,16},{0,24},{9,1},{17,9},{25,17},{1,25},{10,2},{18... | collective-permute-start | bytes 1671176 | tf_op jit(solution)/shard_map/ppermute | solution.py:160
  27.6 16.8 %collective-permute-start.3 = (bf16[2,64,2176]{2,1,0:T(8,128)(2,1)S(1)}, bf16[2,64,2176]{2,1,0:T(8,128)(2,1)S(1)}, u32[]{:S(2)}, u32[]{:S(2)}) collective-permute-start(bf16[2,64,2176]{2,1,0:T(8,128)(2,1)S(1)} %shard_map.85.refs_0_), channel_id=1, source_target_pairs={{16,0},{24,8},{0,16},{8,24},{17,1},{25,9},{1,17},{9,25},{18,2},{26... | collective-permute-start | bytes 1671176 | tf_op jit(solution)/shard_map/ppermute | solution.py:160
  30.4 27.9 %collective-permute-start.4 = (bf16[2,64,2176]{2,1,0:T(8,128)(2,1)S(1)}, bf16[2,64,2176]{2,1,0:T(8,128)(2,1)S(1)}, u32[]{:S(2)}, u32[]{:S(2)}) collective-permute-start(bf16[2,64,2176]{2,1,0:T(8,128)(2,1)S(1)} %shard_map.85.refs_0_), channel_id=1, source_target_pairs={{24,0},{0,8},{8,16},{16,24},{25,1},{1,9},{9,17},{17,25},{26,2},{2,... | collective-permute-start | bytes 1671176 | tf_op jit(solution)/shard_map/ppermute | solution.py:160
  44.4 15.2 %copy-start.4 = (bf16[2,64,2176]{2,1,0:T(8,128)(2,1)}, bf16[2,64,2176]{2,1,0:T(8,128)(2,1)S(1)}, u32[]{:S(2)}) copy-start(bf16[2,64,2176]{2,1,0:T(8,128)(2,1)S(1)} %collective-permute-done.3.refs_2_) | copy-start | bytes 1671172
  58.4 1.2 copy-start.6
  64.9 1.0 copy-start.3
  65.9 1.1 copy-start.5
  67.0 1.1 copy-start.7
  90.1 18.9 %all-to-all-start.2 = ((f16[4,8,64,256]{3,2,1,0:T(8,128)(2,1)}), f16[4,8,64,256]{3,2,1,0:T(8,128)(2,1)}, u32[]{:S(2)}, u32[]{:S(2)}) async-start(f16[4,8,64,256]{3,2,1,0:T(8,128)(2,1)} %broadcast_in_dim.25), calls=%async_computation.2 | async-start | bytes 2097152 | tf_op jit(solution)/shard_map/all_to_all | solution.py:24
  95.5 1.3 %copy-start.1 = (bf16[512,2048]{1,0:T(8,128)(2,1)}, bf16[512,2048]{1,0:T(8,128)(2,1)S(1)}, u32[]{:S(2)}) copy-start(bf16[512,2048]{1,0:T(8,128)(2,1)S(1)} %shard_map.88.c_ref) | copy-start | bytes 6291460
  97.2 13.4 %copy-start.2 = (bf16[512,2048]{1,0:T(8,128)(2,1)S(1)}, bf16[512,2048]{1,0:T(8,128)(2,1)}, u32[]{:S(2)}) copy-start(bf16[512,2048]{1,0:T(8,128)(2,1)} %copy-done.1) | copy-start | bytes 6291460
  110.7 5.6 %copy-start.10 = (f32[64,64]{1,0:T(8,128)S(1)}, f32[64,64]{1,0:T(8,128)}, u32[]{:S(2)}) copy-start(f32[64,64]{1,0:T(8,128)} %param.11) | copy-start | bytes 49156
  110.7 5.9 %copy-start.8 = (f32[1,64,2048]{2,1,0:T(8,128)S(1)}, f32[1,64,2048]{2,1,0:T(8,128)}, u32[]{:S(2)}) copy-start(f32[1,64,2048]{2,1,0:T(8,128)} %param.8) | copy-start | bytes 1572868
  112.8 11.5 %all-to-all-start.3 = ((f32[4,64,512]{2,1,0:T(8,128)}), f32[4,64,512]{2,1,0:T(8,128)S(1)}, u32[]{:S(2)}, u32[]{:S(2)}) async-start(f32[4,64,512]{2,1,0:T(8,128)} %shard_map.89), calls=%async_computation.3 | async-start | bytes 1048576 | tf_op jit(solution)/shard_map/all_to_all | solution.py:208
  116.6 8.6 %copy-start.9 = (f32[64,64]{1,0:T(8,128)}, f32[64,64]{1,0:T(8,128)S(1)}, u32[]{:S(2)}) copy-start(f32[64,64]{1,0:T(8,128)S(1)} %convolution_add_fusion.1) | copy-start | bytes 49156

commit v12 on v9

--- a/solution.py
+++ b/solution.py
@@ -146,11 +146,14 @@
     ix, iz = lax.axis_index("x"), lax.axis_index("z")
 
     route = [(t * group + b, (t - 1) * group + b) for t in range(1, steps) for b in range(group)]
-    s_own, a_own = lax.ppermute((s_own, a_own), ("y", "c", "x", "z"), route)
+    copies = jnp.broadcast_to(c_own[None], (nz, rows, ns))
+    copies, s_own, a_own = lax.optimization_barrier((copies, s_own, a_own))
     packed = pl.pallas_call(
         functools.partial(pack_kernel, cols),
         out_shape=jax.ShapeDtypeStruct((2, rows, ns + 2 * nf), BF16),
+        compiler_params=pltpu.CompilerParams(vmem_limit_bytes=4 << 20),
     )(s_own, a_own)
+    packed = lax.ppermute(packed, ("y", "c", "x", "z"), route)
     succ = jnp.zeros((nx,) + packed.shape, BF16)
     for by in range(nx):
         block = lax.ppermute(packed, "x", [((i + by) % nx, i) for i in range(nx)]) if by else packed
@@ -168,20 +171,21 @@
         place_kernel,
         out_shape=jax.ShapeDtypeStruct((nx, 2 * rows, 2 * nf), BF16),
         in_specs=[in_smem, in_vmem],
+        compiler_params=pltpu.CompilerParams(vmem_limit_bytes=2 << 20),
     )(iz.reshape(1), tails)
 
-    c_rows = spread(c_own, "z").reshape(nz * rows, ns)
+    c_rows = lax.all_to_all(copies, "z", 0, 0, tiled=True).reshape(nz * rows, ns)
     sent = pl.pallas_call(
         functools.partial(cross_kernel, nz),
         out_shape=jax.ShapeDtypeStruct((nz * rows, cols + 2 * nf), F32),
         in_specs=[in_smem] * 2 + [in_vmem] * 4,
-        compiler_params=pltpu.CompilerParams(vmem_limit_bytes=12 << 20),
+        compiler_params=pltpu.CompilerParams(vmem_limit_bytes=10 << 20),
     )(iz.reshape(1), exps, c_rows, succ, place, term)
     c_turned = pl.pallas_call(
         functools.partial(turn_kernel, nx, nz),
         out_shape=jax.ShapeDtypeStruct(c_rows.shape, BF16),
         cost_estimate=pl.CostEstimate(flops=0, bytes_accessed=20 << 20, transcendentals=0),
-        compiler_params=pltpu.CompilerParams(vmem_limit_bytes=8 << 20),
+        compiler_params=pltpu.CompilerParams(vmem_limit_bytes=6 << 20),
     )(c_rows)
     sent = sent.reshape(nz, rows, cols + 2 * nf)
     sent = sent.astype(F16)
@@ -197,13 +201,14 @@
         diag_kernel,
         out_shape=jax.ShapeDtypeStruct((nx, rows, nz * rows), F32),
         scratch_shapes=[pltpu.VMEM((2, cols, ns), BF16)],
-        compiler_params=pltpu.CompilerParams(vmem_limit_bytes=12 << 20),
+        compiler_params=pltpu.CompilerParams(vmem_limit_bytes=10 << 20),
     )(every_top.astype(BF16), every_low, c_turned)
     diag = lax.all_to_all(diag, "x", 0, 0, tiled=True)
 
     cross_rows = pl.pallas_call(
         functools.partial(natural_kernel, nx, nz),
         out_shape=jax.ShapeDtypeStruct((rows, ns), F32),
+        compiler_params=pltpu.CompilerParams(vmem_limit_bytes=4 << 20),
     )(cross.astype(F32) * scale)
     share = sent[..., cols : cols + nf].astype(F32) * jnp.exp2(marks[..., 1:] - 14)
     link_own = lax.dynamic_slice_in_dim(link, (ix * nz + iz) * rows, rows, 0)

time: 129 us -> 128 us (level)
  the two profiles are of different devices: /device:TPU:2 before, /device:TPU:56 now
where the time goes in v12:
time: 128 us
  waiting for transfers between devices  57.2 us (45%)
  starting transfers between devices  31 us (24%)
  blocking collectives  17.6 us (14%)
  local copies, waits for them, and re-layouts  9.76 us (8%)
  Pallas kernels  6.72 us (5%)
  other arithmetic  3.34 us (3%)
    ppermute x3, waiting for transfers between devices, shards(): lax.ppermute(packed, 'x', [((i + by) % nx, i) for i in range(nx)])  23 us
    all_to_all x1, blocking collectives, shards(): sent = lax.all_to_all(sent, 'z', 0, 0, tiled=True)  17.6 us
    all_to_all x1, waiting for transfers between devices, shards(): lax.all_to_all(copies, 'z', 0, 0, tiled=True).reshape(nz * rows, ns)  15 us
    all_to_all x1, waiting for transfers between devices, spread(): lax.all_to_all(jnp.broadcast_to(v[None], (n,) + v.shape), axis, 0, 0, til...  11.3 us
    all_to_all x1, starting transfers between devices, shards(): lax.all_to_all(copies, 'z', 0, 0, tiled=True).reshape(nz * rows, ns)  10.3 us
    ppermute x3, starting transfers between devices, shards(): lax.ppermute(packed, 'x', [((i + by) % nx, i) for i in range(nx)])  10.2 us
    all_to_all x1, waiting for transfers between devices, shards(): diag = lax.all_to_all(diag, 'x', 0, 0, tiled=True)  7.92 us
    unnamed x20, local copies, waits for them, and re-layouts  4.37 us
  transfers between devices with their start and end apart: 7, of which 5 were waited for; matrix products, arithmetic and copies ran while one was open for 3% of the time, Pallas kernels for 2%

profile of v12, /device:TPU:56, one launch (start us, length us, event | category | flops | bytes accessed | tf_op | source)
XLA Modules:
  0.0 127.6 jit_solution(1387805066090407972)
XLA Ops:
  0.7 2.6 %broadcast_in_dim.41 = bf16[8,64,2048]{2,1,0:T(8,128)(2,1)} broadcast(bf16[64,2048]{1,0:T(8,128)(2,1)} %bitcast.45), dimensions={1,2} | broadcast | bytes 2359296 | tf_op jit(solution)/shard_map/broadcast_in_dim | solution.py:149
  3.5 2.7 %collective-permute-start = (bf16[2,64,2176]{2,1,0:T(8,128)(2,1)S(1)}, bf16[2,64,2176]{2,1,0:T(8,128)(2,1)}, u32[]{:S(2)}, u32[]{:S(2)}) collective-permute-start(bf16[2,64,2176]{2,1,0:T(8,128)(2,1)S(1)} %shard_map.85), channel_id=1, source_target_pairs={{32,0},{33,1},{34,2},{35,3},{36,4},{37,5},{38,6},{39,7},{40,8},{41... | collective-permute-start | bytes 1671176 | tf_op jit(solution)/shard_map/ppermute | solution.py:156
  6.2 10.3 %all-to-all-start = ((bf16[8,64,2048]{2,1,0:T(8,128)(2,1)}), bf16[8,64,2048]{2,1,0:T(8,128)(2,1)S(1)}, u32[]{:S(2)}, u32[]{:S(2)}) async-start(bf16[8,64,2048]{2,1,0:T(8,128)(2,1)} %broadcast_in_dim.41), calls=%async_computation | async-start | bytes 4194304 | tf_op jit(solution)/shard_map/all_to_all | solution.py:177
  16.6 4.7 %collective-permute-start.1 = (bf16[2,64,2176]{2,1,0:T(8,128)(2,1)}, bf16[2,64,2176]{2,1,0:T(8,128)(2,1)S(1)}, u32[]{:S(2)}, u32[]{:S(2)}) collective-permute-start(bf16[2,64,2176]{2,1,0:T(8,128)(2,1)} %collective-permute-done), channel_id=1, source_target_pairs={{8,0},{16,8},{24,16},{0,24},{9,1},{17,9},{25,17},{1,25},{10,2},{18... | collective-permute-start | bytes 1671176 | tf_op jit(solution)/shard_map/ppermute | solution.py:159
  21.3 2.7 %collective-permute-start.2 = (bf16[2,64,2176]{2,1,0:T(8,128)(2,1)}, bf16[2,64,2176]{2,1,0:T(8,128)(2,1)S(1)}, u32[]{:S(2)}, u32[]{:S(2)}) collective-permute-start(bf16[2,64,2176]{2,1,0:T(8,128)(2,1)} %collective-permute-done), channel_id=1, source_target_pairs={{16,0},{24,8},{0,16},{8,24},{17,1},{25,9},{1,17},{9,25},{18,2},{26... | collective-permute-start | bytes 1671176 | tf_op jit(solution)/shard_map/ppermute | solution.py:159
  24.0 2.8 %collective-permute-start.3 = (bf16[2,64,2176]{2,1,0:T(8,128)(2,1)}, bf16[2,64,2176]{2,1,0:T(8,128)(2,1)S(1)}, u32[]{:S(2)}, u32[]{:S(2)}) collective-permute-start(bf16[2,64,2176]{2,1,0:T(8,128)(2,1)} %collective-permute-done), channel_id=1, source_target_pairs={{24,0},{0,8},{8,16},{16,24},{25,1},{1,9},{9,17},{17,25},{26,2},{2,... | collective-permute-start | bytes 1671176 | tf_op jit(solution)/shard_map/ppermute | solution.py:159
  27.0 1.1 bitcast_dynamic-update-slice_fusion.3
  28.2 17.6 %collective-permute-done.1 = bf16[2,64,2176]{2,1,0:T(8,128)(2,1)S(1)} collective-permute-done((bf16[2,64,2176]{2,1,0:T(8,128)(2,1)}, bf16[2,64,2176]{2,1,0:T(8,128)(2,1)S(1)}, u32[]{:S(2)}, u32[]{:S(2)}) %collective-permute-start.1) | collective-permute-done | bytes 557088 | tf_op jit(solution)/shard_map/ppermute | solution.py:159
  45.9 5.3 %collective-permute-done.3 = bf16[2,64,2176]{2,1,0:T(8,128)(2,1)S(1)} collective-permute-done((bf16[2,64,2176]{2,1,0:T(8,128)(2,1)}, bf16[2,64,2176]{2,1,0:T(8,128)(2,1)S(1)}, u32[]{:S(2)}, u32[]{:S(2)}) %collective-permute-start.3) | collective-permute-done | bytes 557088 | tf_op jit(solution)/shard_map/ppermute | solution.py:159
  51.7 1.4 %copy-done.1 = bf16[4,2,64,2176]{3,2,1,0:T(8,128)(2,1)} copy-done((bf16[4,2,64,2176]{3,2,1,0:T(8,128)(2,1)}, bf16[4,2,64,2176]{3,2,1,0:T(8,128)(2,1)S(1)}, u32[]{:S(2)}) %copy-start.1) | copy-done | bytes 2228248
  53.5 15.0 %all-to-all-done = bf16[8,64,2048]{2,1,0:T(8,128)(2,1)S(1)} async-done(((bf16[8,64,2048]{2,1,0:T(8,128)(2,1)}), bf16[8,64,2048]{2,1,0:T(8,128)(2,1)S(1)}, u32[]{:S(2)}, u32[]{:S(2)}) %all-to-all-start) | async-done | bytes 2097184 | tf_op jit(solution)/shard_map/all_to_all | solution.py:177
  68.5 1.6 %copy-done.2 = bf16[4,2,64,2176]{3,2,1,0:T(8,128)(2,1)S(1)} copy-done((bf16[4,2,64,2176]{3,2,1,0:T(8,128)(2,1)S(1)}, bf16[4,2,64,2176]{3,2,1,0:T(8,128)(2,1)}, u32[]{:S(2)}) %copy-start.2) | copy-done | bytes 2228248
  70.1 2.1 %shard_map.87 = f32[512,384]{1,0:T(8,128)S(1)} custom-call(s32[1]{0:T(128)} %bitcast.1.iz_ref, f32[4]{0:T(128)S(1)} %pad_maximum_fusion.exps_ref, bf16[512,2048]{1,0:T(8,128)(2,1)S(1)} %bitcast.36, bf16[4,2,64,2176]{3,2,1,0:T(8,128)(2,1)S(1)} %copy-done.2, bf16[4,128,128]{2,1,0:T(8,128)(2,1)S(1)} %shard_map.86.place_ref, f32[512,256]{1,0:T(8,128)S(1)} %fusion.2.term_ref), custom_call_target="tpu_custom_call" | custom-call | tf_op jit(solution)/shard_map/pallas_call | solution.py:178
  72.3 17.6 %all_to_all.20 = f16[8,64,384]{2,1,0:T(8,128)(2,1)S(1)} all-to-all(f16[8,64,384]{2,1,0:T(8,128)(2,1)S(1)} %bitcast.42), channel_id=1, replica_groups=mesh['y'=8,'c'=2,'x'=4,'z'=8] {'z'}, dimensions={0} | all-to-all | bytes 786432 | tf_op jit(solution)/shard_map/all_to_all | solution.py:192
  89.9 1.1 broadcast_in_dim.46
  91.1 4.3 %all-to-all-start.2 = ((f16[4,8,64,256]{3,2,1,0:T(8,128)(2,1)}), f16[4,8,64,256]{3,2,1,0:T(8,128)(2,1)}, u32[]{:S(2)}, u32[]{:S(2)}) async-start(f16[4,8,64,256]{3,2,1,0:T(8,128)(2,1)} %broadcast_in_dim.46), calls=%async_computation.2 | async-start | bytes 2097152 | tf_op jit(solution)/shard_map/all_to_all | solution.py:24
  95.4 1.1 shard_map.88.c_ref
  96.5 1.3 %copy-done.3 = bf16[512,2048]{1,0:T(8,128)(2,1)} copy-done((bf16[512,2048]{1,0:T(8,128)(2,1)}, bf16[512,2048]{1,0:T(8,128)(2,1)S(1)}, u32[]{:S(2)}) %copy-start.3) | copy-done | bytes 2097176
  98.3 1.0 shard_map.90
  99.4 11.3 %all-to-all-done.2 = f16[4,8,64,256]{3,2,1,0:T(8,128)(2,1)} async-done(((f16[4,8,64,256]{3,2,1,0:T(8,128)(2,1)}), f16[4,8,64,256]{3,2,1,0:T(8,128)(2,1)}, u32[]{:S(2)}, u32[]{:S(2)}) %all-to-all-start.2) | async-done | bytes 1048608 | tf_op jit(solution)/shard_map/all_to_all | solution.py:24
  110.7 1.7 %fusion = (bf16[4,8,64,256]{3,2,1,0:T(8,128)(2,1)S(1)}, bf16[4,8,64,256]{3,2,1,0:T(8,128)(2,1)S(1)}) fusion(f16[4,8,64,256]{3,2,1,0:T(8,128)(2,1)} %all-to-all-done.2, f32[8]{0:T(128)S(1)} %get-tuple-element.9), kind=kLoop, calls=%fused_computation.3 | loop fusion | flops 3145728 | bytes 3145760 | tf_op jit(solution)/shard_map/convert_element_type | solution.py:199
  112.4 2.1 %shard_map.89 = f32[4,64,512]{2,1,0:T(8,128)} custom-call(bf16[4,8,64,256]{3,2,1,0:T(8,128)(2,1)S(1)} %get-tuple-element.12.top_ref, bf16[4,8,64,256]{3,2,1,0:T(8,128)(2,1)S(1)} %get-tuple-element.11.low_ref, bf16[512,2048]{1,0:T(8,128)(2,1)S(1)} %copy-done.4), custom_call_target="tpu_custom_call" | custom-call | tf_op jit(solution)/shard_map/pallas_call | solution.py:200
  114.5 3.5 %all-to-all-start.3 = ((f32[4,64,512]{2,1,0:T(8,128)}), f32[4,64,512]{2,1,0:T(8,128)S(1)}, u32[]{:S(2)}, u32[]{:S(2)}) async-start(f32[4,64,512]{2,1,0:T(8,128)} %shard_map.89), calls=%async_computation.3 | async-start | bytes 1048576 | tf_op jit(solution)/shard_map/all_to_all | solution.py:206
  118.8 7.9 %all-to-all-done.3 = f32[4,64,512]{2,1,0:T(8,128)S(1)} async-done(((f32[4,64,512]{2,1,0:T(8,128)}), f32[4,64,512]{2,1,0:T(8,128)S(1)}, u32[]{:S(2)}, u32[]{:S(2)}) %all-to-all-start.3) | async-done | bytes 524320 | tf_op jit(solution)/shard_map/all_to_all | solution.py:206
  (42 shorter events, 3.7 us)
Async XLA Ops:
  0.6 52.5 %copy-start = (f32[1,2048,64]{1,2,0:T(8,128)S(1)}, f32[1,2048,64]{1,2,0:T(8,128)}, u32[]{:S(2)}) copy-start(f32[1,2048,64]{1,2,0:T(8,128)} %param.7) | copy-start | bytes 1572868
  0.6 2.6 %copy-start.5 = (f32[1,64,2048]{2,1,0:T(8,128)S(1)}, f32[1,64,2048]{2,1,0:T(8,128)}, u32[]{:S(2)}) copy-start(f32[1,64,2048]{2,1,0:T(8,128)} %param.9) | copy-start | bytes 1572868
  0.7 2.6 %copy-start.6 = (f32[1,64,64]{2,1,0:T(8,128)S(1)}, f32[1,64,64]{2,1,0:T(8,128)}, u32[]{:S(2)}) copy-start(f32[1,64,64]{2,1,0:T(8,128)} %param.10) | copy-start | bytes 49156
  3.5 13.0 %collective-permute-start = (bf16[2,64,2176]{2,1,0:T(8,128)(2,1)S(1)}, bf16[2,64,2176]{2,1,0:T(8,128)(2,1)}, u32[]{:S(2)}, u32[]{:S(2)}) collective-permute-start(bf16[2,64,2176]{2,1,0:T(8,128)(2,1)S(1)} %shard_map.85), channel_id=1, source_target_pairs={{32,0},{33,1},{34,2},{35,3},{36,4},{37,5},{38,6},{39,7},{40,8},{41... | collective-permute-start | bytes 1671176 | tf_op jit(solution)/shard_map/ppermute | solution.py:156
  6.2 62.3 %all-to-all-start = ((bf16[8,64,2048]{2,1,0:T(8,128)(2,1)}), bf16[8,64,2048]{2,1,0:T(8,128)(2,1)S(1)}, u32[]{:S(2)}, u32[]{:S(2)}) async-start(bf16[8,64,2048]{2,1,0:T(8,128)(2,1)} %broadcast_in_dim.41), calls=%async_computation | async-start | bytes 4194304 | tf_op jit(solution)/shard_map/all_to_all | solution.py:177
  16.6 29.2 %collective-permute-start.1 = (bf16[2,64,2176]{2,1,0:T(8,128)(2,1)}, bf16[2,64,2176]{2,1,0:T(8,128)(2,1)S(1)}, u32[]{:S(2)}, u32[]{:S(2)}) collective-permute-start(bf16[2,64,2176]{2,1,0:T(8,128)(2,1)} %collective-permute-done), channel_id=1, source_target_pairs={{8,0},{16,8},{24,16},{0,24},{9,1},{17,9},{25,17},{1,25},{10,2},{18... | collective-permute-start | bytes 1671176 | tf_op jit(solution)/shard_map/ppermute | solution.py:159
  21.3 24.6 %collective-permute-start.2 = (bf16[2,64,2176]{2,1,0:T(8,128)(2,1)}, bf16[2,64,2176]{2,1,0:T(8,128)(2,1)S(1)}, u32[]{:S(2)}, u32[]{:S(2)}) collective-permute-start(bf16[2,64,2176]{2,1,0:T(8,128)(2,1)} %collective-permute-done), channel_id=1, source_target_pairs={{16,0},{24,8},{0,16},{8,24},{17,1},{25,9},{1,17},{9,25},{18,2},{26... | collective-permute-start | bytes 1671176 | tf_op jit(solution)/shard_map/ppermute | solution.py:159
  24.0 27.3 %collective-permute-start.3 = (bf16[2,64,2176]{2,1,0:T(8,128)(2,1)}, bf16[2,64,2176]{2,1,0:T(8,128)(2,1)S(1)}, u32[]{:S(2)}, u32[]{:S(2)}) collective-permute-start(bf16[2,64,2176]{2,1,0:T(8,128)(2,1)} %collective-permute-done), channel_id=1, source_target_pairs={{24,0},{0,8},{8,16},{16,24},{25,1},{1,9},{9,17},{17,25},{26,2},{2,... | collective-permute-start | bytes 1671176 | tf_op jit(solution)/shard_map/ppermute | solution.py:159
  51.7 1.4 %copy-start.1 = (bf16[4,2,64,2176]{3,2,1,0:T(8,128)(2,1)}, bf16[4,2,64,2176]{3,2,1,0:T(8,128)(2,1)S(1)}, u32[]{:S(2)}) copy-start(bf16[4,2,64,2176]{3,2,1,0:T(8,128)(2,1)S(1)} %bitcast_dynamic-update-slice_fusion.s_ref) | copy-start | bytes 6684676
  68.5 1.6 %copy-start.2 = (bf16[4,2,64,2176]{3,2,1,0:T(8,128)(2,1)S(1)}, bf16[4,2,64,2176]{3,2,1,0:T(8,128)(2,1)}, u32[]{:S(2)}) copy-start(bf16[4,2,64,2176]{3,2,1,0:T(8,128)(2,1)} %copy-done.1) | copy-start | bytes 6684676
  91.1 19.6 %all-to-all-start.2 = ((f16[4,8,64,256]{3,2,1,0:T(8,128)(2,1)}), f16[4,8,64,256]{3,2,1,0:T(8,128)(2,1)}, u32[]{:S(2)}, u32[]{:S(2)}) async-start(f16[4,8,64,256]{3,2,1,0:T(8,128)(2,1)} %broadcast_in_dim.46), calls=%async_computation.2 | async-start | bytes 2097152 | tf_op jit(solution)/shard_map/all_to_all | solution.py:24
  96.5 1.3 %copy-start.3 = (bf16[512,2048]{1,0:T(8,128)(2,1)}, bf16[512,2048]{1,0:T(8,128)(2,1)S(1)}, u32[]{:S(2)}) copy-start(bf16[512,2048]{1,0:T(8,128)(2,1)S(1)} %shard_map.88.c_ref) | copy-start | bytes 6291460
  98.2 14.2 %copy-start.4 = (bf16[512,2048]{1,0:T(8,128)(2,1)S(1)}, bf16[512,2048]{1,0:T(8,128)(2,1)}, u32[]{:S(2)}) copy-start(bf16[512,2048]{1,0:T(8,128)(2,1)} %copy-done.3) | copy-start | bytes 6291460
  112.4 5.6 %copy-start.9 = (f32[64,64]{1,0:T(8,128)S(1)}, f32[64,64]{1,0:T(8,128)}, u32[]{:S(2)}) copy-start(f32[64,64]{1,0:T(8,128)} %param.11) | copy-start | bytes 49156
  112.4 5.9 %copy-start.7 = (f32[1,64,2048]{2,1,0:T(8,128)S(1)}, f32[1,64,2048]{2,1,0:T(8,128)}, u32[]{:S(2)}) copy-start(f32[1,64,2048]{2,1,0:T(8,128)} %param.8) | copy-start | bytes 1572868
  114.5 12.1 %all-to-all-start.3 = ((f32[4,64,512]{2,1,0:T(8,128)}), f32[4,64,512]{2,1,0:T(8,128)S(1)}, u32[]{:S(2)}, u32[]{:S(2)}) async-start(f32[4,64,512]{2,1,0:T(8,128)} %shard_map.89), calls=%async_computation.3 | async-start | bytes 1048576 | tf_op jit(solution)/shard_map/all_to_all | solution.py:206
  118.4 9.2 %copy-start.8 = (f32[64,64]{1,0:T(8,128)}, f32[64,64]{1,0:T(8,128)S(1)}, u32[]{:S(2)}) copy-start(f32[64,64]{1,0:T(8,128)S(1)} %convolution_add_fusion.1) | copy-start | bytes 49156

commit v13 on v11

--- a/solution.py
+++ b/solution.py
@@ -29,6 +29,11 @@
     low = jnp.where(lane < 64, first, pltpu.roll(second, 64, 1))
     high = jnp.where(lane < 64, pltpu.roll(first, 64, 1), second)
     return low, high
+
+
+def copies_kernel(in_ref, out_ref):
+    for z in range(out_ref.shape[0]):
+        out_ref[z] = in_ref[...]
 
 
 def pack_kernel(cols, s_ref, a_ref, packed_ref):
@@ -175,7 +180,12 @@
         compiler_params=pltpu.CompilerParams(vmem_limit_bytes=2 << 20),
     )(iz.reshape(1), tails)
 
-    c_rows = spread(c_own, "z").reshape(nz * rows, ns)
+    copies = pl.pallas_call(
+        copies_kernel,
+        out_shape=jax.ShapeDtypeStruct((nz, rows, ns), BF16),
+        compiler_params=pltpu.CompilerParams(vmem_limit_bytes=56 << 20),
+    )(c_own)
+    c_rows = lax.all_to_all(copies, "z", 0, 0, tiled=True).reshape(nz * rows, ns)
     sent = pl.pallas_call(
         functools.partial(cross_kernel, nx, nz),
         out_shape=jax.ShapeDtypeStruct((nz * rows, cols + 2 * nf), F32),

time: 126 us -> 126 us (level)
  local copies, waits for them, and re-layouts: 9.98 us -> 7.38 us
  Pallas kernels: 7.34 us -> 9.82 us
    all_to_all x0 -> x1, starting transfers between devices: none -> 10.4 us  [shards(): lax.all_to_all(copies, 'z', 0, 0, tiled=True).reshape(nz * rows, ns)]
    all_to_all x2 -> x1, starting transfers between devices: 14.7 us -> 4.25 us  [spread(): lax.all_to_all(jnp.broadcast_to(v[None], (n,) + v.shape), axis, 0, 0, til...]
    all_to_all x0 -> x1, waiting for transfers between devices: none -> 4.04 us  [shards(): lax.all_to_all(copies, 'z', 0, 0, tiled=True).reshape(nz * rows, ns)]
    all_to_all x2 -> x1, waiting for transfers between devices: 14.6 us -> 10.6 us  [spread(): lax.all_to_all(jnp.broadcast_to(v[None], (n,) + v.shape), axis, 0, 0, til...]
    broadcast_in_dim x2 -> x1, local copies, waits for them, and re-layouts: 3.73 us -> 1.13 us  [spread(): jnp.broadcast_to(v[None], (n,) + v.shape)]
    pallas_call x0 -> x1, Pallas kernels: none -> 2.48 us  [shards(): pl.pallas_call(copies_kernel, out_shape=jax.ShapeDtypeStruct((nz, rows, n...]
where the time goes in v13:
time: 126 us; the launch traced here: 125 us
  waiting for transfers between devices  50.9 us (40%)
  starting transfers between devices  32.7 us (26%)
  blocking collectives  18 us (14%)
  Pallas kernels  9.82 us (8%)
  local copies, waits for them, and re-layouts  7.38 us (6%)
  other arithmetic  3.43 us (3%)
  matrix products  1.92 us (2%)
    ppermute x3, waiting for transfers between devices, shards(): lax.ppermute(packed, 'x', [((i + by) % nx, i) for i in range(nx)])  24.4 us
    all_to_all x1, blocking collectives, shards(): sent = lax.all_to_all(sent, 'z', 0, 0, tiled=True)  18 us
    all_to_all x1, waiting for transfers between devices, spread(): lax.all_to_all(jnp.broadcast_to(v[None], (n,) + v.shape), axis, 0, 0, til...  10.6 us
    all_to_all x1, starting transfers between devices, shards(): lax.all_to_all(copies, 'z', 0, 0, tiled=True).reshape(nz * rows, ns)  10.4 us
    ppermute x3, starting transfers between devices, shards(): lax.ppermute(packed, 'x', [((i + by) % nx, i) for i in range(nx)])  10.2 us
    all_to_all x1, waiting for transfers between devices, shards(): diag = lax.all_to_all(diag, 'x', 0, 0, tiled=True)  7.31 us
    unnamed x33, local copies, waits for them, and re-layouts  6.14 us
    ppermute x2, waiting for transfers between devices, shards(): s_own, a_own = lax.ppermute((s_own, a_own), ('y', 'c', 'x', 'z'), route)  4.55 us
  transfers between devices with their start and end apart: 8, of which 7 were waited for; matrix products, arithmetic and copies ran while one was open for 3% of the time, Pallas kernels for 2%

profile of v13, /device:TPU:24, one launch (start us, length us, event | category | flops | bytes accessed | tf_op | source)
XLA Modules:
  0.0 125.1 jit_solution(13891602547897257273)
XLA Ops:
  0.6 2.5 %shard_map.86 = bf16[8,64,2048]{2,1,0:T(8,128)(2,1)} custom-call(bf16[64,2048]{1,0:T(8,128)(2,1)} %bitcast.60), custom_call_target="tpu_custom_call" | custom-call | tf_op jit(solution)/shard_map/pallas_call | solution.py:183
  3.1 10.4 %all-to-all-start = ((bf16[8,64,2048]{2,1,0:T(8,128)(2,1)}), bf16[8,64,2048]{2,1,0:T(8,128)(2,1)S(1)}, u32[]{:S(2)}, u32[]{:S(2)}) async-start(bf16[8,64,2048]{2,1,0:T(8,128)(2,1)} %shard_map.86), calls=%async_computation | async-start | bytes 4194304 | tf_op jit(solution)/shard_map/all_to_all | solution.py:188
  13.6 1.9 %collective-permute-start = (f32[64,2048]{1,0:T(8,128)S(1)}, f32[64,2048]{1,0:T(8,128)S(1)}, u32[]{:S(2)}, u32[]{:S(2)}) collective-permute-start(f32[64,2048]{1,0:T(8,128)S(1)} %bitcast.62), channel_id=1, source_target_pairs={{32,0},{33,1},{34,2},{35,3},{36,4},{37,5},{38,6},{39,7},{40,8},{41... | collective-permute-start | bytes 1572872 | tf_op jit(solution)/shard_map/ppermute | solution.py:157
  15.5 2.5 %collective-permute-start.1 = (f32[64,64]{1,0:T(8,128)S(1)}, f32[64,64]{1,0:T(8,128)S(1)}, u32[]{:S(2)}, u32[]{:S(2)}) collective-permute-start(f32[64,64]{1,0:T(8,128)S(1)} %bitcast.63), channel_id=1, source_target_pairs={{32,0},{33,1},{34,2},{35,3},{36,4},{37,5},{38,6},{39,7},{40,8},{41... | collective-permute-start | bytes 49160 | tf_op jit(solution)/shard_map/ppermute | solution.py:157
  18.0 4.5 %collective-permute-done.1.a_ref = f32[64,64]{1,0:T(8,128)S(1)} collective-permute-done((f32[64,64]{1,0:T(8,128)S(1)}, f32[64,64]{1,0:T(8,128)S(1)}, u32[]{:S(2)}, u32[]{:S(2)}) %collective-permute-start.1) | collective-permute-done | bytes 16416 | tf_op jit(solution)/shard_map/ppermute | solution.py:157
  22.8 4.7 %collective-permute-start.2 = (bf16[2,64,2176]{2,1,0:T(8,128)(2,1)S(1)}, bf16[2,64,2176]{2,1,0:T(8,128)(2,1)}, u32[]{:S(2)}, u32[]{:S(2)}) collective-permute-start(bf16[2,64,2176]{2,1,0:T(8,128)(2,1)S(1)} %shard_map.85.refs_0_), channel_id=1, source_target_pairs={{8,0},{16,8},{24,16},{0,24},{9,1},{17,9},{25,17},{1,25},{10,2},{18... | collective-permute-start | bytes 1671176 | tf_op jit(solution)/shard_map/ppermute | solution.py:165
  27.5 2.7 %collective-permute-start.3 = (bf16[2,64,2176]{2,1,0:T(8,128)(2,1)S(1)}, bf16[2,64,2176]{2,1,0:T(8,128)(2,1)S(1)}, u32[]{:S(2)}, u32[]{:S(2)}) collective-permute-start(bf16[2,64,2176]{2,1,0:T(8,128)(2,1)S(1)} %shard_map.85.refs_0_), channel_id=1, source_target_pairs={{16,0},{24,8},{0,16},{8,24},{17,1},{25,9},{1,17},{9,25},{18,2},{26... | collective-permute-start | bytes 1671176 | tf_op jit(solution)/shard_map/ppermute | solution.py:165
  30.3 2.8 %collective-permute-start.4 = (bf16[2,64,2176]{2,1,0:T(8,128)(2,1)S(1)}, bf16[2,64,2176]{2,1,0:T(8,128)(2,1)S(1)}, u32[]{:S(2)}, u32[]{:S(2)}) collective-permute-start(bf16[2,64,2176]{2,1,0:T(8,128)(2,1)S(1)} %shard_map.85.refs_0_), channel_id=1, source_target_pairs={{24,0},{0,8},{8,16},{16,24},{25,1},{1,9},{9,17},{17,25},{26,2},{2,... | collective-permute-start | bytes 1671176 | tf_op jit(solution)/shard_map/ppermute | solution.py:165
  33.1 5.7 %collective-permute-done.2.refs_1_ = bf16[2,64,2176]{2,1,0:T(8,128)(2,1)} collective-permute-done((bf16[2,64,2176]{2,1,0:T(8,128)(2,1)S(1)}, bf16[2,64,2176]{2,1,0:T(8,128)(2,1)}, u32[]{:S(2)}, u32[]{:S(2)}) %collective-permute-start.2) | collective-permute-done | bytes 557088 | tf_op jit(solution)/shard_map/ppermute | solution.py:165
  39.6 4.7 %collective-permute-done.3.refs_2_ = bf16[2,64,2176]{2,1,0:T(8,128)(2,1)S(1)} collective-permute-done((bf16[2,64,2176]{2,1,0:T(8,128)(2,1)S(1)}, bf16[2,64,2176]{2,1,0:T(8,128)(2,1)S(1)}, u32[]{:S(2)}, u32[]{:S(2)}) %collective-permute-start.3) | collective-permute-done | bytes 557088 | tf_op jit(solution)/shard_map/ppermute | solution.py:165
  44.3 13.9 %collective-permute-done.4.refs_3_ = bf16[2,64,2176]{2,1,0:T(8,128)(2,1)S(1)} collective-permute-done((bf16[2,64,2176]{2,1,0:T(8,128)(2,1)S(1)}, bf16[2,64,2176]{2,1,0:T(8,128)(2,1)S(1)}, u32[]{:S(2)}, u32[]{:S(2)}) %collective-permute-start.4) | collective-permute-done | bytes 557088 | tf_op jit(solution)/shard_map/ppermute | solution.py:165
  59.5 1.2 fusion.2.term_ref
  60.7 4.0 %all-to-all-done = bf16[8,64,2048]{2,1,0:T(8,128)(2,1)S(1)} async-done(((bf16[8,64,2048]{2,1,0:T(8,128)(2,1)}), bf16[8,64,2048]{2,1,0:T(8,128)(2,1)S(1)}, u32[]{:S(2)}, u32[]{:S(2)}) %all-to-all-start) | async-done | bytes 2097184 | tf_op jit(solution)/shard_map/all_to_all | solution.py:188
  67.9 2.7 %shard_map.88 = f32[512,384]{1,0:T(8,128)S(1)} custom-call(s32[2]{0:T(128)S(1)} %pad_add_fusion.at_ref, f32[4]{0:T(128)S(1)} %pad_maximum_fusion.exps_ref, bf16[512,2048]{1,0:T(8,128)(2,1)S(1)} %bitcast.53, bf16[4,128,128]{2,1,0:T(8,128)(2,1)S(1)} %shard_map.87.place_ref, f32[512,256]{1,0:T(8,128)S(1)} %copy-done.3, ...), custom_call_target="tpu_custom_call" | custom-call | tf_op jit(solution)/shard_map/pallas_call | solution.py:189
  70.7 18.0 %all_to_all.20 = f16[8,64,384]{2,1,0:T(8,128)(2,1)S(1)} all-to-all(f16[8,64,384]{2,1,0:T(8,128)(2,1)S(1)} %bitcast.57), channel_id=1, replica_groups=mesh['y'=8,'c'=2,'x'=4,'z'=8] {'z'}, dimensions={0} | all-to-all | bytes 786432 | tf_op jit(solution)/shard_map/all_to_all | solution.py:204
  88.8 1.1 broadcast_in_dim.16
  90.0 4.3 %all-to-all-start.2 = ((f16[4,8,64,256]{3,2,1,0:T(8,128)(2,1)}), f16[4,8,64,256]{3,2,1,0:T(8,128)(2,1)}, u32[]{:S(2)}, u32[]{:S(2)}) async-start(f16[4,8,64,256]{3,2,1,0:T(8,128)(2,1)} %broadcast_in_dim.16), calls=%async_computation.2 | async-start | bytes 2097152 | tf_op jit(solution)/shard_map/all_to_all | solution.py:24
  94.2 1.1 shard_map.89.c_ref
  95.4 1.3 %copy-done.1 = bf16[512,2048]{1,0:T(8,128)(2,1)} copy-done((bf16[512,2048]{1,0:T(8,128)(2,1)}, bf16[512,2048]{1,0:T(8,128)(2,1)S(1)}, u32[]{:S(2)}) %copy-start.1) | copy-done | bytes 2097176
  98.2 10.6 %all-to-all-done.2 = f16[4,8,64,256]{3,2,1,0:T(8,128)(2,1)} async-done(((f16[4,8,64,256]{3,2,1,0:T(8,128)(2,1)}), f16[4,8,64,256]{3,2,1,0:T(8,128)(2,1)}, u32[]{:S(2)}, u32[]{:S(2)}) %all-to-all-start.2) | async-done | bytes 1048608 | tf_op jit(solution)/shard_map/all_to_all | solution.py:24
  108.8 1.7 %fusion = (bf16[4,8,64,256]{3,2,1,0:T(8,128)(2,1)S(1)}, bf16[4,8,64,256]{3,2,1,0:T(8,128)(2,1)S(1)}) fusion(f16[4,8,64,256]{3,2,1,0:T(8,128)(2,1)} %all-to-all-done.2, f32[8]{0:T(128)S(1)} %get-tuple-element.3), kind=kLoop, calls=%fused_computation.3 | loop fusion | flops 3145728 | bytes 3145760 | tf_op jit(solution)/shard_map/convert_element_type | solution.py:211
  110.6 2.1 %shard_map.90 = f32[4,64,512]{2,1,0:T(8,128)} custom-call(bf16[4,8,64,256]{3,2,1,0:T(8,128)(2,1)S(1)} %get-tuple-element.6.top_ref, bf16[4,8,64,256]{3,2,1,0:T(8,128)(2,1)S(1)} %get-tuple-element.5.low_ref, bf16[512,2048]{1,0:T(8,128)(2,1)S(1)} %copy-done.2), custom_call_target="tpu_custom_call" | custom-call | tf_op jit(solution)/shard_map/pallas_call | solution.py:212
  112.7 3.5 %all-to-all-start.3 = ((f32[4,64,512]{2,1,0:T(8,128)}), f32[4,64,512]{2,1,0:T(8,128)S(1)}, u32[]{:S(2)}, u32[]{:S(2)}) async-start(f32[4,64,512]{2,1,0:T(8,128)} %shard_map.90), calls=%async_computation.3 | async-start | bytes 1048576 | tf_op jit(solution)/shard_map/all_to_all | solution.py:218
  116.9 7.3 %all-to-all-done.3 = f32[4,64,512]{2,1,0:T(8,128)S(1)} async-done(((f32[4,64,512]{2,1,0:T(8,128)}), f32[4,64,512]{2,1,0:T(8,128)S(1)}, u32[]{:S(2)}, u32[]{:S(2)}) %all-to-all-start.3) | async-done | bytes 524320 | tf_op jit(solution)/shard_map/all_to_all | solution.py:218
  (54 shorter events, 8.7 us)
Async XLA Ops:
  0.6 58.9 %copy-start = (f32[1,2048,64]{1,2,0:T(8,128)S(1)}, f32[1,2048,64]{1,2,0:T(8,128)}, u32[]{:S(2)}) copy-start(f32[1,2048,64]{1,2,0:T(8,128)} %param.7) | copy-start | bytes 1572868
  3.1 10.5 %copy-start.11 = (f32[1,64,2048]{2,1,0:T(8,128)S(1)}, f32[1,64,2048]{2,1,0:T(8,128)}, u32[]{:S(2)}) copy-start(f32[1,64,2048]{2,1,0:T(8,128)} %param.9) | copy-start | bytes 1572868
  3.1 12.4 %copy-start.12 = (f32[1,64,64]{2,1,0:T(8,128)S(1)}, f32[1,64,64]{2,1,0:T(8,128)}, u32[]{:S(2)}) copy-start(f32[1,64,64]{2,1,0:T(8,128)} %param.10) | copy-start | bytes 49156
  3.1 61.6 %all-to-all-start = ((bf16[8,64,2048]{2,1,0:T(8,128)(2,1)}), bf16[8,64,2048]{2,1,0:T(8,128)(2,1)S(1)}, u32[]{:S(2)}, u32[]{:S(2)}) async-start(bf16[8,64,2048]{2,1,0:T(8,128)(2,1)} %shard_map.86), calls=%async_computation | async-start | bytes 4194304 | tf_op jit(solution)/shard_map/all_to_all | solution.py:188
  13.6 9.0 %collective-permute-start = (f32[64,2048]{1,0:T(8,128)S(1)}, f32[64,2048]{1,0:T(8,128)S(1)}, u32[]{:S(2)}, u32[]{:S(2)}) collective-permute-start(f32[64,2048]{1,0:T(8,128)S(1)} %bitcast.62), channel_id=1, source_target_pairs={{32,0},{33,1},{34,2},{35,3},{36,4},{37,5},{38,6},{39,7},{40,8},{41... | collective-permute-start | bytes 1572872 | tf_op jit(solution)/shard_map/ppermute | solution.py:157
  15.5 7.0 %collective-permute-start.1 = (f32[64,64]{1,0:T(8,128)S(1)}, f32[64,64]{1,0:T(8,128)S(1)}, u32[]{:S(2)}, u32[]{:S(2)}) collective-permute-start(f32[64,64]{1,0:T(8,128)S(1)} %bitcast.63), channel_id=1, source_target_pairs={{32,0},{33,1},{34,2},{35,3},{36,4},{37,5},{38,6},{39,7},{40,8},{41... | collective-permute-start | bytes 49160 | tf_op jit(solution)/shard_map/ppermute | solution.py:157
  22.8 16.0 %collective-permute-start.2 = (bf16[2,64,2176]{2,1,0:T(8,128)(2,1)S(1)}, bf16[2,64,2176]{2,1,0:T(8,128)(2,1)}, u32[]{:S(2)}, u32[]{:S(2)}) collective-permute-start(bf16[2,64,2176]{2,1,0:T(8,128)(2,1)S(1)} %shard_map.85.refs_0_), channel_id=1, source_target_pairs={{8,0},{16,8},{24,16},{0,24},{9,1},{17,9},{25,17},{1,25},{10,2},{18... | collective-permute-start | bytes 1671176 | tf_op jit(solution)/shard_map/ppermute | solution.py:165
  27.5 16.8 %collective-permute-start.3 = (bf16[2,64,2176]{2,1,0:T(8,128)(2,1)S(1)}, bf16[2,64,2176]{2,1,0:T(8,128)(2,1)S(1)}, u32[]{:S(2)}, u32[]{:S(2)}) collective-permute-start(bf16[2,64,2176]{2,1,0:T(8,128)(2,1)S(1)} %shard_map.85.refs_0_), channel_id=1, source_target_pairs={{16,0},{24,8},{0,16},{8,24},{17,1},{25,9},{1,17},{9,25},{18,2},{26... | collective-permute-start | bytes 1671176 | tf_op jit(solution)/shard_map/ppermute | solution.py:165
  30.3 27.9 %collective-permute-start.4 = (bf16[2,64,2176]{2,1,0:T(8,128)(2,1)S(1)}, bf16[2,64,2176]{2,1,0:T(8,128)(2,1)S(1)}, u32[]{:S(2)}, u32[]{:S(2)}) collective-permute-start(bf16[2,64,2176]{2,1,0:T(8,128)(2,1)S(1)} %shard_map.85.refs_0_), channel_id=1, source_target_pairs={{24,0},{0,8},{8,16},{16,24},{25,1},{1,9},{9,17},{17,25},{26,2},{2,... | collective-permute-start | bytes 1671176 | tf_op jit(solution)/shard_map/ppermute | solution.py:165
  44.3 15.2 %copy-start.4 = (bf16[2,64,2176]{2,1,0:T(8,128)(2,1)}, bf16[2,64,2176]{2,1,0:T(8,128)(2,1)S(1)}, u32[]{:S(2)}) copy-start(bf16[2,64,2176]{2,1,0:T(8,128)(2,1)S(1)} %collective-permute-done.3.refs_2_) | copy-start | bytes 1671172
  58.2 1.2 copy-start.6
  64.8 1.0 copy-start.3
  65.8 1.1 copy-start.5
  66.9 1.1 copy-start.7
  90.0 18.9 %all-to-all-start.2 = ((f16[4,8,64,256]{3,2,1,0:T(8,128)(2,1)}), f16[4,8,64,256]{3,2,1,0:T(8,128)(2,1)}, u32[]{:S(2)}, u32[]{:S(2)}) async-start(f16[4,8,64,256]{3,2,1,0:T(8,128)(2,1)} %broadcast_in_dim.16), calls=%async_computation.2 | async-start | bytes 2097152 | tf_op jit(solution)/shard_map/all_to_all | solution.py:24
  95.4 1.3 %copy-start.1 = (bf16[512,2048]{1,0:T(8,128)(2,1)}, bf16[512,2048]{1,0:T(8,128)(2,1)S(1)}, u32[]{:S(2)}) copy-start(bf16[512,2048]{1,0:T(8,128)(2,1)S(1)} %shard_map.89.c_ref) | copy-start | bytes 6291460
  97.1 13.4 %copy-start.2 = (bf16[512,2048]{1,0:T(8,128)(2,1)S(1)}, bf16[512,2048]{1,0:T(8,128)(2,1)}, u32[]{:S(2)}) copy-start(bf16[512,2048]{1,0:T(8,128)(2,1)} %copy-done.1) | copy-start | bytes 6291460
  110.6 5.6 %copy-start.10 = (f32[64,64]{1,0:T(8,128)S(1)}, f32[64,64]{1,0:T(8,128)}, u32[]{:S(2)}) copy-start(f32[64,64]{1,0:T(8,128)} %param.11) | copy-start | bytes 49156
  110.6 5.9 %copy-start.8 = (f32[1,64,2048]{2,1,0:T(8,128)S(1)}, f32[1,64,2048]{2,1,0:T(8,128)}, u32[]{:S(2)}) copy-start(f32[1,64,2048]{2,1,0:T(8,128)} %param.8) | copy-start | bytes 1572868
  112.7 11.5 %all-to-all-start.3 = ((f32[4,64,512]{2,1,0:T(8,128)}), f32[4,64,512]{2,1,0:T(8,128)S(1)}, u32[]{:S(2)}, u32[]{:S(2)}) async-start(f32[4,64,512]{2,1,0:T(8,128)} %shard_map.90), calls=%async_computation.3 | async-start | bytes 1048576 | tf_op jit(solution)/shard_map/all_to_all | solution.py:218
  116.5 8.6 %copy-start.9 = (f32[64,64]{1,0:T(8,128)}, f32[64,64]{1,0:T(8,128)S(1)}, u32[]{:S(2)}) copy-start(f32[64,64]{1,0:T(8,128)S(1)} %convolution_add_fusion.1) | copy-start | bytes 49156
